TPU v7x, 32 devices: a whole 2x2x4 slice. The times are simulated.
32 devices in a mesh: rows: 2 (over core), seq: 16 (over z, y, x).
Axes of the slice: x: 2, y: 2, z: 4, core: 2. Of those that a mesh axis runs over, the one named last changes fastest.
Arguments:
- tokens: bfloat16 [2, 1024, 2, 512], P(None, 'seq', 'rows'), may hold values from -6 to 6
- memory: bfloat16 [2, 1024, 2, 512], P(None, 'seq', 'rows'), may hold values from -6 to 6
- cotangent: bfloat16 [2, 1024, 2, 512], P(None, 'seq', 'rows'), may hold values from -6 to 6
- tgt_lengths: int32 [2, 2, 32], P(None, 'rows'), may hold values from 1 to 993, as said below
- src_lengths: int32 [2, 2, 32], P(None, 'rows'), may hold values from 1 to 993, as said below
- tgt_mask: int32 [2, 1024, 2], P(None, 'seq', 'rows'), may hold values 0 or 1
- src_mask: int32 [2, 1024, 2], P(None, 'seq', 'rows'), may hold values 0 or 1
- attn_in: bfloat16 [2, 3, 512, 512], P(None, None, ('rows', 'seq')), may hold values from -0.25 to 0.25
- attn_out: bfloat16 [2, 512, 512], P(None, ('rows', 'seq')), may hold values from -1 to 1
- w_up: bfloat16 [512, 2048], P(('rows', 'seq')), may hold values from -0.25 to 0.25
- w_down: bfloat16 [2048, 512], P(('rows', 'seq')), may hold values from -0.125 to 0.125
- biases: float32 [7, 512], replicated, may hold values from -1.2 to 1.2
- up_bias: float32 [2048], replicated, may hold values from -1.2 to 1.2
- norm_gain: float32 [3, 512], replicated, may hold values from 0.5 to 1.5
- norm_shift: float32 [3, 512], replicated, may hold values from -0.8 to 0.8
- omega: float32 [3, 512], replicated, may hold values from 0.5 to 1.5
Outputs:
- result: bfloat16 [2, 1024, 2, 512], P(None, 'seq', 'rows')
- grad_tokens: bfloat16 [2, 1024, 2, 512], P(None, 'seq', 'rows')
- grad_memory: bfloat16 [2, 1024, 2, 512], P(None, 'seq', 'rows')
- grad_attn_in: float32 [2, 3, 512, 512], P(None, None, ('rows', 'seq'))
- grad_attn_out: float32 [2, 512, 512], P(None, ('rows', 'seq'))
- grad_w_up: float32 [512, 2048], P(('rows', 'seq'))
- grad_w_down: float32 [2048, 512], P(('rows', 'seq'))
- grad_biases: float32 [7, 512], P(None, ('rows', 'seq'))
- grad_up_bias: float32 [2048], P(('rows', 'seq'))
- grad_norm_gain: float32 [3, 512], P(None, ('rows', 'seq'))
- grad_norm_shift: float32 [3, 512], P(None, ('rows', 'seq'))
- grad_omega: float32 [3, 512], P(None, ('rows', 'seq'))
Inputs may be any that keep to these rules, and one draw needn't show every extreme that they name: `tgt_lengths`: each row's 32 lengths sum to 1024. `src_lengths`: each row's 32 lengths sum to 1024.
All inputs are finite; a program needn't handle non-finite values. No bound on the sum of `tgt_mask` or of `src_mask` on one device may be relied on, other than what follows from the above.
Results may differ from a plain program's by a relative error of at most 0.03.
Values may be sent and summed in bfloat16 or wider, within the bound.
A program may use at most 256 MiB of HBM per device.

v0:
```python
import math

import jax
import jax.numpy as jnp
from jax import lax
from jax.sharding import PartitionSpec as P

HEADS = 8


def norm_block(branch, skip, scale, gain, shift):
    mixed = skip * scale + branch
    centered = mixed - jnp.mean(mixed, axis=-1, keepdims=True)
    variance = jnp.mean(centered * centered, axis=-1, keepdims=True)
    return centered * lax.rsqrt(variance + 1e-05) * gain + shift


def project(values, matrix):
    return jnp.einsum("trd,de->tre", values, matrix, preferred_element_type=jnp.float32)


def project_back(grads, matrix):
    return jnp.einsum("tre,de->trd", grads, matrix, preferred_element_type=jnp.float32)


def matrix_grad(values, grads):
    return jnp.einsum("trd,tre->de", values, grads, preferred_element_type=jnp.float32)


def column_sum(grads):
    return jnp.sum(grads.astype(jnp.float32), axis=(0, 1))


def segment_of(positions, ends):
    return jnp.sum((ends[None, :, :] <= positions[:, None, None]).astype(jnp.int32), axis=-1)


def segment_bounds(first, last, ends):
    lowest = jnp.sum((ends <= first).astype(jnp.int32), axis=-1)
    highest = jnp.sum((ends <= last).astype(jnp.int32), axis=-1)
    return (lowest, highest)


def ranges_share(query_bounds, key_bounds):
    return jnp.any((key_bounds[0] <= query_bounds[1]) & (key_bounds[1] >= query_bounds[0]))


def key_status(positions, real_marks, ends, starts, causal):
    segments = segment_of(positions, ends)
    usable = real_marks > 0.5
    if not causal:
        usable = usable | jnp.any(starts[None, :, :] == positions[:, None, None], axis=-1)
    return (segments, usable)


def permitted(query_pos, query_seg, key_pos, key_seg, usable, causal):
    same = jnp.transpose(query_seg)[:, :, None] == jnp.transpose(key_seg)[:, None, :]
    usable_keys = jnp.transpose(usable)[:, None, :]
    if causal:
        before = (key_pos[None, :] <= query_pos[:, None])[None]
        itself = (key_pos[None, :] == query_pos[:, None])[None]
        return same & before & (usable_keys | itself)
    return same & usable_keys


def block_grads(query_heads, grad_heads, lambdas, key_heads, value_heads, permit):
    scores = (
        jnp.einsum("arhd,brhd->rhab", query_heads, key_heads, preferred_element_type=jnp.float32)
        * 0.125
    )
    weights = jnp.where(permit[:, None], jnp.exp(scores), 0.0)
    spread = jnp.einsum(
        "arhd,brhd->rhab", grad_heads, value_heads, preferred_element_type=jnp.float32
    )
    slopes = weights * (spread + jnp.transpose(lambdas, (1, 2, 0))[..., None])
    return (weights.astype(jnp.bfloat16), slopes.astype(jnp.bfloat16))


def local(
    tokens,
    memory,
    cotangent,
    tgt_lengths,
    src_lengths,
    tgt_mask,
    src_mask,
    attn_in,
    attn_out,
    w_up,
    w_down,
    biases,
    up_bias,
    norm_gain,
    norm_shift,
    omega,
):
    micro_count, tokens_here, rows_here, width = tokens.shape
    head_size = width // HEADS
    my_pos = lax.axis_index("seq") * tokens_here + jnp.arange(tokens_here, dtype=jnp.int32)
    my_first = my_pos[0]
    my_last = my_pos[tokens_here - 1]

    def split_heads(values):
        return values.reshape(values.shape[0], rows_here, HEADS, head_size)

    def zero_heads():
        return jnp.zeros((tokens_here, rows_here, HEADS, head_size), jnp.float32)

    results = []
    grads_words = []
    grads_sources = []
    shares_all = None
    for micro_index in range(micro_count):
        in_weights = lax.all_gather(attn_in, ("rows", "seq"), axis=2, tiled=True)
        out_weights = lax.all_gather(attn_out, ("rows", "seq"), axis=1, tiled=True)
        up_weights = lax.all_gather(w_up, ("rows", "seq"), axis=0, tiled=True)
        down_weights = lax.all_gather(w_down, ("rows", "seq"), axis=0, tiled=True)
        words = tokens[micro_index]
        sources = memory[micro_index]
        words_full = words.astype(jnp.float32)
        tgt_len = tgt_lengths[micro_index]
        src_len = src_lengths[micro_index]
        tgt_ends = jnp.cumsum(tgt_len, axis=-1)
        src_ends = jnp.cumsum(src_len, axis=-1)
        src_starts = src_ends - src_len
        query_seg = segment_of(my_pos, tgt_ends)
        query_bounds = segment_bounds(my_first, my_last, tgt_ends)
        tgt_real = tgt_mask[micro_index].astype(jnp.bfloat16)
        src_real = src_mask[micro_index].astype(jnp.bfloat16)

        def attend(queries, keys, values, real_marks, ends, starts, causal):
            full_keys, full_values, full_real = (
                lax.all_gather(keys, "seq", axis=0, tiled=True),
                lax.all_gather(values, "seq", axis=0, tiled=True),
                lax.all_gather(real_marks, "seq", axis=0, tiled=True),
            )
            length = full_keys.shape[0]
            block = math.gcd(length, 512)
            query_heads = split_heads(queries)

            def step(carry, block_index):
                begin = block_index * block
                shares = ranges_share(query_bounds, segment_bounds(begin, begin + block - 1, ends))

                def step_compute(state):
                    totals, accum = state
                    key_heads = split_heads(lax.dynamic_slice_in_dim(full_keys, begin, block, 0))
                    value_heads = split_heads(
                        lax.dynamic_slice_in_dim(full_values, begin, block, 0)
                    )
                    key_pos = begin + jnp.arange(block, dtype=jnp.int32)
                    key_seg, usable = key_status(
                        key_pos,
                        lax.dynamic_slice_in_dim(full_real, begin, block, 0),
                        ends,
                        starts,
                        causal,
                    )
                    permit = permitted(my_pos, query_seg, key_pos, key_seg, usable, causal)
                    scores = (
                        jnp.einsum(
                            "trhd,krhd->rhtk",
                            query_heads,
                            key_heads,
                            preferred_element_type=jnp.float32,
                        )
                        * 0.125
                    )
                    weights = jnp.where(permit[:, None], jnp.exp(scores), 0.0)
                    totals = totals + jnp.sum(weights, axis=-1)
                    accum = accum + jnp.einsum(
                        "rhtk,krhd->trhd",
                        weights.astype(jnp.bfloat16),
                        value_heads,
                        preferred_element_type=jnp.float32,
                    )
                    return (totals, accum)

                return (lax.cond(shares, step_compute, lambda unchanged: unchanged, carry), None)

            start_carry = (jnp.zeros((rows_here, HEADS, tokens_here), jnp.float32), zero_heads())
            (totals, accum), unused = lax.scan(
                step, start_carry, jnp.arange(length // block, dtype=jnp.int32)
            )
            sums = jnp.transpose(totals, (2, 0, 1))
            output = (accum / sums[..., None]).reshape(tokens_here, rows_here, width)
            return (output, sums, (full_keys, full_values, full_real))

        def attention_back(
            grad_out,
            output,
            sums,
            queries,
            keys,
            values,
            real_marks,
            gathered_set,
            ends,
            starts,
            causal,
        ):
            full_keys, full_values, full_real = gathered_set
            grad_heads = split_heads(grad_out)
            lambdas = -jnp.sum(grad_heads * split_heads(output), axis=-1) / sums
            scaled = (grad_heads / sums[..., None]).astype(jnp.bfloat16)
            query_heads = split_heads(queries)
            length = full_keys.shape[0]
            block = math.gcd(length, 512)

            def query_step(accum, block_index):
                begin = block_index * block
                shares = ranges_share(query_bounds, segment_bounds(begin, begin + block - 1, ends))

                def query_compute(state):
                    key_heads = split_heads(lax.dynamic_slice_in_dim(full_keys, begin, block, 0))
                    value_heads = split_heads(
                        lax.dynamic_slice_in_dim(full_values, begin, block, 0)
                    )
                    key_pos = begin + jnp.arange(block, dtype=jnp.int32)
                    key_seg, usable = key_status(
                        key_pos,
                        lax.dynamic_slice_in_dim(full_real, begin, block, 0),
                        ends,
                        starts,
                        causal,
                    )
                    permit = permitted(my_pos, query_seg, key_pos, key_seg, usable, causal)
                    weights, slopes = block_grads(
                        query_heads, scaled, lambdas, key_heads, value_heads, permit
                    )
                    return (
                        state
                        + jnp.einsum(
                            "rhab,brhd->arhd", slopes, key_heads, preferred_element_type=jnp.float32
                        )
                        * 0.125
                    )

                return (lax.cond(shares, query_compute, lambda unchanged: unchanged, accum), None)

            grad_query, unused = lax.scan(
                query_step, zero_heads(), jnp.arange(length // block, dtype=jnp.int32)
            )
            all_lambdas = lax.all_gather(lambdas, "seq", axis=0, tiled=True)
            local_seg, local_usable = key_status(my_pos, real_marks, ends, starts, causal)
            local_bounds = segment_bounds(my_first, my_last, ends)
            local_keys = split_heads(keys)
            local_values = split_heads(values)
            query_piece = lax.all_gather(queries, "seq", axis=0, tiled=True)
            scaled_piece = lax.all_gather(
                scaled.reshape(tokens_here, rows_here, width), "seq", axis=0, tiled=True
            )
            size = query_piece.shape[0]
            inner = math.gcd(size, 512)

            def inner_step(inner_carry, inner_index):
                offset = inner_index * inner
                piece_first = offset
                shares = ranges_share(
                    segment_bounds(piece_first, piece_first + inner - 1, tgt_ends), local_bounds
                )

                def inner_compute(state):
                    acc_key, acc_value = state
                    query_blk = split_heads(lax.dynamic_slice_in_dim(query_piece, offset, inner, 0))
                    scaled_blk = split_heads(
                        lax.dynamic_slice_in_dim(scaled_piece, offset, inner, 0)
                    )
                    lambda_blk = lax.dynamic_slice_in_dim(all_lambdas, piece_first, inner, 0)
                    query_pos = piece_first + jnp.arange(inner, dtype=jnp.int32)
                    permit = permitted(
                        query_pos,
                        segment_of(query_pos, tgt_ends),
                        my_pos,
                        local_seg,
                        local_usable,
                        causal,
                    )
                    weights, slopes = block_grads(
                        query_blk, scaled_blk, lambda_blk, local_keys, local_values, permit
                    )
                    acc_key = (
                        acc_key
                        + jnp.einsum(
                            "rhab,arhd->brhd", slopes, query_blk, preferred_element_type=jnp.float32
                        )
                        * 0.125
                    )
                    acc_value = acc_value + jnp.einsum(
                        "rhab,arhd->brhd", weights, scaled_blk, preferred_element_type=jnp.float32
                    )
                    return (acc_key, acc_value)

                return (
                    lax.cond(shares, inner_compute, lambda unchanged: unchanged, inner_carry),
                    None,
                )

            folded, unused_inner = lax.scan(
                inner_step, (zero_heads(), zero_heads()), jnp.arange(size // inner, dtype=jnp.int32)
            )
            grad_key, grad_value = folded
            grad_key = grad_key.reshape(tokens_here, rows_here, width)
            grad_value = grad_value.reshape(tokens_here, rows_here, width)
            return (grad_query.reshape(tokens_here, rows_here, width), grad_key, grad_value)

        self_query = (project(words, in_weights[0, 0]) + biases[0]).astype(jnp.bfloat16)
        self_key = project(words, in_weights[0, 1]).astype(jnp.bfloat16)
        self_value = (project(words, in_weights[0, 2]) + biases[1]).astype(jnp.bfloat16)
        heard, heard_sums, self_set = attend(
            self_query, self_key, self_value, tgt_real, tgt_ends, None, True
        )
        heard_low = heard.astype(jnp.bfloat16)
        branch_self = project(heard_low, out_weights[0]) + biases[2]
        hidden_one, pull_one = jax.vjp(
            norm_block, branch_self, words_full, omega[0], norm_gain[0], norm_shift[0]
        )
        hidden_one_low = hidden_one.astype(jnp.bfloat16)
        cross_query = (project(hidden_one_low, in_weights[1, 0]) + biases[3]).astype(jnp.bfloat16)
        cross_key = project(sources, in_weights[1, 1]).astype(jnp.bfloat16)
        cross_value = (project(sources, in_weights[1, 2]) + biases[4]).astype(jnp.bfloat16)
        recalled, recalled_sums, cross_set = attend(
            cross_query, cross_key, cross_value, src_real, src_ends, src_starts, False
        )
        recalled_low = recalled.astype(jnp.bfloat16)
        branch_cross = project(recalled_low, out_weights[1]) + biases[5]
        hidden_two, pull_two = jax.vjp(
            norm_block, branch_cross, hidden_one, omega[1], norm_gain[1], norm_shift[1]
        )
        hidden_two_low = hidden_two.astype(jnp.bfloat16)
        up_pre = project(hidden_two_low, up_weights) + up_bias
        active, pull_active = jax.vjp(jax.nn.gelu, up_pre)
        active_low = active.astype(jnp.bfloat16)
        branch_ffn = project(active_low, down_weights) + biases[6]
        outcome, pull_three = jax.vjp(
            norm_block, branch_ffn, hidden_two, omega[2], norm_gain[2], norm_shift[2]
        )
        grad_result = cotangent[micro_index].astype(jnp.float32)
        grad_ffn, grad_two, omega_three, gain_three, shift_three = pull_three(grad_result)
        grad_ffn_low = grad_ffn.astype(jnp.bfloat16)
        grad_down = matrix_grad(active_low, grad_ffn_low)
        bias_ffn = column_sum(grad_ffn_low)
        grad_up_pre = pull_active(project_back(grad_ffn_low, down_weights))[0].astype(jnp.bfloat16)
        grad_up = matrix_grad(hidden_two_low, grad_up_pre)
        bias_up = column_sum(grad_up_pre)
        grad_two = grad_two + project_back(grad_up_pre, up_weights)
        grad_cross, grad_one, omega_two, gain_two, shift_two = pull_two(grad_two)
        grad_cross_low = grad_cross.astype(jnp.bfloat16)
        grad_out_cross = matrix_grad(recalled_low, grad_cross_low)
        bias_out_cross = column_sum(grad_cross_low)
        grad_recalled = project_back(grad_cross_low, out_weights[1])
        cross_gq, cross_gk, cross_gv = attention_back(
            grad_recalled,
            recalled,
            recalled_sums,
            cross_query,
            cross_key,
            cross_value,
            src_real,
            cross_set,
            src_ends,
            src_starts,
            False,
        )
        cross_gq = cross_gq.astype(jnp.bfloat16)
        cross_gk = cross_gk.astype(jnp.bfloat16)
        cross_gv = cross_gv.astype(jnp.bfloat16)
        grad_cross_query = matrix_grad(hidden_one_low, cross_gq)
        grad_cross_key = matrix_grad(sources, cross_gk)
        grad_cross_value = matrix_grad(sources, cross_gv)
        grad_one = grad_one + project_back(cross_gq, in_weights[1, 0])
        grad_sources = project_back(cross_gk, in_weights[1, 1]) + project_back(
            cross_gv, in_weights[1, 2]
        )
        grad_self, grad_words, omega_one, gain_one, shift_one = pull_one(grad_one)
        grad_self_low = grad_self.astype(jnp.bfloat16)
        grad_out_self = matrix_grad(heard_low, grad_self_low)
        bias_out_self = column_sum(grad_self_low)
        grad_heard = project_back(grad_self_low, out_weights[0])
        self_gq, self_gk, self_gv = attention_back(
            grad_heard,
            heard,
            heard_sums,
            self_query,
            self_key,
            self_value,
            tgt_real,
            self_set,
            tgt_ends,
            None,
            True,
        )
        self_gq = self_gq.astype(jnp.bfloat16)
        self_gk = self_gk.astype(jnp.bfloat16)
        self_gv = self_gv.astype(jnp.bfloat16)
        grad_words = (
            grad_words
            + project_back(self_gq, in_weights[0, 0])
            + project_back(self_gk, in_weights[0, 1])
            + project_back(self_gv, in_weights[0, 2])
        )
        grad_in = jnp.stack(
            [
                jnp.stack(
                    [
                        matrix_grad(words, self_gq),
                        matrix_grad(words, self_gk),
                        matrix_grad(words, self_gv),
                    ]
                ),
                jnp.stack([grad_cross_query, grad_cross_key, grad_cross_value]),
            ]
        )
        grad_out = jnp.stack([grad_out_self, grad_out_cross])
        grad_bias = jnp.stack(
            [
                column_sum(self_gq),
                column_sum(self_gv),
                bias_out_self,
                column_sum(cross_gq),
                column_sum(cross_gv),
                bias_out_cross,
                bias_ffn,
            ]
        )
        grad_gain = jnp.stack([gain_one, gain_two, gain_three])
        grad_shift = jnp.stack([shift_one, shift_two, shift_three])
        grad_omega = jnp.stack([omega_one, omega_two, omega_three])
        grads = (
            grad_in,
            grad_out,
            grad_up,
            grad_down,
            grad_bias,
            bias_up,
            grad_gain,
            grad_shift,
            grad_omega,
        )
        outcome, grad_words, grad_sources, grads = (
            outcome.astype(jnp.bfloat16),
            grad_words.astype(jnp.bfloat16),
            grad_sources.astype(jnp.bfloat16),
            grads,
        )
        results.append(outcome)
        grads_words.append(grad_words)
        grads_sources.append(grad_sources)
        part_shares = (
            lax.psum_scatter(grads[0], ("rows", "seq"), scatter_dimension=2, tiled=True),
            lax.psum_scatter(grads[1], ("rows", "seq"), scatter_dimension=1, tiled=True),
            lax.psum_scatter(grads[2], ("rows", "seq"), scatter_dimension=0, tiled=True),
            lax.psum_scatter(grads[3], ("rows", "seq"), scatter_dimension=0, tiled=True),
            lax.psum_scatter(grads[4], ("rows", "seq"), scatter_dimension=1, tiled=True),
            lax.psum_scatter(grads[5], ("rows", "seq"), scatter_dimension=0, tiled=True),
            lax.psum_scatter(grads[6], ("rows", "seq"), scatter_dimension=1, tiled=True),
            lax.psum_scatter(grads[7], ("rows", "seq"), scatter_dimension=1, tiled=True),
            lax.psum_scatter(grads[8], ("rows", "seq"), scatter_dimension=1, tiled=True),
        )
        shares_all = (
            part_shares if shares_all is None else jax.tree.map(jnp.add, shares_all, part_shares)
        )
    return (jnp.stack(results), jnp.stack(grads_words), jnp.stack(grads_sources)) + tuple(
        shares_all
    )


def solution(mesh):
    return jax.shard_map(
        local,
        mesh=mesh,
        in_specs=(
            P(None, "seq", "rows", None),
            P(None, "seq", "rows", None),
            P(None, "seq", "rows", None),
            P(None, "rows", None),
            P(None, "rows", None),
            P(None, "seq", "rows"),
            P(None, "seq", "rows"),
            P(None, None, ("rows", "seq"), None),
            P(None, ("rows", "seq"), None),
            P(("rows", "seq"), None),
            P(("rows", "seq"), None),
            P(),
            P(),
            P(),
            P(),
            P(),
        ),
        out_specs=(
            P(None, "seq", "rows", None),
            P(None, "seq", "rows", None),
            P(None, "seq", "rows", None),
            P(None, None, ("rows", "seq"), None),
            P(None, ("rows", "seq"), None),
            P(("rows", "seq"), None),
            P(("rows", "seq"), None),
            P(None, ("rows", "seq")),
            P(("rows", "seq")),
            P(None, ("rows", "seq")),
            P(None, ("rows", "seq")),
            P(None, ("rows", "seq")),
        ),
        check_vma=False,
    )
```

profile of v0, /device:TPU:0, one launch (start us, length us, event | category | flops | bytes accessed | tf_op | source)
XLA Modules:
  0.0 2308.1 jit_solution(12478468952239144224)
XLA Ops:
  8.0 64.8 %all-gather.41.cloned.1.call-done = bf16[2,3,512,512]{3,2,1,0:T(8,128)(2,1)} async-done(((bf16[2,3,16,512]{3,2,1,0:T(8,128)(2,1)}), bf16[2,3,512,512]{3,2,1,0:T(8,128)(2,1)}) %all-gather.41.cloned.1.call-update) | async-done | bytes 3145744 | tf_op jit(solution)/shard_map/all_gather | solution.py:114
  94.6 40.5 %all-reduce.6 = (bf16[1024]{0:T(1024)(128)(2,1)S(1)}, bf16[1024]{0:T(1024)(128)(2,1)S(1)}, bf16[1024]{0:T(1024)(128)(2,1)S(1)}, bf16[1024]{0:T(1024)(128)(2,1)S(1)}) all-reduce(bf16[1024]{0:T(1024)(128)(2,1)S(1)} %dynamic-update-slice.3, bf16[1024]{0:T(1024)(128)(2,1)S(1)} %dynamic-update-slice.2, ...), channel_id=11, replica_groups=mesh['rows'=2,'seq'=16] {'seq'}, use_global_device_ids=true, to_apply=%add.3 | all-reduce | flops 4096 | bytes 16384
  151.1 36.6 %all-gather.49.cloned.1.call-done = bf16[1024,512]{1,0:T(8,128)(2,1)} async-done(((bf16[64,512]{1,0:T(8,128)(2,1)}), bf16[1024,512]{1,0:T(8,128)(2,1)}) %all-gather.49.cloned.1.call-update) | async-done | bytes 1048592 | tf_op jit(solution)/shard_map/all_gather | solution.py:133
  189.2 55.2 %all-gather.51.cloned.1.call-done = bf16[1024,512]{1,0:T(8,128)(2,1)} async-done(((bf16[64,512]{1,0:T(8,128)(2,1)}), bf16[1024,512]{1,0:T(8,128)(2,1)}) %all-gather.51.cloned.1.call-update) | async-done | bytes 1048592 | tf_op jit(solution)/shard_map/all_gather | solution.py:134
  261.5 38.3 %all-gather.43.cloned.1.call-done = bf16[2,512,512]{2,1,0:T(8,128)(2,1)} async-done(((bf16[2,16,512]{2,1,0:T(8,128)(2,1)}), bf16[2,512,512]{2,1,0:T(8,128)(2,1)}) %all-gather.43.cloned.1.call-update) | async-done | bytes 1048592 | tf_op jit(solution)/shard_map/all_gather | solution.py:115
  302.9 53.8 %all-gather.55.cloned.1.call-done = bf16[1024,512]{1,0:T(8,128)(2,1)} async-done(((bf16[64,512]{1,0:T(8,128)(2,1)}), bf16[1024,512]{1,0:T(8,128)(2,1)}) %all-gather.55.cloned.1.call-update) | async-done | bytes 1048592 | tf_op jit(solution)/shard_map/all_gather | solution.py:134
  375.7 39.1 %all-gather.45.cloned.1.call-done = bf16[512,2048]{1,0:T(8,128)(2,1)} async-done(((bf16[16,2048]{1,0:T(8,128)(2,1)}), bf16[512,2048]{1,0:T(8,128)(2,1)}) %all-gather.45.cloned.1.call-update) | async-done | bytes 2097168 | tf_op jit(solution)/shard_map/all_gather | solution.py:116
  416.9 56.0 %all-gather.47.cloned.1.call-done = bf16[2048,512]{1,0:T(8,128)(2,1)} async-done(((bf16[64,512]{1,0:T(8,128)(2,1)}), bf16[2048,512]{1,0:T(8,128)(2,1)}) %all-gather.47.cloned.1.call-update) | async-done | bytes 2097168 | tf_op jit(solution)/shard_map/all_gather | solution.py:117
  475.9 53.9 %all-gather.61.cloned.1.call-done = bf16[1024,512]{1,0:T(8,128)(2,1)} async-done(((bf16[64,512]{1,0:T(8,128)(2,1)}), bf16[1024,512]{1,0:T(8,128)(2,1)}) %all-gather.61.cloned.1.call-update) | async-done | bytes 1048592 | tf_op jit(solution)/shard_map/all_gather | solution.py:133
  532.2 54.4 %all-gather.57.cloned.1.call-done = bf16[1024,512]{1,0:T(8,128)(2,1)} async-done(((bf16[64,512]{1,0:T(8,128)(2,1)}), bf16[1024,512]{1,0:T(8,128)(2,1)}) %all-gather.57.cloned.1.call-update) | async-done | bytes 1048592 | tf_op jit(solution)/shard_map/all_gather | solution.py:133
  588.1 55.4 %all-gather.59.cloned.1.call-done = bf16[1024,512]{1,0:T(8,128)(2,1)} async-done(((bf16[64,512]{1,0:T(8,128)(2,1)}), bf16[1024,512]{1,0:T(8,128)(2,1)}) %all-gather.59.cloned.1.call-update) | async-done | bytes 1048592 | tf_op jit(solution)/shard_map/all_gather | solution.py:134
  645.5 19.7 while.209
  673.4 26.7 %all-gather.63.cloned.1.call-done = bf16[1024,512]{1,0:T(8,128)(2,1)} async-done(((bf16[64,512]{1,0:T(8,128)(2,1)}), bf16[1024,512]{1,0:T(8,128)(2,1)}) %all-gather.63.cloned.1.call-update) | async-done | bytes 1048592 | tf_op jit(solution)/shard_map/all_gather | solution.py:134
  703.0 24.9 %while.203 = (s32[]{:T(128)}, f32[1,8,64]{2,1,0:T(8,128)S(1)}, f32[64,1,8,64]{0,3,2,1:T(8,128)S(1)}, s32[2]{0:T(128)}, s32[1,32]{1,0:T(1,128)}, /*index=5*/s32[1...) while((s32[]{:T(128)}, f32[1,8,64]{2,1,0:T(8,128)S(1)}, ...), condition=%wide.region_51.52_spmd, body=%wide.region_43.51_spmd.sunk | while | flops 68339400 | bytes 4610065 | solution.py:182
  748.0 26.2 %while.205 = (s32[]{:T(128)}, f32[64,1,8,64]{0,3,2,1:T(8,128)S(1)}, s32[2]{0:T(128)}, s32[1,32]{1,0:T(1,128)}, s32[1]{0:T(128)}, /*index=5*/s32[1]{0:T(128)}, bf...) while((s32[]{:T(128)}, f32[64,1,8,64]{0,3,2,1:T(8,128)S(1)}, ...), condition=%wide.region_98.99_spmd, body=%wide.region_91.98_spmd.sunk | while | flops 102188744 | bytes 6242305 | solution.py:241
  825.5 42.6 %all_gather.109 = f32[1024,1,8]{2,1,0:T(1,128)S(1)} all-gather(f32[64,1,8]{2,1,0:T(1,128)S(1)} %bitcast.1093), channel_id=1, replica_groups=mesh['rows'=2,'seq'=16] {'seq'}, dimensions={0}, use_global_device_ids=true | all-gather | bytes 34816 | tf_op jit(solution)/shard_map/all_gather | solution.py:244
  872.3 39.3 %all_gather.106 = f32[1024,1,8]{2,1,0:T(1,128)S(1)} all-gather(f32[64,1,8]{2,1,0:T(1,128)S(1)} %bitcast.1094), channel_id=1, replica_groups=mesh['rows'=2,'seq'=16] {'seq'}, dimensions={0}, use_global_device_ids=true | all-gather | bytes 34816 | tf_op jit(solution)/shard_map/all_gather | solution.py:244
  933.9 18.5 while.212
  956.9 41.0 %all_gather.115 = f32[1024,1,8]{2,1,0:T(1,128)S(1)} all-gather(f32[64,1,8]{2,1,0:T(1,128)S(1)} %bitcast.1087), channel_id=1, replica_groups=mesh['rows'=2,'seq'=16] {'seq'}, dimensions={0}, use_global_device_ids=true | all-gather | bytes 34816 | tf_op jit(solution)/shard_map/all_gather | solution.py:244
  999.8 39.5 %all_gather.112 = f32[1024,1,8]{2,1,0:T(1,128)S(1)} all-gather(f32[64,1,8]{2,1,0:T(1,128)S(1)} %bitcast.1088), channel_id=1, replica_groups=mesh['rows'=2,'seq'=16] {'seq'}, dimensions={0}, use_global_device_ids=true | all-gather | bytes 34816 | tf_op jit(solution)/shard_map/all_gather | solution.py:244
  1047.4 25.1 %while.213 = (s32[]{:T(128)}, f32[64,1,8,64]{0,3,2,1:T(8,128)S(1)}, f32[64,1,8,64]{0,3,2,1:T(8,128)}, s32[2]{0:T(128)}, s32[1,32]{1,0:T(1,128)}, /*index=5*/s32[...) while((s32[]{:T(128)}, f32[64,1,8,64]{0,3,2,1:T(8,128)S(1)}, ...), condition=%wide.region_115.116_spmd.clone, body=%wide.region_109.0_spmd.clone.sunk | while | flops 136134912 | bytes 8253465 | solution.py:299
  1105.2 25.1 %while.207 = (s32[]{:T(128)}, f32[64,1,8,64]{0,3,2,1:T(8,128)S(1)}, f32[64,1,8,64]{0,3,2,1:T(8,128)}, s32[2]{0:T(128)}, s32[1,32]{1,0:T(1,128)}, /*index=5*/s32[...) while((s32[]{:T(128)}, f32[64,1,8,64]{0,3,2,1:T(8,128)S(1)}, ...), condition=%wide.region_137.138_spmd, body=%wide.region_131.0_spmd.sunk | while | flops 136003776 | bytes 8250365 | solution.py:299
  1134.7 25.4 %all-gather.75.cloned.1.call-done = bf16[1024,512]{1,0:T(8,128)(2,1)} async-done(((bf16[64,512]{1,0:T(8,128)(2,1)}), bf16[1024,512]{1,0:T(8,128)(2,1)}) %all-gather.75.cloned.1.call-update) | async-done | bytes 1048592 | tf_op jit(solution)/shard_map/all_gather | solution.py:250
  1163.6 18.3 while.206
  1229.3 45.1 %all-reduce.5 = f32[2048]{0:T(1024)} all-reduce(f32[2048]{0:T(1024)S(1)} %add.1164), channel_id=36, replica_groups=mesh['rows'=2,'seq'=16] {'rows','seq'}, use_global_device_ids=true, to_apply=%region_163.164.clone | all-reduce | flops 2048 | bytes 16384
  1299.6 134.7 %reduce-scatter.26.cloned.1.call-done = f32[16,3]{1,0:T(8,128)} async-done(((f32[512,3]{1,0:T(8,128)}), f32[16,3]{1,0:T(8,128)}) %reduce-scatter.26.cloned.1.call-update) | async-done | bytes 208
  1435.7 134.6 %reduce-scatter.28.cloned.1.call-done = f32[16,3]{1,0:T(8,128)} async-done(((f32[512,3]{1,0:T(8,128)}), f32[16,3]{1,0:T(8,128)}) %reduce-scatter.28.cloned.1.call-update) | async-done | bytes 208
  1578.2 128.1 %reduce-scatter.22.cloned.1.call-done = f32[16,7]{1,0:T(8,128)} async-done(((f32[512,7]{1,0:T(8,128)}), f32[16,7]{1,0:T(8,128)}) %reduce-scatter.22.cloned.1.call-update) | async-done | bytes 464
  1707.6 156.9 %all-reduce.9.cloned.1.call-done = f32[2,3,512,512]{3,0,1,2:T(2,128)} async-done(((f32[2,3,512,512]{3,0,1,2:T(2,128)}), f32[2,3,512,512]{3,0,1,2:T(2,128)}) %all-reduce.9.cloned.1.call-update) | async-done | bytes 6291472
  1866.2 143.1 %reduce-scatter.16.cloned.1.call-done = f32[2,16,512]{2,1,0:T(8,128)} async-done(((f32[2,512,512]{2,1,0:T(8,128)}), f32[2,16,512]{2,1,0:T(8,128)}) %reduce-scatter.16.cloned.1.call-update) | async-done | bytes 65552 | tf_op jit(solution)/shard_map/reduce_scatter | solution.py:451
  2009.3 145.1 %reduce-scatter.18.cloned.1.call-done = f32[16,2048]{1,0:T(8,128)} async-done(((f32[512,2048]{1,0:T(8,128)}), f32[16,2048]{1,0:T(8,128)}) %reduce-scatter.18.cloned.1.call-update) | async-done | bytes 131088 | tf_op jit(solution)/shard_map/reduce_scatter | solution.py:452
  2154.4 146.6 %reduce-scatter.20.cloned.1.call-done = f32[64,512]{1,0:T(8,128)} async-done(((f32[2048,512]{1,0:T(8,128)}), f32[64,512]{1,0:T(8,128)}) %reduce-scatter.20.cloned.1.call-update) | async-done | bytes 131088 | tf_op jit(solution)/shard_map/reduce_scatter | solution.py:453
  (1085 shorter events, 598.8 us)
Async XLA Ops:
  7.2 65.6 %all-gather.41.cloned.1.call-start = ((), (), s32[]{:S(2)}) async-start(), calls=%async_computation.7 | async-start | bytes 3244032 | tf_op jit(solution)/shard_map/all_gather | solution.py:114
  8.0 140.9 %all-gather.53.cloned.1.call-start = ((), (), s32[]{:S(2)}) async-start(), calls=%async_computation.13 | async-start | bytes 1114112 | tf_op jit(solution)/shard_map/all_gather | solution.py:133
  74.9 112.8 %all-gather.49.cloned.1.call-start = ((), (), s32[]{:S(2)}) async-start(), calls=%async_computation.11 | async-start | bytes 1114112 | tf_op jit(solution)/shard_map/all_gather | solution.py:133
  76.9 167.6 %all-gather.51.cloned.1.call-start = ((), (), s32[]{:S(2)}) async-start(), calls=%async_computation.12 | async-start | bytes 1114112 | tf_op jit(solution)/shard_map/all_gather | solution.py:134
  80.5 219.3 %all-gather.43.cloned.1.call-start = ((), (), s32[]{:S(2)}) async-start(), calls=%async_computation.8 | async-start | bytes 1081344 | tf_op jit(solution)/shard_map/all_gather | solution.py:115
  81.1 275.6 %all-gather.55.cloned.1.call-start = ((), (), s32[]{:S(2)}) async-start(), calls=%async_computation.14 | async-start | bytes 1114112 | tf_op jit(solution)/shard_map/all_gather | solution.py:134
  83.0 331.7 %all-gather.45.cloned.1.call-start = ((), (), s32[]{:S(2)}) async-start(), calls=%async_computation.9 | async-start | bytes 2162688 | tf_op jit(solution)/shard_map/all_gather | solution.py:116
  83.8 389.1 %all-gather.47.cloned.1.call-start = ((), (), s32[]{:S(2)}) async-start(), calls=%async_computation.10 | async-start | bytes 2162688 | tf_op jit(solution)/shard_map/all_gather | solution.py:117
  84.5 445.3 %all-gather.61.cloned.1.call-start = ((), (), s32[]{:S(2)}) async-start(), calls=%async_computation.17 | async-start | bytes 1114112 | tf_op jit(solution)/shard_map/all_gather | solution.py:133
  86.3 500.3 %all-gather.57.cloned.1.call-start = ((), (), s32[]{:S(2)}) async-start(), calls=%async_computation.15 | async-start | bytes 1114112 | tf_op jit(solution)/shard_map/all_gather | solution.py:133
  87.2 556.2 %all-gather.59.cloned.1.call-start = ((), (), s32[]{:S(2)}) async-start(), calls=%async_computation.16 | async-start | bytes 1114112 | tf_op jit(solution)/shard_map/all_gather | solution.py:134
  88.1 612.1 %all-gather.63.cloned.1.call-start = ((), (), s32[]{:S(2)}) async-start(), calls=%async_computation.18 | async-start | bytes 1114112 | tf_op jit(solution)/shard_map/all_gather | solution.py:134
  89.0 734.1 %all-gather.69.cloned.1.call-start = ((), (), s32[]{:S(2)}) async-start(), calls=%async_computation.21 | async-start | bytes 1114112 | tf_op jit(solution)/shard_map/all_gather | solution.py:249
  93.6 776.4 %all-gather.65.cloned.1.call-start = ((), (), s32[]{:S(2)}) async-start(), calls=%async_computation.19 | async-start | bytes 1114112 | tf_op jit(solution)/shard_map/all_gather | solution.py:249
  148.5 895.4 %all-gather.71.cloned.1.call-start = ((), (), s32[]{:S(2)}) async-start(), calls=%async_computation.22 | async-start | bytes 1114112 | tf_op jit(solution)/shard_map/all_gather | solution.py:250
  416.9 169.6 %copy-start.32 = (f32[64,2048]{1,0:T(8,128)}, f32[64,2048]{1,0:T(8,128)S(1)}, u32[]{:S(2)}) copy-start(f32[64,2048]{1,0:T(8,128)S(1)} %convolution_add_fusion.11) | copy-start | bytes 1572868
  475.2 169.7 %copy-start.194 = (f32[64]{0:T(128)}, f32[64]{0:T(128)S(1)}, u32[]{:S(2)}) copy-start(f32[64]{0:T(128)S(1)} %broadcast_multiply_fusion.3) | copy-start | bytes 772
  808.5 266.9 %all-gather.67.cloned.1.call-start = ((), (), s32[]{:S(2)}) async-start(), calls=%async_computation.20 | async-start | bytes 1114112 | tf_op jit(solution)/shard_map/all_gather | solution.py:250
  810.9 289.3 %all-gather.77.cloned.1.call-start = ((), (), s32[]{:S(2)}) async-start(), calls=%async_computation.25 | async-start | bytes 1114112 | tf_op jit(solution)/shard_map/all_gather | solution.py:249
  811.5 290.2 %all-gather.79.cloned.1.call-start = ((), (), s32[]{:S(2)}) async-start(), calls=%async_computation.26 | async-start | bytes 1114112 | tf_op jit(solution)/shard_map/all_gather | solution.py:250
  812.0 321.1 %all-gather.73.cloned.1.call-start = ((), (), s32[]{:S(2)}) async-start(), calls=%async_computation.23 | async-start | bytes 1114112 | tf_op jit(solution)/shard_map/all_gather | solution.py:249
  812.8 347.3 %all-gather.75.cloned.1.call-start = ((), (), s32[]{:S(2)}) async-start(), calls=%async_computation.24 | async-start | bytes 1114112 | tf_op jit(solution)/shard_map/all_gather | solution.py:250
  869.0 429.3 %reduce-scatter.24.cloned.1.call-start = ((), (), s32[]{:S(2)}) async-start(), calls=%async_computation.31 | async-start | bytes 270336
  956.8 477.6 %reduce-scatter.26.cloned.1.call-start = ((), (), s32[]{:S(2)}) async-start(), calls=%async_computation.32 | async-start | bytes 270336
  999.6 570.7 %reduce-scatter.28.cloned.1.call-start = ((), (), s32[]{:S(2)}) async-start(), calls=%async_computation.33 | async-start | bytes 270336
  1043.6 662.7 %reduce-scatter.22.cloned.1.call-start = ((), (), s32[]{:S(2)}) async-start(), calls=%async_computation.30 | async-start | bytes 270336
  1195.9 668.6 %all-reduce.9.cloned.1.call-start = ((), (), s32[]{:S(2)}) async-start(), calls=%async_computation.34 | async-start | bytes 12582912
  1216.1 793.3 %reduce-scatter.16.cloned.1.call-start = ((), (), s32[]{:S(2)}) async-start(), calls=%async_computation.27 | async-start | bytes 2162688 | tf_op jit(solution)/shard_map/reduce_scatter | solution.py:451
  1220.2 934.2 %reduce-scatter.18.cloned.1.call-start = ((), (), s32[]{:S(2)}) async-start(), calls=%async_computation.28 | async-start | bytes 4325376 | tf_op jit(solution)/shard_map/reduce_scatter | solution.py:452
  1223.9 1077.1 %reduce-scatter.20.cloned.1.call-start = ((), (), s32[]{:S(2)}) async-start(), calls=%async_computation.29 | async-start | bytes 4325376 | tf_op jit(solution)/shard_map/reduce_scatter | solution.py:453
  1279.1 296.3 %copy-start.54 = (bf16[64,1,8,64]{0,3,2,1:T(8,128)(2,1)S(1)}, bf16[64,1,8,64]{0,3,2,1:T(8,128)(2,1)}, u32[]{:S(2)}) copy-start(bf16[64,1,8,64]{0,3,2,1:T(8,128)(2,1)} %get-tuple-element.5379) | copy-start | bytes 196612
  1281.0 295.3 %copy-start.56 = (bf16[64,1,8,64]{0,3,2,1:T(8,128)(2,1)S(1)}, bf16[64,1,8,64]{0,3,2,1:T(8,128)(2,1)}, u32[]{:S(2)}) copy-start(bf16[64,1,8,64]{0,3,2,1:T(8,128)(2,1)} %convert_element_type.1589) | copy-start | bytes 196612
  (231 other events, 6037.1 us)
Sparse Core Ops, SparseCore 0:
  10.9 61.8 all-gather.40
  76.1 54.5 all-gather.52
  133.5 54.1 all-gather.48
  190.4 54.0 all-gather.50
  247.2 52.5 all-gather.42
  302.4 54.2 all-gather.54
  359.5 55.2 all-gather.44
  417.6 55.2 all-gather.46
  475.7 54.1 all-gather.60
  532.4 54.0 all-gather.56
  589.3 54.0 all-gather.58
  646.0 54.0 all-gather.62
  702.9 54.1 all-gather.68
  759.7 54.0 all-gather.64
  816.5 56.0 all-gather.70
  875.2 54.8 all-gather.66
  932.6 56.1 all-gather.76
  991.4 54.5 all-gather.78
  1048.8 54.4 all-gather.72
  1105.9 54.1 all-gather.74
  1162.3 135.9 reduce-scatter.23
  1300.6 133.7 reduce-scatter.25
  1436.6 133.7 reduce-scatter.27
  1572.5 133.7 reduce-scatter.21
  1711.9 152.5 all-reduce.8
  1867.3 141.9 reduce-scatter.15
  2012.0 142.3 reduce-scatter.17
  2157.3 143.7 reduce-scatter.19
where the time goes:
time: 2320 us; the launch traced here: 2310 us
  waiting for transfers between devices  1570 us (68%)
  blocking collectives  248 us (11%)
  local copies, waits for them, and re-layouts  155 us (7%)
  matrix products  119 us (5%)
  other arithmetic  116 us (5%)
  loops' own time  78.7 us (3%)
    unnamed x33, waiting for transfers between devices  576 us
    all_gather x4, waiting for transfers between devices, attend(): lax.all_gather(values, 'seq', axis=0, tiled=True)  191 us
    all_gather x4, blocking collectives, attention_back(): all_lambdas = lax.all_gather(lambdas, 'seq', axis=0, tiled=True)  162 us
    reduce_scatter x1, waiting for transfers between devices, local(): lax.psum_scatter(grads[3], ('rows', 'seq'), scatter_dimension=0, tiled=True)  147 us
    reduce_scatter x1, waiting for transfers between devices, local(): lax.psum_scatter(grads[2], ('rows', 'seq'), scatter_dimension=0, tiled=True)  145 us
    all_gather x4, waiting for transfers between devices, attend(): lax.all_gather(keys, 'seq', axis=0, tiled=True)  145 us
    reduce_scatter x1, waiting for transfers between devices, local(): lax.psum_scatter(grads[1], ('rows', 'seq'), scatter_dimension=1, tiled=True)  143 us
    unnamed x2, blocking collectives  85.7 us
  transfers between devices with their start and end apart: 28, of which 20 were waited for; matrix products, arithmetic and copies ran while one was open for 17% of the time, Pallas kernels for 0%

commit v1 on v0

--- a/solution.py
+++ b/solution.py
@@ -1,8 +1,11 @@
+import functools
 import math
 
 import jax
 import jax.numpy as jnp
 from jax import lax
+from jax.experimental import pallas as pl
+from jax.experimental.pallas import tpu as pltpu
 from jax.sharding import PartitionSpec as P
 
 HEADS = 8
@@ -465,9 +468,9 @@
     )
 
 
-def solution(mesh):
+def over(mesh, function):
     return jax.shard_map(
-        local,
+        function,
         mesh=mesh,
         in_specs=(
             P(None, "seq", "rows", None),
@@ -503,3 +506,749 @@
         ),
         check_vma=False,
     )
+
+
+def general(mesh):
+    return over(mesh, local)
+
+
+MESH = pl.DeviceIdType.MESH
+F32 = jnp.float32
+BF16 = jnp.bfloat16
+PLANES, YS, XS, CORES = 4, 2, 2, 2
+GROUP = YS * XS * CORES
+
+
+def nn(left, right):
+    return lax.dot_general(left, right, (((1,), (0,)), ((), ())), preferred_element_type=F32)
+
+
+def nt(left, right):
+    return lax.dot_general(left, right, (((1,), (1,)), ((), ())), preferred_element_type=F32)
+
+
+def tn(left, right):
+    return lax.dot_general(left, right, (((0,), (0,)), ((), ())), preferred_element_type=F32)
+
+
+def flip(value):
+    return jnp.transpose(value.astype(F32))
+
+
+def fused_kernel(
+    tok, mem, cot, meta, s_in, s_out, s_up, s_dn, biases, up_bias, gain, shift, omega,
+    o_res, o_tok, o_mem, o_in, o_out, o_up, o_dn, o_bias, o_upb, o_gain, o_shift, o_omega,
+    w_in, w_out, w_up, w_dn, g_in, g_out, g_up, g_dn,
+    c_in, c_out, c_up, c_dn,
+    p_in, p_out, p_up, p_dn,
+    q_in, q_out, q_up, q_dn,
+    z_in, z_out, z_up, z_dn,
+    in_tok, in_mem, in_cot, in_meta, all_meta,
+    a1, b1, a2, b2, a3, b3, a4, b4, a5, b5, a6, b6, a7, b7, a8, b8, a9, b9,
+    out_res, out_tok, out_mem,
+    sg0, sg1, sg2, sg3, sg4, sr0, sr1, sr2, sr3,
+    code_self, code_cross, key_pos, rows_f,
+    qt0, kt0, vt0, k0, v0, pt0, l0, ot0,
+    qt1, kt1, vt1, k1, v1, pt1, l1, ot1,
+    dnt, acc_k, acc_v, acc_q,
+    act, slope, xh0, xh1, xh2, h1_f, h2_f,
+    ss, rs,
+):
+    c = lax.axis_index("rows")
+    seq = lax.axis_index("seq")
+    z = seq // (YS * XS)
+    yx = lax.rem(seq, YS * XS)
+    y = yx // XS
+    x = lax.rem(yx, XS)
+    width = 512
+    here = 2 * 64
+
+    def at(zz, yy, xx):
+        return zz * (YS * XS) + yy * XS + xx
+
+    def slot(cc, yy, xx):
+        return cc * 4 + yy * 2 + xx
+
+    def head(cc, yy, xx):
+        return (yy * 2 + xx) * 2 + cc
+
+    me_slot, me_head = slot(c, y, x), head(c, y, x)
+    plane_peers = []
+    for k in range(1, GROUP):
+        cc = 1 - c if k & 4 else c
+        yy = 1 - y if k & 2 else y
+        xx = 1 - x if k & 1 else x
+        plane_peers.append((cc, yy, xx))
+    z_peers = [lax.rem(z + k, PLANES) for k in (1, 2, 3)]
+
+    barrier = pltpu.get_barrier_semaphore()
+    greet = [(cc, at(z, yy, xx)) for cc, yy, xx in plane_peers]
+    greet += [(cc, at(zz, y, x)) for zz in z_peers for cc in (c, 1 - c)]
+    for device in greet:
+        pl.semaphore_signal(barrier, inc=1, device_id=device, device_id_type=MESH)
+    pl.semaphore_wait(barrier, len(greet))
+
+    names = {}
+    pending = []
+
+    def sem(name):
+        return names.setdefault(name, len(names))
+
+    def wait(semaphore, ref):
+        pltpu.make_async_copy(ref, ref, semaphore).wait()
+
+    def send(name, src, dst, device):
+        i = sem(name)
+        pltpu.make_async_remote_copy(
+            src_ref=src, dst_ref=dst, send_sem=ss.at[i], recv_sem=rs.at[i], device_id=device, device_id_type=MESH
+        ).start()
+
+    def keep(name, src, dst):
+        pltpu.make_async_copy(src, dst, rs.at[sem(name)]).start()
+
+    def landed(name, ref):
+        wait(rs.at[sem(name)], ref)
+
+    def sent_later(name, ref):
+        pending.append((name, ref))
+
+    def to_plane(name, src, dst):
+        for m in range(2):
+            plane = 2 * m + c
+            core = z // 2
+            half = lax.rem(z, 2)
+            own = (plane == z) & (core == c)
+            part = dst.at[half]
+
+            @pl.when(own)
+            def _():
+                keep(name, src.at[m], part)
+
+            @pl.when(jnp.logical_not(own))
+            def _():
+                i = sem(name)
+                j = sem(name + str(m))
+                pltpu.make_async_remote_copy(
+                    src_ref=src.at[m], dst_ref=part, send_sem=ss.at[j], recv_sem=rs.at[i],
+                    device_id=(core, at(plane, y, x)), device_id_type=MESH,
+                ).start()
+
+            pending.append((name + str(m), src.at[m], jnp.logical_not(own)))
+
+    def from_plane(name, src, dst):
+        micro, core = z // 2, lax.rem(z, 2)
+        for half in range(2):
+            zz = 2 * c + half
+            own = (core == c) & (zz == z)
+            part = dst.at[micro]
+
+            @pl.when(own)
+            def _():
+                keep(name, src.at[half], part)
+
+            @pl.when(jnp.logical_not(own))
+            def _():
+                i = sem(name)
+                j = sem(name + str(half))
+                pltpu.make_async_remote_copy(
+                    src_ref=src.at[half], dst_ref=part, send_sem=ss.at[j], recv_sem=rs.at[i],
+                    device_id=(core, at(zz, y, x)), device_id_type=MESH,
+                ).start()
+
+            pending.append((name + str(half), src.at[half], jnp.logical_not(own)))
+
+    def to_heads(name, src, dst):
+        keep(name, src.at[me_head], dst.at[me_slot])
+        for cc, yy, xx in plane_peers:
+            send(name, src.at[head(cc, yy, xx)], dst.at[me_slot], (cc, at(z, yy, xx)))
+        sent_later(name, src.at[pl.ds(0, GROUP - 1)])
+
+    def to_slots(name, src, dst):
+        keep(name, src.at[me_slot], dst.at[me_head])
+        for cc, yy, xx in plane_peers:
+            send(name, src.at[slot(cc, yy, xx)], dst.at[me_head], (cc, at(z, yy, xx)))
+        sent_later(name, src.at[pl.ds(0, GROUP - 1)])
+
+    weights = {
+        "in0": (w_in.at[0], s_in.at[0], g_in.at[0], c_in.at[0], p_in.at[0], q_in.at[0], z_in.at[0], o_in.at[0]),
+        "in1": (w_in.at[1], s_in.at[1], g_in.at[1], c_in.at[1], p_in.at[1], q_in.at[1], z_in.at[1], o_in.at[1]),
+        "out": (w_out, s_out, g_out, c_out, p_out, q_out, z_out, o_out),
+        "up": (w_up, s_up, g_up, c_up, p_up, q_up, z_up, o_up),
+        "dn": (w_dn, s_dn, g_dn, c_dn, p_dn, q_dn, z_dn, o_dn),
+    }
+
+    def halves(ref):
+        cols = ref.shape[-1] // 2
+        return pl.ds(0, cols), pl.ds(cols, cols)
+
+    x_next, y_next, core_next = (c, at(z, y, 1 - x)), (c, at(z, 1 - y, x)), (1 - c, seq)
+
+    def gather_z(g):
+        full, shard = weights[g][:2]
+        keep(g + "z", shard, full.at[:, c, z, y, x])
+        for zz in z_peers:
+            send(g + "z", shard, full.at[:, c, z, y, x], (c, at(zz, y, x)))
+        sent_later(g + "z", full.at[:, c, pl.ds(0, 3), y, x])
+
+    def gather_1(g):
+        full = weights[g][0]
+        first, second = halves(full)
+        landed(g + "z", full.at[:, c, :, y, x])
+        part = full.at[:, c, :, y, x, :, first]
+        send(g + "1a", part, part, x_next)
+        sent_later(g + "1a", part)
+        part = full.at[:, c, :, y, x, :, second]
+        send(g + "1b", part, part, y_next)
+        sent_later(g + "1b", part)
+
+    def gather_2(g):
+        full = weights[g][0]
+        first, second = halves(full)
+        landed(g + "1a", full.at[:, c, :, y, 1 - x, :, first])
+        part = full.at[:, c, :, y, :, :, first]
+        send(g + "2a", part, part, y_next)
+        sent_later(g + "2a", part)
+        landed(g + "1b", full.at[:, c, :, 1 - y, x, :, second])
+        part = full.at[:, c, :, :, x, :, second]
+        send(g + "2b", part, part, x_next)
+        sent_later(g + "2b", part)
+
+    def gather_3(g):
+        full = weights[g][0]
+        first, second = halves(full)
+        landed(g + "2a", full.at[:, c, :, 1 - y, :, :, first])
+        landed(g + "2b", full.at[:, c, :, :, 1 - x, :, second])
+        send(g + "3", full.at[:, c], full.at[:, c], core_next)
+        sent_later(g + "3", full.at[:, c])
+
+    def gathered(g):
+        landed(g + "3", weights[g][0].at[:, 1 - c])
+
+    def add(target, other):
+        target[...] = (target[...].astype(F32) + other[...].astype(F32)).astype(BF16)
+
+    def scatter_0(g):
+        grad, across = weights[g][2:4]
+        send(g + "r0", grad.at[:, 1 - c], across, core_next)
+        sent_later(g + "r0", across)
+
+    def scatter_1(g):
+        grad, across, part = weights[g][2:5]
+        first, second = halves(grad)
+        landed(g + "r0", across)
+        for lead in range(grad.shape[0]):
+
+            @pl.loop(0, PLANES)
+            def _(zz):
+                add(grad.at[lead, c, zz], across.at[lead, zz])
+
+        send(g + "r1a", grad.at[:, c, :, 1 - y, :, :, first], part.at[0], y_next)
+        sent_later(g + "r1a", part.at[0])
+        send(g + "r1b", grad.at[:, c, :, :, 1 - x, :, second], part.at[1], x_next)
+        sent_later(g + "r1b", part.at[1])
+
+    def scatter_2(g):
+        grad, _, part, piece = weights[g][2:6]
+        first, second = halves(grad)
+        landed(g + "r1a", part.at[0])
+        landed(g + "r1b", part.at[1])
+        for lead in range(grad.shape[0]):
+
+            @pl.loop(0, PLANES)
+            def _(zz):
+                add(grad.at[lead, c, zz, y, :, :, first], part.at[0, lead, zz])
+                add(grad.at[lead, c, zz, :, x, :, second], part.at[1, lead, zz])
+
+        send(g + "r2a", grad.at[:, c, :, y, 1 - x, :, first], piece.at[0], x_next)
+        sent_later(g + "r2a", piece.at[0])
+        send(g + "r2b", grad.at[:, c, :, 1 - y, x, :, second], piece.at[1], y_next)
+        sent_later(g + "r2b", piece.at[1])
+
+    def scatter_3(g):
+        grad, _, _, piece, line = weights[g][2:7]
+        first, second = halves(grad)
+        landed(g + "r2a", piece.at[0])
+        landed(g + "r2b", piece.at[1])
+        for lead in range(grad.shape[0]):
+
+            @pl.loop(0, PLANES)
+            def _(zz):
+                add(grad.at[lead, c, zz, y, x, :, first], piece.at[0, lead, zz])
+                add(grad.at[lead, c, zz, y, x, :, second], piece.at[1, lead, zz])
+
+        for k in range(3):
+            send(g + "r3", grad.at[:, c, z_peers[k], y, x], line.at[2 - k], (c, at(z_peers[k], y, x)))
+        sent_later(g + "r3", line)
+
+    def scattered(g):
+        grad, _, _, _, line, result = weights[g][2:8]
+        landed(g + "r3", line)
+        total = grad[:, c, z, y, x].astype(F32)
+        for k in range(3):
+            total = total + line[k].astype(F32)
+        result[...] = total
+
+    def matrix(ref):
+        return ref[...].reshape(-1, ref.shape[-1])
+
+    def put(ref, value):
+        ref[...] = value.astype(BF16).reshape(ref.shape)
+
+    def norm(r, i, kept):
+        centered = r - jnp.mean(r, axis=1, keepdims=True)
+        scale = lax.rsqrt(jnp.mean(centered * centered, axis=1, keepdims=True) + 1e-05)
+        xhat = centered * scale
+        kept[...] = xhat
+        return xhat * gain[i : i + 1, :] + shift[i : i + 1, :], scale
+
+    def column(row, value):
+        sg0[row : row + 1, :] = jnp.sum(value, axis=0, keepdims=True)
+
+    def norm_back(grad, i, kept, scale, skip):
+        xhat = kept[...]
+        column(11 + i, grad * xhat)
+        column(14 + i, grad)
+        dxhat = grad * gain[i : i + 1, :]
+        dr = dxhat - jnp.mean(dxhat, axis=1, keepdims=True)
+        dr = (dr - xhat * jnp.mean(dxhat * xhat, axis=1, keepdims=True)) * scale
+        column(17 + i, dr * skip)
+        return dr, dr * omega[i : i + 1, :]
+
+    def take(index, buffer, queries, keys, keys_t, values, values_t, which):
+        for s in range(GROUP):
+            cols = slice(s * here, (s + 1) * here)
+            if "q" in which:
+                queries[:, cols] = (buffer[(s,) + index["q"]].astype(F32) * 0.125).astype(BF16)
+            if "k" in which:
+                block = buffer[(s,) + index["k"]]
+                keys_t[:, cols] = block
+                keys[cols, :] = flip(block).astype(BF16)
+                block = buffer[(s,) + index["v"]]
+                values_t[:, cols] = block
+                values[cols, :] = flip(block).astype(BF16)
+
+    BLOCK = 256
+
+    def attend(queries, keys, values_t, weights_t, sums, outputs, causal, target):
+        def make(extent):
+            def body(b):
+                cols = pl.ds(pl.multiple_of(b * BLOCK, BLOCK), BLOCK)
+                scores = nn(keys[:extent, :], queries[:, cols])
+                seg = rows_f[0:1, cols]
+                code = (code_self if causal else code_cross)[:extent, :]
+                permit = jnp.concatenate([code, code], axis=1) == seg
+                if causal:
+                    pos = key_pos[:extent, :]
+                    pos = jnp.concatenate([pos, pos], axis=1)
+                    mine = rows_f[1:2, cols]
+                    permit = (permit & (pos <= mine)) | (pos == mine)
+                weight = jnp.where(permit, jnp.exp(scores), 0.0)
+                total = jnp.sum(weight, axis=0, keepdims=True)
+                low = weight.astype(BF16)
+                weights_t[:extent, cols] = low
+                out = nn(values_t[:, :extent], low) / total
+                sums[0:1, cols] = total
+                outputs[:, cols] = out
+
+            return body
+
+        if causal:
+            pl.loop(0, 2)(make(512))
+            pl.loop(2, 4)(make(1024))
+        else:
+            pl.loop(0, 4)(make(1024))
+        for s in range(GROUP):
+            target[s] = outputs[:, s * here : (s + 1) * here].astype(BF16)
+
+    def attend_back(buffer, queries, keys_t, values, weights_t, sums, outputs, causal, target):
+        acc_k[...] = jnp.zeros_like(acc_k)
+        acc_v[...] = jnp.zeros_like(acc_v)
+        for s in range(GROUP):
+            cols = slice(s * here, (s + 1) * here)
+            grad = buffer[s].astype(F32)
+            inverse = 1.0 / sums[0:1, cols]
+            dnt[:, cols] = (grad * inverse).astype(BF16)
+            rows_f[2:3, cols] = -jnp.sum(grad * outputs[:, cols], axis=0, keepdims=True) * inverse
+
+        def make(extent):
+            def body(b):
+                cols = pl.ds(pl.multiple_of(b * BLOCK, BLOCK), BLOCK)
+                low = weights_t[:extent, cols]
+                dn = dnt[:, cols]
+                spread = nn(values[:extent, :], dn)
+                slopes = (low.astype(F32) * (spread + rows_f[2:3, cols])).astype(BF16)
+                acc_q[:, cols] = nn(keys_t[:, :extent], slopes) * 0.125
+                acc_k[:, :extent] += nt(queries[:, cols], slopes)
+                acc_v[:, :extent] += nt(dn, low)
+
+            return body
+
+        if causal:
+            pl.loop(0, 2)(make(512))
+            pl.loop(2, 4)(make(1024))
+        else:
+            pl.loop(0, 4)(make(1024))
+        for s in range(GROUP):
+            cols = slice(s * here, (s + 1) * here)
+            target[s, 0] = acc_q[:, cols].astype(BF16)
+            target[s, 1] = acc_k[:, cols].astype(BF16)
+            target[s, 2] = acc_v[:, cols].astype(BF16)
+
+    def by_head(target, index, value):
+        low = flip(value).astype(BF16).reshape(GROUP, 64, here)
+        target[(slice(None),) + index] = low
+
+    def bias(i):
+        return biases[i : i + 1, :]
+
+    to_plane("meta", meta, in_meta)
+    to_plane("tok", tok, in_tok)
+    gather_z("in0")
+    to_plane("mem", mem, in_mem)
+    gather_z("in1")
+    gather_z("out")
+    to_plane("cot", cot, in_cot)
+    gather_z("up")
+    gather_z("dn")
+
+    landed("meta", in_meta)
+    lane = lax.broadcasted_iota(jnp.int32, (8, 128), 1)
+    all_meta[me_slot] = jnp.where(lane < 64, in_meta[0], in_meta[1])
+    for cc, yy, xx in plane_peers:
+        send("marks", all_meta.at[me_slot], all_meta.at[me_slot], (cc, at(z, yy, xx)))
+    sent_later("marks", all_meta.at[pl.ds(0, 7)])
+    gather_1("in0")
+    gather_1("in1")
+    gather_2("in0")
+    gather_1("out")
+    gather_2("in1")
+    gather_3("in0")
+    gather_1("up")
+    gathered("in0")
+    landed("tok", in_tok)
+
+    words = in_tok[...].reshape(here, width)
+    for j, extra in ((0, 0), (1, None), (2, 1)):
+        value = nn(words, matrix(w_in.at[0, j]))
+        by_head(a1, (j,), value if extra is None else value + bias(extra))
+    to_heads("x1", a1, b1)
+    gather_3("in1")
+    gather_2("out")
+    gather_1("dn")
+    gathered("in1")
+    landed("mem", in_mem)
+    sources = in_mem[...].reshape(here, width)
+    by_head(a2, (0,), nn(sources, matrix(w_in.at[1, 1])))
+    by_head(a2, (1,), nn(sources, matrix(w_in.at[1, 2])) + bias(4))
+    to_heads("x2", a2, b2)
+    gather_3("out")
+
+    landed("marks", all_meta.at[pl.ds(0, 7)])
+    order = lax.broadcasted_iota(jnp.int32, (1, 1024), 1)
+    place = (order // 512) * 512 + lax.rem(order // 64, 2) * 256 + lax.rem(order // 128, 4) * 64 + lax.rem(order, 64)
+    place = place.astype(F32)
+    marks = [all_meta[s].astype(F32) for s in range(GROUP)]
+    tgt_real = jnp.concatenate([mark[0:1, :] for mark in marks], axis=1)
+    src_real = jnp.concatenate([mark[1:2, :] for mark in marks], axis=1)
+    lower = lax.broadcasted_iota(jnp.int32, (32, 128), 1)
+    later = lax.broadcasted_iota(jnp.int32, (32, 128), 0)
+
+    def ends_of(row):
+        lengths = jnp.broadcast_to(row, (32, 128))
+        ends = jnp.sum(jnp.where(lower <= later, lengths, 0.0), axis=1, keepdims=True)
+        starts = jnp.sum(jnp.where(lower < later, lengths, 0.0), axis=1, keepdims=True)
+        return ends, starts
+
+    def count(flags):
+        return jnp.sum(jnp.where(flags, 1.0, 0.0), axis=0, keepdims=True)
+
+    tgt_ends, _ = ends_of(marks[0][2:3, :])
+    src_ends, src_starts = ends_of(marks[0][3:4, :])
+    tgt_seg = count(tgt_ends <= place)
+    src_seg = count(src_ends <= place)
+    src_first = count(src_starts == place)
+    self_row = jnp.where(tgt_real > 0.5, tgt_seg, -1.0)
+    cross_row = jnp.where((src_real > 0.5) | (src_first > 0.5), src_seg, -1.0)
+    rows_f[0:1, :] = tgt_seg
+    rows_f[1:2, :] = place
+    code_self[...] = jnp.transpose(jnp.broadcast_to(self_row, (128, 1024)))
+    code_cross[...] = jnp.transpose(jnp.broadcast_to(cross_row, (128, 1024)))
+    key_pos[...] = jnp.transpose(jnp.broadcast_to(place, (128, 1024)))
+
+    landed("x1", b1)
+    take({"q": (0,), "k": (1,), "v": (2,)}, b1, qt0, k0, kt0, v0, vt0, "qk")
+    attend(qt0, k0, vt0, pt0, l0, ot0, True, a3)
+    to_slots("x3", a3, b3)
+    gather_2("up")
+    gather_2("dn")
+    gathered("out")
+    landed("x2", b2)
+    take({"k": (0,), "v": (1,)}, b2, qt1, k1, kt1, v1, vt1, "k")
+
+    landed("x3", b3)
+    words_f = words.astype(F32)
+    branch = tn(b3[...].reshape(width, here), matrix(w_out.at[0])) + bias(2)
+    h1, scale0 = norm(words_f * omega[0:1, :] + branch, 0, xh0)
+    h1_f[...] = h1
+    h1_low = h1.astype(BF16)
+    by_head(a4, (), nn(h1_low, matrix(w_in.at[1, 0])) + bias(3))
+    to_heads("x4", a4, b4)
+
+    landed("x4", b4)
+    take({"q": ()}, b4, qt1, k1, kt1, v1, vt1, "q")
+    attend(qt1, k1, vt1, pt1, l1, ot1, False, a5)
+    to_slots("x5", a5, b5)
+    gather_3("up")
+    gather_3("dn")
+
+    landed("x5", b5)
+    branch = tn(b5[...].reshape(width, here), matrix(w_out.at[1])) + bias(5)
+    h2, scale1 = norm(h1_f[...] * omega[1:2, :] + branch, 1, xh1)
+    h2_f[...] = h2
+    h2_low = h2.astype(BF16)
+
+    gathered("up")
+    for k in range(4):
+        cols = slice(k * width, (k + 1) * width)
+        u = nn(h2_low, matrix(w_up.at[0, :, :, :, :, :, cols])) + up_bias[0:1, cols]
+        square = u * u
+        t = jnp.tanh(u * (0.7978845608028654 + 0.035677408136300125 * square))
+        act[:, cols] = (0.5 * u * (1.0 + t)).astype(BF16)
+        inner = 0.7978845608028654 + 0.10703222440890037 * square
+        slope[:, cols] = 0.5 * (1.0 + t) + 0.5 * u * (1.0 - t * t) * inner
+    gathered("dn")
+    branch = bias(6)
+    for k in range(4):
+        rows = w_dn.at[0, k // 2, pl.ds(2 * (k % 2), 2)]
+        branch = branch + nn(act[:, k * width : (k + 1) * width], matrix(rows))
+    h3, scale2 = norm(h2_f[...] * omega[2:3, :] + branch, 2, xh2)
+    out_res[...] = h3.astype(BF16).reshape(2, 64, width)
+    from_plane("res", out_res, o_res)
+
+    landed("cot", in_cot)
+    grad = in_cot[...].reshape(here, width).astype(F32)
+    dr, skip = norm_back(grad, 2, xh2, scale2, h2_f[...])
+    gf = dr.astype(BF16)
+    column(6, gf.astype(F32))
+    back = skip
+    for k in range(4):
+        cols = slice(k * width, (k + 1) * width)
+        part = act[:, cols]
+        put(g_dn.at[0, k // 2, pl.ds(2 * (k % 2), 2)], tn(part, gf))
+        gu = nt(gf, matrix(w_dn.at[0, k // 2, pl.ds(2 * (k % 2), 2)])) * slope[:, cols]
+        gu = gu.astype(BF16)
+        column(7 + k, gu.astype(F32))
+        put(g_up.at[0, :, :, :, :, :, cols], tn(h2_low, gu))
+        back = back + nt(gu, matrix(w_up.at[0, :, :, :, :, :, cols]))
+    scatter_0("dn")
+    scatter_0("up")
+
+    dr, skip = norm_back(back, 1, xh1, scale1, h1_f[...])
+    gc = dr.astype(BF16)
+    column(5, gc.astype(F32))
+    by_head(a6, (), nt(gc, matrix(w_out.at[1])))
+    to_heads("x6", a6, b6)
+    back = skip
+    put(g_out.at[1], nn(b5[...].reshape(width, here), gc))
+    scatter_1("dn")
+    scatter_1("up")
+
+    landed("x6", b6)
+    attend_back(b6, qt1, kt1, v1, pt1, l1, ot1, False, a7)
+    to_slots("x7", a7, b7)
+    scatter_2("dn")
+    scatter_2("up")
+
+    landed("x7", b7)
+    dq, dk, dv = (b7[:, j].reshape(width, here) for j in range(3))
+    dq_row, dv_row = flip(dq), flip(dv)
+    column(3, dq_row)
+    column(4, dv_row)
+    back = back + nt(dq_row.astype(BF16), matrix(w_in.at[1, 0]))
+    dr, skip = norm_back(back, 0, xh0, scale0, words_f)
+    ga = dr.astype(BF16)
+    column(2, ga.astype(F32))
+    by_head(a8, (), nt(ga, matrix(w_out.at[0])))
+    to_heads("x8", a8, b8)
+    back = skip
+    put(g_out.at[0], nn(b3[...].reshape(width, here), ga))
+    scatter_0("out")
+    h1_t = flip(h1_low).astype(BF16)
+    put(g_in.at[1, 0], nt(h1_t, dq))
+    sources_t = flip(sources).astype(BF16)
+    put(g_in.at[1, 1], nt(sources_t, dk))
+    put(g_in.at[1, 2], nt(sources_t, dv))
+    scatter_0("in1")
+    grad_mem = nt(flip(dk).astype(BF16), matrix(w_in.at[1, 1])) + nt(dv_row.astype(BF16), matrix(w_in.at[1, 2]))
+    out_mem[...] = grad_mem.astype(BF16).reshape(2, 64, width)
+    from_plane("gmem", out_mem, o_mem)
+    scatter_3("dn")
+    scatter_3("up")
+    scatter_1("out")
+    scatter_1("in1")
+
+    landed("x8", b8)
+    attend_back(b8, qt0, kt0, v0, pt0, l0, ot0, True, a9)
+    to_slots("x9", a9, b9)
+    scatter_2("out")
+    scatter_2("in1")
+    scattered("dn")
+    scattered("up")
+
+    landed("x9", b9)
+    dq, dk, dv = (b9[:, j].reshape(width, here) for j in range(3))
+    words_t = flip(words).astype(BF16)
+    for j, value in enumerate((dq, dk, dv)):
+        put(g_in.at[0, j], nt(words_t, value))
+    scatter_0("in0")
+    for j, value in enumerate((dq, dk, dv)):
+        value = flip(value)
+        if j != 1:
+            column(j // 2, value)
+        back = back + nt(value.astype(BF16), matrix(w_in.at[0, j]))
+    out_tok[...] = back.astype(BF16).reshape(2, 64, width)
+    from_plane("gtok", out_tok, o_tok)
+
+    send("s0", sg0, sr0, core_next)
+    sent_later("s0", sr0)
+    scatter_1("in0")
+    scatter_3("out")
+    landed("s0", sr0)
+    sg1[...] = sg0[...] + sr0[...]
+    send("s1", sg1, sr1, y_next)
+    sent_later("s1", sr1)
+    scatter_3("in1")
+    landed("s1", sr1)
+    sg2[...] = sg1[...] + sr1[...]
+    send("s2", sg2, sr2, x_next)
+    sent_later("s2", sr2)
+    scatter_2("in0")
+    landed("s2", sr2)
+    sg3[...] = sg2[...] + sr2[...]
+    for k in range(3):
+        send("s3", sg3, sr3.at[2 - k], (c, at(z_peers[k], y, x)))
+    sent_later("s3", sr3)
+    scatter_3("in0")
+    scattered("out")
+    scattered("in1")
+    landed("s3", sr3)
+    sg0_total = sg3[...] + sr3[0] + sr3[1] + sr3[2]
+    sg4[...] = sg0_total
+    block = c * 16 + seq
+    tile = sg4[:, pl.ds(pl.multiple_of((block // 8) * 128, 128), 128)]
+    turned = pltpu.roll(tile, lax.rem(128 - lax.rem(block, 8) * 16, 128), 1)
+    o_bias[...] = turned[0:7, 0:16]
+    o_gain[...] = turned[11:14, 0:16]
+    o_shift[...] = turned[14:17, 0:16]
+    o_omega[...] = turned[17:20, 0:16]
+    tile = sg4[:, pl.ds(pl.multiple_of((lax.rem(block, 8) // 2) * 128, 128), 128)]
+    turned = pltpu.roll(tile, lax.rem(block, 2) * 64, 1)
+    wanted = block // 8
+    row = jnp.zeros((1, 64), F32)
+    for k in range(4):
+        row = row + turned[7 + k : 8 + k, 0:64] * (wanted == k).astype(F32)
+    o_upb[...] = row
+    scattered("in0")
+
+    landed("res", o_res)
+    landed("gmem", o_mem)
+    landed("gtok", o_tok)
+    for entry in pending:
+        if len(entry) == 2:
+            wait(ss.at[sem(entry[0])], entry[1])
+        else:
+
+            @pl.when(entry[2])
+            def _():
+                wait(ss.at[sem(entry[0])], entry[1])
+
+    assert len(names) <= ss.shape[0], len(names)
+
+
+def fused_local(
+    tokens, memory, cotangent, tgt_lengths, src_lengths, tgt_mask, src_mask, attn_in, attn_out, w_up, w_down,
+    biases, up_bias, norm_gain, norm_shift, omega,
+):
+    tgt_row = jnp.transpose(tgt_mask, (0, 2, 1))
+    src_row = jnp.transpose(src_mask, (0, 2, 1))
+    meta = jnp.concatenate(
+        [
+            jnp.concatenate([tgt_row, tgt_row], axis=2),
+            jnp.concatenate([src_row, src_row], axis=2),
+            jnp.pad(tgt_lengths, ((0, 0), (0, 0), (0, 96))),
+            jnp.pad(src_lengths, ((0, 0), (0, 0), (0, 96))),
+            jnp.zeros((2, 4, 128), jnp.int32),
+        ],
+        axis=1,
+    )
+    any_space = pl.BlockSpec(memory_space=pl.ANY)
+    vmem = pl.BlockSpec(memory_space=pltpu.VMEM)
+    lines = (CORES, PLANES, YS, XS)
+    leads = {"in": (2, 3), "out": (2,), "up": (1,), "dn": (1,)}
+    shards = {"in": (16, 512), "out": (16, 512), "up": (16, 2048), "dn": (64, 512)}
+    kinds = tuple(leads)
+
+    def half(shape):
+        return shape[:-1] + (shape[-1] // 2,)
+
+    def split_lead(lead, extra):
+        return lead[:-1] + extra + lead[-1:]
+
+    def low(shape):
+        return pltpu.VMEM(shape, BF16)
+
+    full = [low(leads[k] + lines + shards[k]) for k in kinds]
+    across = [low(leads[k] + lines[1:] + shards[k]) for k in kinds]
+    part = [low(split_lead(leads[k], (2,)) + (PLANES, 2) + half(shards[k])) for k in kinds]
+    piece = [low(split_lead(leads[k], (2,)) + (PLANES,) + half(shards[k])) for k in kinds]
+    line = [low(split_lead(leads[k], (3,)) + shards[k]) for k in kinds]
+    local_rows = low((2, 64, 512))
+    one = low((GROUP, 64, 128))
+    many = lambda n: low((GROUP, n, 64, 128))
+    small = pltpu.VMEM((24, 512), F32)
+    attn = [low((64, 1024))] * 3 + [low((1024, 64))] * 2 + [low((1024, 1024))]
+    attn += [pltpu.VMEM((1, 1024), F32), pltpu.VMEM((64, 1024), F32)]
+    wide = pltpu.VMEM((128, 512), F32)
+    scratch = full + full + across + part + piece + line
+    scratch += [local_rows] * 3 + [pltpu.VMEM((2, 8, 128), jnp.int32), pltpu.VMEM((GROUP, 8, 128), jnp.int32)]
+    for n in (3, 2, 1, 1, 1, 1, 3, 1, 3):
+        scratch += [one if n == 1 else many(n)] * 2
+    scratch += [local_rows] * 3
+    scratch += [small] * 8 + [pltpu.VMEM((3, 24, 512), F32)]
+    scratch += [pltpu.VMEM((1024, 128), F32)] * 3 + [pltpu.VMEM((8, 1024), F32)]
+    scratch += attn + attn
+    scratch += [low((64, 1024))] + [pltpu.VMEM((64, 1024), F32)] * 3
+    scratch += [low((128, 2048)), pltpu.VMEM((128, 2048), F32)] + [wide] * 5
+    scratch += [pltpu.SemaphoreType.DMA((96,)), pltpu.SemaphoreType.DMA((96,))]
+    rows = jax.ShapeDtypeStruct((2, 64, 512), BF16)
+
+    def wide_out(*shape):
+        return jax.ShapeDtypeStruct(shape, F32)
+
+    outs = pl.pallas_call(
+        fused_kernel,
+        name="layer",
+        out_shape=(
+            rows, rows, rows, wide_out(2, 3, 16, 512), wide_out(2, 16, 512), wide_out(1, 16, 2048),
+            wide_out(1, 64, 512), wide_out(7, 16), wide_out(1, 64), wide_out(3, 16), wide_out(3, 16), wide_out(3, 16),
+        ),
+        in_specs=[any_space] * 3 + [any_space] + [any_space] * 4 + [vmem] * 5,
+        out_specs=(any_space,) * 3 + (vmem,) * 9,
+        scratch_shapes=scratch,
+        compiler_params=pltpu.CompilerParams(collective_id=0, has_side_effects=True, vmem_limit_bytes=60 * 1024 * 1024),
+    )(
+        tokens.reshape(2, 64, 512), memory.reshape(2, 64, 512), cotangent.reshape(2, 64, 512), meta,
+        attn_in, attn_out, w_up.reshape(1, 16, 2048), w_down.reshape(1, 64, 512),
+        biases, up_bias.reshape(1, 2048), norm_gain, norm_shift, omega,
+    )
+    shaped = [out.reshape(2, 64, 1, 512) for out in outs[:3]]
+    return (
+        *shaped, outs[3], outs[4], outs[5].reshape(16, 2048), outs[6].reshape(64, 512), outs[7], outs[8].reshape(64),
+        outs[9], outs[10], outs[11],
+    )
+
+
+def solution(mesh):
+    if mesh.shape["seq"] != PLANES * YS * XS or mesh.shape["rows"] != CORES:
+        return general(mesh)
+    return over(mesh, fused_local)

time: 2320 us -> 158 us (0.07)
  waiting for transfers between devices: 1570 us -> 0 us
  blocking collectives: 248 us -> 0 us
  Pallas kernels: 0 us -> 144 us
  local copies, waits for them, and re-layouts: 155 us -> 12.1 us
  matrix products: 119 us -> 0 us
  other arithmetic: 116 us -> 0.07 us
  loops' own time: 78.7 us -> 0 us
    unnamed x33 -> x0, waiting for transfers between devices: 576 us -> none
    all_gather x20 -> x0, waiting for transfers between devices: 560 us -> none  [the longest x4 191 us: attend(): lax.all_gather(values, 'seq', axis=0, tiled=True)]
    reduce_scatter x3 -> x0, waiting for transfers between devices: 435 us -> none  [the longest x1 147 us: local(): lax.psum_scatter(grads[3], ('rows', 'seq'), scatter_dimension=0, tiled=True)]
    all_gather x4 -> x0, blocking collectives: 162 us -> none  [attention_back(): all_lambdas = lax.all_gather(lambdas, 'seq', axis=0, tiled=True)]
    pallas_call x0 -> x1, Pallas kernels: none -> 144 us  [fused_local(): pl.pallas_call(fused_kernel, name='layer', out_shape=(rows, rows, rows, w...]
    dot_general x102 -> x0, matrix products: 119 us -> none  [the longest x20 28.8 us: project(): jnp.einsum('trd,de->tre', values, matrix, preferred_element_type=jnp.floa...]
    unnamed x2 -> x0, blocking collectives: 85.7 us -> none
    another operation x36 -> x0, loops' own time: 78.7 us -> none  [the longest x4 26.2 us: attend(): lax.scan(step, start_carry, jnp.arange(length // block, dtype=jnp.int32))]
  transfers between devices with their start and end apart: 28 -> 0, of which waited for: 20 -> 0; matrix products, arithmetic and copies ran while one was open for 17% -> 0% of each run, Pallas kernels for 0% -> 0%
where the time goes in v1:
time: 158 us; the launch traced here: 157 us
  Pallas kernels  144 us (91%)
  local copies, waits for them, and re-layouts  12.1 us (8%)
    pallas_call x1, Pallas kernels, fused_local(): pl.pallas_call(fused_kernel, name='layer', out_shape=(rows, rows, rows, w...  144 us
    unnamed x42, local copies, waits for them, and re-layouts  11.5 us

profile of v1, /device:TPU:0, one launch (start us, length us, event | category | flops | bytes accessed | tf_op | source)
XLA Modules:
  0.0 157.4 jit_solution(13327372447867797328)
XLA Ops:
  0.6 0.0 copy-start.10
  0.7 0.7 copy-done.10
  1.3 0.7 copy-done.11
  2.0 0.7 copy-done.12
  2.7 0.0 copy-done.13
  2.7 0.1 pad_add_fusion
  2.8 0.6 concatenate.11.meta
  3.4 144.5 %layer.1 = (bf16[2,64,512]{2,1,0:T(8,128)(2,1)}, bf16[2,64,512]{2,1,0:T(8,128)(2,1)}, bf16[2,64,512]{2,1,0:T(8,128)(2,1)}, f32[2,3,16,512]{3,2,1,0:T(8,128)}, f3...) custom-call(bf16[2,64,512]{2,1,0:T(8,128)(2,1)} %bitcast.29, ...), custom_call_target="tpu_custom_call" | custom-call | tf_op jit(solution)/shard_map/layer/pallas_call | solution.py:1228
  147.9 0.0 copy-start.4
  147.9 0.0 copy-start.3
  147.9 1.6 %copy.47 = bf16[2,64,1,512]{3,1,2,0:T(8,128)(2,1)} copy(bf16[2,64,1,512]{3,1,2,0:T(8,128)(2,1)} %bitcast.28) | data formatting | bytes 262144
  149.5 0.0 copy-done.4
  149.5 0.7 copy.48
  150.2 0.0 copy-done.3
  150.2 0.7 copy.49
  150.8 0.0 copy-done
  150.8 0.7 copy.50
  151.5 0.2 copy-done.5
  151.7 0.6 copy.51
  152.3 0.3 copy-done.2
  152.6 0.7 copy.52
  153.3 0.3 copy-done.1
  153.6 0.7 copy.53
  154.2 0.0 copy-done.6
  154.3 0.6 copy.54
  154.9 0.1 copy-done.14
  154.9 0.5 copy.55
  155.4 0.6 copy.56
  156.0 0.1 copy-done.8
  156.1 0.6 copy.57
  156.7 0.1 copy-done.7
  156.8 0.6 copy.58
  (16 shorter events, 0.0 us)
Async XLA Ops:
  0.6 0.7 copy-start.10
  1.3 0.7 copy-start.11
  2.0 0.7 copy-start.12
  2.0 0.7 copy-start.13
  147.9 1.6 %copy-start.4 = (bf16[2,64,512]{2,1,0:T(8,128)(2,1)S(1)}, bf16[2,64,512]{2,1,0:T(8,128)(2,1)}, u32[]{:S(2)}) copy-start(bf16[2,64,512]{2,1,0:T(8,128)(2,1)} %get-tuple-element.25) | copy-start | bytes 393220
  147.9 2.3 %copy-start.3 = (bf16[2,64,512]{2,1,0:T(8,128)(2,1)S(1)}, bf16[2,64,512]{2,1,0:T(8,128)(2,1)}, u32[]{:S(2)}) copy-start(bf16[2,64,512]{2,1,0:T(8,128)(2,1)} %get-tuple-element.26) | copy-start | bytes 393220
  149.5 1.3 copy-start
  150.8 0.9 copy-start.5
  151.7 0.9 copy-start.2
  152.6 1.0 copy-start.1
  153.6 0.7 copy-start.6
  153.6 1.9 %copy-start.9 = (f32[3,16]{1,0:T(4,128)S(1)}, f32[3,16]{1,0:T(4,128)}, u32[]{:S(2)}) copy-start(f32[3,16]{1,0:T(4,128)} %get-tuple-element.71) | copy-start | bytes 580
  154.3 0.7 copy-start.14
  155.4 0.7 copy-start.8
  156.1 0.7 copy-start.7

commit v2 on v1

--- a/solution.py
+++ b/solution.py
@@ -536,22 +536,25 @@
 
 
 def fused_kernel(
-    tok, mem, cot, meta, s_in, s_out, s_up, s_dn, biases, up_bias, gain, shift, omega,
+    tok, mem, cot, tgt_len, src_len, tgt_msk, src_msk, s_in, s_out, s_up, s_dn, biases, up_bias, gain, shift, omega,
     o_res, o_tok, o_mem, o_in, o_out, o_up, o_dn, o_bias, o_upb, o_gain, o_shift, o_omega,
-    w_in, w_out, w_up, w_dn, g_in, g_out, g_up, g_dn,
-    c_in, c_out, c_up, c_dn,
-    p_in, p_out, p_up, p_dn,
-    q_in, q_out, q_up, q_dn,
-    z_in, z_out, z_up, z_dn,
-    in_tok, in_mem, in_cot, in_meta, all_meta,
-    a1, b1, a2, b2, a3, b3, a4, b4, a5, b5, a6, b6, a7, b7, a8, b8, a9, b9,
+    w_q, w_out, w_up, w_dn, g_q, g_out, g_up, g_dn,
+    c_q, c_out, c_up, c_dn,
+    p_q, p_out, p_up, p_dn,
+    q_q, q_out, q_up, q_dn,
+    z_q, z_out, z_up, z_dn,
+    ws0, ws1, gs0, gs1, cs0, cs1, zs0, zs1, fs0, fs1,
+    all_tok, all_mem, in_cot, raw_tl, raw_sl, raw_tm, raw_sm, meta, in_meta, all_meta,
+    dx0, dx1, dc0, dc1, dp0, dp1,
+    a3, b3, a4, b4, a5, b5, a6, b6, a7, b7, a8, b8,
     out_res, out_tok, out_mem,
     sg0, sg1, sg2, sg3, sg4, sr0, sr1, sr2, sr3,
     code_self, code_cross, key_pos, rows_f,
     qt0, kt0, vt0, k0, v0, pt0, l0, ot0,
     qt1, kt1, vt1, k1, v1, pt1, l1, ot1,
     dnt, acc_k, acc_v, acc_q,
-    act, slope, xh0, xh1, xh2, h1_f, h2_f,
+    act, slope, gul, xh0, xh1, xh2, h1_f, h2_f,
+    wt, bias_cols, wz, dt0, dt1, col_sums,
     ss, rs,
 ):
     c = lax.axis_index("rows")
@@ -579,14 +582,8 @@
         yy = 1 - y if k & 2 else y
         xx = 1 - x if k & 1 else x
         plane_peers.append((cc, yy, xx))
+    trio = [(1 - y, x), (y, 1 - x), (1 - y, 1 - x)]
     z_peers = [lax.rem(z + k, PLANES) for k in (1, 2, 3)]
-
-    barrier = pltpu.get_barrier_semaphore()
-    greet = [(cc, at(z, yy, xx)) for cc, yy, xx in plane_peers]
-    greet += [(cc, at(zz, y, x)) for zz in z_peers for cc in (c, 1 - c)]
-    for device in greet:
-        pl.semaphore_signal(barrier, inc=1, device_id=device, device_id_type=MESH)
-    pl.semaphore_wait(barrier, len(greet))
 
     names = {}
     pending = []
@@ -612,13 +609,13 @@
     def sent_later(name, ref):
         pending.append((name, ref))
 
-    def to_plane(name, src, dst):
+    def to_plane(name, src, dst, slotted=False):
         for m in range(2):
             plane = 2 * m + c
             core = z // 2
             half = lax.rem(z, 2)
             own = (plane == z) & (core == c)
-            part = dst.at[half]
+            part = dst.at[slot(core, y, x), half] if slotted else dst.at[half]
 
             @pl.when(own)
             def _():
@@ -670,8 +667,7 @@
         sent_later(name, src.at[pl.ds(0, GROUP - 1)])
 
     weights = {
-        "in0": (w_in.at[0], s_in.at[0], g_in.at[0], c_in.at[0], p_in.at[0], q_in.at[0], z_in.at[0], o_in.at[0]),
-        "in1": (w_in.at[1], s_in.at[1], g_in.at[1], c_in.at[1], p_in.at[1], q_in.at[1], z_in.at[1], o_in.at[1]),
+        "q": (w_q, s_in.at[1, pl.ds(0, 1)], g_q, c_q, p_q, q_q, z_q, o_in.at[1, pl.ds(0, 1)]),
         "out": (w_out, s_out, g_out, c_out, p_out, q_out, z_out, o_out),
         "up": (w_up, s_up, g_up, c_up, p_up, q_up, z_up, o_up),
         "dn": (w_dn, s_dn, g_dn, c_dn, p_dn, q_dn, z_dn, o_dn),
@@ -788,6 +784,96 @@
             total = total + line[k].astype(F32)
         result[...] = total
 
+    def spread_1(name, full):
+        own = full.at[me_slot]
+        for yy, xx in trio:
+            send(name + "p", own, own, (c, at(z, yy, xx)))
+        sent_later(name + "p", full.at[pl.ds(0, 3)])
+        send(name + "c", own, own, core_next)
+        sent_later(name + "c", own)
+
+    def spread_2(name, full):
+        landed(name + "p", full.at[pl.ds(0, 3)])
+        for yy, xx in trio:
+            part = full.at[slot(c, yy, xx)]
+            send(name + "d", part, part, core_next)
+        sent_later(name + "d", full.at[pl.ds(0, 3)])
+
+    def spread_3(name, full):
+        landed(name + "c", full.at[0])
+        landed(name + "d", full.at[pl.ds(0, 3)])
+
+    def merge_0(name, full, across):
+        send(name + "c", full.at[pl.ds((1 - c) * 4, 4)], across, core_next)
+        sent_later(name + "c", across)
+
+    def merge_1(name, full, across, parts):
+        landed(name + "c", across)
+
+        @pl.loop(0, 4)
+        def _(i):
+            add(full.at[c * 4 + i], across.at[i])
+
+        for k, (yy, xx) in enumerate(trio):
+            send(name + "p", full.at[slot(c, yy, xx)], parts.at[k], (c, at(z, yy, xx)))
+        sent_later(name + "p", parts)
+
+    def merge_2(name, full, parts):
+        landed(name + "p", parts)
+        total = full[me_slot].astype(F32)
+        for k in range(3):
+            total = total + parts[k].astype(F32)
+        return total.reshape(here, width)
+
+    def tile(index):
+        return pl.ds(pl.multiple_of(index * 128, 128), 128)
+
+    def slice_1(name, shard, full):
+        keep(name + "p", shard.at[:, :, tile(yx)], full.at[:, c, z, yx])
+        for yy, xx in trio:
+            send(name + "p", shard.at[:, :, tile(yy * 2 + xx)], full.at[:, c, z, yx], (c, at(z, yy, xx)))
+        sent_later(name + "p", full.at[:, c, z, pl.ds(0, 3)])
+
+    def slice_2(name, full):
+        landed(name + "p", full.at[:, c, z])
+        for zz in z_peers:
+            send(name + "z", full.at[:, c, z], full.at[:, c, z], (c, at(zz, y, x)))
+        sent_later(name + "z", full.at[:, c, pl.ds(0, 3)])
+
+    def slice_3(name, full):
+        landed(name + "z", full.at[:, c, pl.ds(0, 3)])
+        send(name + "c", full.at[:, c], full.at[:, c], core_next)
+        sent_later(name + "c", full.at[:, c])
+
+    def slice_4(name, full):
+        landed(name + "c", full.at[:, 1 - c])
+
+    def unslice_0(name, grad, across):
+        send(name + "c", grad.at[:, 1 - c], across, core_next)
+        sent_later(name + "c", across)
+
+    def unslice_1(name, grad, across, line):
+        landed(name + "c", across)
+        for lead in range(grad.shape[0]):
+            add(grad.at[lead, c], across.at[lead])
+        for k in range(3):
+            send(name + "z", grad.at[:, c, z_peers[k]], line.at[2 - k], (c, at(z_peers[k], y, x)))
+        sent_later(name + "z", line)
+
+    def unslice_2(name, grad, line, total, result):
+        landed(name + "z", line)
+        value = grad[:, c, z].astype(F32)
+        for k in range(3):
+            value = value + line[k].astype(F32)
+        total[...] = value
+        for yy, xx in trio:
+            send(name + "p", total.at[:, yy * 2 + xx], result.at[:, :, tile(yx)], (c, at(z, yy, xx)))
+        sent_later(name + "p", total.at[:, pl.ds(0, 3)])
+        result[:, :, tile(yx)] = total[:, yx]
+
+    def unslice_3(name, result):
+        landed(name + "p", result.at[:, :, pl.ds(0, 384)])
+
     def matrix(ref):
         return ref[...].reshape(-1, ref.shape[-1])
 
@@ -813,19 +899,6 @@
         dr = (dr - xhat * jnp.mean(dxhat * xhat, axis=1, keepdims=True)) * scale
         column(17 + i, dr * skip)
         return dr, dr * omega[i : i + 1, :]
-
-    def take(index, buffer, queries, keys, keys_t, values, values_t, which):
-        for s in range(GROUP):
-            cols = slice(s * here, (s + 1) * here)
-            if "q" in which:
-                queries[:, cols] = (buffer[(s,) + index["q"]].astype(F32) * 0.125).astype(BF16)
-            if "k" in which:
-                block = buffer[(s,) + index["k"]]
-                keys_t[:, cols] = block
-                keys[cols, :] = flip(block).astype(BF16)
-                block = buffer[(s,) + index["v"]]
-                values_t[:, cols] = block
-                values[cols, :] = flip(block).astype(BF16)
 
     BLOCK = 256
 
@@ -860,7 +933,7 @@
         for s in range(GROUP):
             target[s] = outputs[:, s * here : (s + 1) * here].astype(BF16)
 
-    def attend_back(buffer, queries, keys_t, values, weights_t, sums, outputs, causal, target):
+    def attend_back(buffer, queries, keys_t, values, weights_t, sums, outputs, causal):
         acc_k[...] = jnp.zeros_like(acc_k)
         acc_v[...] = jnp.zeros_like(acc_v)
         for s in range(GROUP):
@@ -888,60 +961,96 @@
             pl.loop(2, 4)(make(1024))
         else:
             pl.loop(0, 4)(make(1024))
-        for s in range(GROUP):
-            cols = slice(s * here, (s + 1) * here)
-            target[s, 0] = acc_q[:, cols].astype(BF16)
-            target[s, 1] = acc_k[:, cols].astype(BF16)
-            target[s, 2] = acc_v[:, cols].astype(BF16)
-
-    def by_head(target, index, value):
-        low = flip(value).astype(BF16).reshape(GROUP, 64, here)
-        target[(slice(None),) + index] = low
+    def by_head(target, value):
+        target[...] = flip(value).astype(BF16).reshape(GROUP, 64, here)
+
+    def heads_weights(first, full):
+        for j in range(full.shape[0]):
+            wt[first + j] = flip(matrix(full.at[j])).astype(BF16)
+
+    own_rows = pl.ds(pl.multiple_of(c * 64, 64), 64)
+    own_head = pl.ds(pl.multiple_of(me_head * 64, 64), 64)
+
+    def own_weights(first, count):
+        return jnp.concatenate([wt[first + j, own_rows, :] for j in range(count)], axis=0)
+
+    def wide_bias(i):
+        col = bias_cols[i, own_head, :]
+        return jnp.concatenate([col, col], axis=1)
+
+    def project_heads(rows, first, queries, keys, keys_t, values, values_t):
+        count = 2 if queries is None else 3
+        own = own_weights(first, count)
+        for b in range(4):
+            cols = slice(b * 256, (b + 1) * 256)
+            out = nt(own, rows[2 * b : 2 * b + 2].reshape(256, width))
+            if queries is not None:
+                queries[:, cols] = ((out[0:64] + wide_bias(0)).astype(BF16).astype(F32) * 0.125).astype(BF16)
+            at_k = 64 * (count - 2)
+            block = out[at_k : at_k + 64].astype(BF16)
+            keys_t[:, cols] = block
+            keys[cols, :] = flip(block).astype(BF16)
+            block = (out[at_k + 64 : at_k + 128] + wide_bias(1 if count == 3 else 2)).astype(BF16)
+            values_t[:, cols] = block
+            values[cols, :] = flip(block).astype(BF16)
+
+    def rows_back(grads_t, first, target, core):
+        count = grads_t.shape[0] // 64
+        own = own_weights(first, count)
+        for b in range(2):
+            cols = pl.ds(pl.multiple_of(core * 512 + b * 256, 256), 256)
+            out = tn(grads_t[:, cols], own)
+            target[pl.ds(core * 4 + b * 2, 2)] = out.astype(BF16).reshape(2, 2, 64, width)
+
+    def slices_back(grads_t, rows, grad):
+        count = grads_t.shape[0] // 64
+        out = nn(grads_t[...], rows[...].reshape(1024, width))
+        wz[...] = jnp.zeros_like(wz)
+        for j in range(count):
+            wz[j, own_rows, :] = out[j * 64 : (j + 1) * 64]
+            put(grad.at[j], jnp.transpose(wz[j]))
 
     def bias(i):
         return biases[i : i + 1, :]
 
+    raw = ((raw_tm, tgt_msk), (raw_sm, src_msk), (raw_tl, tgt_len), (raw_sl, src_len))
+    for i, (ref, given) in enumerate(raw):
+        keep("raw" + str(i), given, ref)
+    barrier = pltpu.get_barrier_semaphore()
+    greet = [(cc, at(z, yy, xx)) for cc, yy, xx in plane_peers]
+    greet += [(cc, at(zz, y, x)) for zz in z_peers for cc in (c, 1 - c)]
+    for device in greet:
+        pl.semaphore_signal(barrier, inc=1, device_id=device, device_id_type=MESH)
+    pl.semaphore_wait(barrier, len(greet))
+
+    to_plane("tok", tok, all_tok, True)
+    slice_1("w0", s_in.at[0], ws0)
+    slice_1("w1", s_in.at[1, pl.ds(1, 2)], ws1)
+    for i, (ref, _) in enumerate(raw):
+        landed("raw" + str(i), ref)
+        span = ref.shape[2]
+        for m in range(2):
+            for start in (0, 64):
+                meta[m, i : i + 1, start : start + span] = ref[m]
     to_plane("meta", meta, in_meta)
-    to_plane("tok", tok, in_tok)
-    gather_z("in0")
-    to_plane("mem", mem, in_mem)
-    gather_z("in1")
+    slice_2("w0", ws0)
     gather_z("out")
-    to_plane("cot", cot, in_cot)
+    to_plane("mem", mem, all_mem, True)
+    landed("tok", all_tok.at[me_slot])
+    spread_1("x", all_tok)
+    slice_2("w1", ws1)
+    gather_z("q")
     gather_z("up")
     gather_z("dn")
-
+    to_plane("cot", cot, in_cot)
     landed("meta", in_meta)
     lane = lax.broadcasted_iota(jnp.int32, (8, 128), 1)
     all_meta[me_slot] = jnp.where(lane < 64, in_meta[0], in_meta[1])
     for cc, yy, xx in plane_peers:
         send("marks", all_meta.at[me_slot], all_meta.at[me_slot], (cc, at(z, yy, xx)))
     sent_later("marks", all_meta.at[pl.ds(0, 7)])
-    gather_1("in0")
-    gather_1("in1")
-    gather_2("in0")
-    gather_1("out")
-    gather_2("in1")
-    gather_3("in0")
-    gather_1("up")
-    gathered("in0")
-    landed("tok", in_tok)
-
-    words = in_tok[...].reshape(here, width)
-    for j, extra in ((0, 0), (1, None), (2, 1)):
-        value = nn(words, matrix(w_in.at[0, j]))
-        by_head(a1, (j,), value if extra is None else value + bias(extra))
-    to_heads("x1", a1, b1)
-    gather_3("in1")
-    gather_2("out")
-    gather_1("dn")
-    gathered("in1")
-    landed("mem", in_mem)
-    sources = in_mem[...].reshape(here, width)
-    by_head(a2, (0,), nn(sources, matrix(w_in.at[1, 1])))
-    by_head(a2, (1,), nn(sources, matrix(w_in.at[1, 2])) + bias(4))
-    to_heads("x2", a2, b2)
-    gather_3("out")
+    for i, row in enumerate((0, 1, 4)):
+        bias_cols[i] = jnp.transpose(jnp.broadcast_to(bias(row), (128, width)))
 
     landed("marks", all_meta.at[pl.ds(0, 7)])
     order = lax.broadcasted_iota(jnp.int32, (1, 1024), 1)
@@ -975,37 +1084,58 @@
     code_cross[...] = jnp.transpose(jnp.broadcast_to(cross_row, (128, 1024)))
     key_pos[...] = jnp.transpose(jnp.broadcast_to(place, (128, 1024)))
 
-    landed("x1", b1)
-    take({"q": (0,), "k": (1,), "v": (2,)}, b1, qt0, k0, kt0, v0, vt0, "qk")
+    slice_3("w0", ws0)
+    gather_1("out")
+    spread_2("x", all_tok)
+    slice_4("w0", ws0)
+    heads_weights(0, ws0)
+    landed("mem", all_mem.at[me_slot])
+    spread_1("m", all_mem)
+    gather_2("out")
+    spread_3("x", all_tok)
+
+    project_heads(all_tok, 0, qt0, k0, kt0, v0, vt0)
     attend(qt0, k0, vt0, pt0, l0, ot0, True, a3)
     to_slots("x3", a3, b3)
-    gather_2("up")
-    gather_2("dn")
+    gather_3("out")
+    slice_3("w1", ws1)
+    gather_1("q")
+    spread_2("m", all_mem)
+    gather_2("q")
+    gather_1("up")
+    slice_4("w1", ws1)
+    heads_weights(3, ws1)
+    spread_3("m", all_mem)
+    project_heads(all_mem, 3, None, k1, kt1, v1, vt1)
+    gather_3("q")
     gathered("out")
-    landed("x2", b2)
-    take({"k": (0,), "v": (1,)}, b2, qt1, k1, kt1, v1, vt1, "k")
 
     landed("x3", b3)
-    words_f = words.astype(F32)
+    words_f = all_tok[me_slot].reshape(here, width).astype(F32)
     branch = tn(b3[...].reshape(width, here), matrix(w_out.at[0])) + bias(2)
     h1, scale0 = norm(words_f * omega[0:1, :] + branch, 0, xh0)
     h1_f[...] = h1
     h1_low = h1.astype(BF16)
-    by_head(a4, (), nn(h1_low, matrix(w_in.at[1, 0])) + bias(3))
+    gathered("q")
+    by_head(a4, nn(h1_low, matrix(w_q.at[0])) + bias(3))
     to_heads("x4", a4, b4)
+    gather_1("dn")
+    gather_2("up")
 
     landed("x4", b4)
-    take({"q": ()}, b4, qt1, k1, kt1, v1, vt1, "q")
+    for s in range(GROUP):
+        qt1[:, s * here : (s + 1) * here] = (b4[s].astype(F32) * 0.125).astype(BF16)
     attend(qt1, k1, vt1, pt1, l1, ot1, False, a5)
     to_slots("x5", a5, b5)
+    gather_2("dn")
     gather_3("up")
-    gather_3("dn")
 
     landed("x5", b5)
     branch = tn(b5[...].reshape(width, here), matrix(w_out.at[1])) + bias(5)
     h2, scale1 = norm(h1_f[...] * omega[1:2, :] + branch, 1, xh1)
     h2_f[...] = h2
     h2_low = h2.astype(BF16)
+    gather_3("dn")
 
     gathered("up")
     for k in range(4):
@@ -1033,104 +1163,119 @@
     back = skip
     for k in range(4):
         cols = slice(k * width, (k + 1) * width)
-        part = act[:, cols]
-        put(g_dn.at[0, k // 2, pl.ds(2 * (k % 2), 2)], tn(part, gf))
         gu = nt(gf, matrix(w_dn.at[0, k // 2, pl.ds(2 * (k % 2), 2)])) * slope[:, cols]
         gu = gu.astype(BF16)
+        gul[:, cols] = gu
         column(7 + k, gu.astype(F32))
-        put(g_up.at[0, :, :, :, :, :, cols], tn(h2_low, gu))
         back = back + nt(gu, matrix(w_up.at[0, :, :, :, :, :, cols]))
-    scatter_0("dn")
-    scatter_0("up")
 
     dr, skip = norm_back(back, 1, xh1, scale1, h1_f[...])
     gc = dr.astype(BF16)
     column(5, gc.astype(F32))
-    by_head(a6, (), nt(gc, matrix(w_out.at[1])))
+    by_head(a6, nt(gc, matrix(w_out.at[1])))
     to_heads("x6", a6, b6)
     back = skip
+    for k in range(4):
+        put(g_dn.at[0, k // 2, pl.ds(2 * (k % 2), 2)], tn(act[:, k * width : (k + 1) * width], gf))
+    scatter_0("dn")
+    for k in range(4):
+        cols = slice(k * width, (k + 1) * width)
+        put(g_up.at[0, :, :, :, :, :, cols], tn(h2_low, gul[:, cols]))
+    scatter_0("up")
+    scatter_1("dn")
+
+    landed("x6", b6)
+    attend_back(b6, qt1, kt1, v1, pt1, l1, ot1, False)
+    for s in range(GROUP):
+        a7[s] = acc_q[:, s * here : (s + 1) * here].astype(BF16)
+    to_slots("x7", a7, b7)
+    scatter_1("up")
+    dt1[0:64, :] = acc_k[...].astype(BF16)
+    dt1[64:128, :] = acc_v[...].astype(BF16)
+    rows_back(dt1, 3, dx1, 1 - c)
+    merge_0("dm", dx1, dc1)
+    rows_back(dt1, 3, dx1, c)
+    slices_back(dt1, all_mem, gs1)
+    unslice_0("u1", gs1, cs1)
+    col_sums[0] = jnp.broadcast_to(jnp.sum(dt1[64:128, :].astype(F32), axis=1, keepdims=True), (64, 128))
     put(g_out.at[1], nn(b5[...].reshape(width, here), gc))
-    scatter_1("dn")
-    scatter_1("up")
-
-    landed("x6", b6)
-    attend_back(b6, qt1, kt1, v1, pt1, l1, ot1, False, a7)
-    to_slots("x7", a7, b7)
-    scatter_2("dn")
-    scatter_2("up")
 
     landed("x7", b7)
-    dq, dk, dv = (b7[:, j].reshape(width, here) for j in range(3))
-    dq_row, dv_row = flip(dq), flip(dv)
+    dq = b7[...].reshape(width, here)
+    dq_row = flip(dq)
     column(3, dq_row)
-    column(4, dv_row)
-    back = back + nt(dq_row.astype(BF16), matrix(w_in.at[1, 0]))
+    back = back + nt(dq_row.astype(BF16), matrix(w_q.at[0]))
     dr, skip = norm_back(back, 0, xh0, scale0, words_f)
     ga = dr.astype(BF16)
     column(2, ga.astype(F32))
-    by_head(a8, (), nt(ga, matrix(w_out.at[0])))
+    by_head(a8, nt(ga, matrix(w_out.at[0])))
     to_heads("x8", a8, b8)
     back = skip
+    scatter_2("dn")
+    merge_1("dm", dx1, dc1, dp1)
     put(g_out.at[0], nn(b3[...].reshape(width, here), ga))
     scatter_0("out")
-    h1_t = flip(h1_low).astype(BF16)
-    put(g_in.at[1, 0], nt(h1_t, dq))
-    sources_t = flip(sources).astype(BF16)
-    put(g_in.at[1, 1], nt(sources_t, dk))
-    put(g_in.at[1, 2], nt(sources_t, dv))
-    scatter_0("in1")
-    grad_mem = nt(flip(dk).astype(BF16), matrix(w_in.at[1, 1])) + nt(dv_row.astype(BF16), matrix(w_in.at[1, 2]))
-    out_mem[...] = grad_mem.astype(BF16).reshape(2, 64, width)
-    from_plane("gmem", out_mem, o_mem)
+    put(g_q.at[0], nt(flip(h1_low).astype(BF16), dq))
+    scatter_0("q")
+    unslice_1("u1", gs1, cs1, zs1)
+    scatter_2("up")
     scatter_3("dn")
-    scatter_3("up")
-    scatter_1("out")
-    scatter_1("in1")
 
     landed("x8", b8)
-    attend_back(b8, qt0, kt0, v0, pt0, l0, ot0, True, a9)
-    to_slots("x9", a9, b9)
-    scatter_2("out")
-    scatter_2("in1")
-    scattered("dn")
-    scattered("up")
-
-    landed("x9", b9)
-    dq, dk, dv = (b9[:, j].reshape(width, here) for j in range(3))
-    words_t = flip(words).astype(BF16)
-    for j, value in enumerate((dq, dk, dv)):
-        put(g_in.at[0, j], nt(words_t, value))
-    scatter_0("in0")
-    for j, value in enumerate((dq, dk, dv)):
-        value = flip(value)
-        if j != 1:
-            column(j // 2, value)
-        back = back + nt(value.astype(BF16), matrix(w_in.at[0, j]))
-    out_tok[...] = back.astype(BF16).reshape(2, 64, width)
-    from_plane("gtok", out_tok, o_tok)
+    attend_back(b8, qt0, kt0, v0, pt0, l0, ot0, True)
+    dt0[0:64, :] = acc_q[...].astype(BF16)
+    dt0[64:128, :] = acc_k[...].astype(BF16)
+    dt0[128:192, :] = acc_v[...].astype(BF16)
+    rows_back(dt0, 0, dx0, 1 - c)
+    merge_0("dx", dx0, dc0)
+    rows_back(dt0, 0, dx0, c)
+    merge_1("dx", dx0, dc0, dp0)
+    slices_back(dt0, all_tok, gs0)
+    unslice_0("u0", gs0, cs0)
+    lanes = lax.broadcasted_iota(jnp.int32, (64, 128), 1)
+    dq_sum = jnp.sum(dt0[0:64, :].astype(F32), axis=1, keepdims=True)
+    dv_sum = jnp.sum(dt0[128:192, :].astype(F32), axis=1, keepdims=True)
+    bias_cols[0] = jnp.zeros((width, 128), F32)
+    bias_cols[0, own_head, :] = jnp.where(lanes == 0, dq_sum, jnp.where(lanes == 1, dv_sum, col_sums[0]))
+    turned = jnp.transpose(bias_cols[0])
+    sg0[0:2, :] = turned[0:2, :]
+    sg0[4:5, :] = turned[2:3, :]
 
     send("s0", sg0, sr0, core_next)
     sent_later("s0", sr0)
-    scatter_1("in0")
-    scatter_3("out")
+    scatter_1("out")
+    scatter_1("q")
+    out_mem[...] = merge_2("dm", dx1, dp1).astype(BF16).reshape(2, 64, width)
+    from_plane("gmem", out_mem, o_mem)
+    unslice_2("u1", gs1, zs1, fs1, o_in.at[1, pl.ds(1, 2)])
+    scatter_3("up")
+    unslice_1("u0", gs0, cs0, zs0)
     landed("s0", sr0)
     sg1[...] = sg0[...] + sr0[...]
     send("s1", sg1, sr1, y_next)
     sent_later("s1", sr1)
-    scatter_3("in1")
+    scatter_2("out")
+    scatter_2("q")
+    out_tok[...] = (merge_2("dx", dx0, dp0) + back).astype(BF16).reshape(2, 64, width)
+    from_plane("gtok", out_tok, o_tok)
     landed("s1", sr1)
     sg2[...] = sg1[...] + sr1[...]
     send("s2", sg2, sr2, x_next)
     sent_later("s2", sr2)
-    scatter_2("in0")
+    scatter_3("out")
+    scatter_3("q")
+    unslice_2("u0", gs0, zs0, fs0, o_in.at[0])
+    scattered("dn")
+    scattered("up")
     landed("s2", sr2)
     sg3[...] = sg2[...] + sr2[...]
     for k in range(3):
         send("s3", sg3, sr3.at[2 - k], (c, at(z_peers[k], y, x)))
     sent_later("s3", sr3)
-    scatter_3("in0")
     scattered("out")
-    scattered("in1")
+    scattered("q")
+    unslice_3("u1", o_in.at[1, pl.ds(1, 2)])
+    unslice_3("u0", o_in.at[0])
     landed("s3", sr3)
     sg0_total = sg3[...] + sr3[0] + sr3[1] + sr3[2]
     sg4[...] = sg0_total
@@ -1148,7 +1293,6 @@
     for k in range(4):
         row = row + turned[7 + k : 8 + k, 0:64] * (wanted == k).astype(F32)
     o_upb[...] = row
-    scattered("in0")
 
     landed("res", o_res)
     landed("gmem", o_mem)
@@ -1165,61 +1309,54 @@
     assert len(names) <= ss.shape[0], len(names)
 
 
+def copy_kernel(*refs):
+    count = len(refs) // 2
+    for i in range(count):
+        refs[count + i][...] = refs[i][...]
+
+
 def fused_local(
     tokens, memory, cotangent, tgt_lengths, src_lengths, tgt_mask, src_mask, attn_in, attn_out, w_up, w_down,
     biases, up_bias, norm_gain, norm_shift, omega,
 ):
-    tgt_row = jnp.transpose(tgt_mask, (0, 2, 1))
-    src_row = jnp.transpose(src_mask, (0, 2, 1))
-    meta = jnp.concatenate(
-        [
-            jnp.concatenate([tgt_row, tgt_row], axis=2),
-            jnp.concatenate([src_row, src_row], axis=2),
-            jnp.pad(tgt_lengths, ((0, 0), (0, 0), (0, 96))),
-            jnp.pad(src_lengths, ((0, 0), (0, 0), (0, 96))),
-            jnp.zeros((2, 4, 128), jnp.int32),
-        ],
-        axis=1,
-    )
     any_space = pl.BlockSpec(memory_space=pl.ANY)
     vmem = pl.BlockSpec(memory_space=pltpu.VMEM)
     lines = (CORES, PLANES, YS, XS)
-    leads = {"in": (2, 3), "out": (2,), "up": (1,), "dn": (1,)}
-    shards = {"in": (16, 512), "out": (16, 512), "up": (16, 2048), "dn": (64, 512)}
+    leads = {"q": 1, "out": 2, "up": 1, "dn": 1}
+    shards = {"q": (16, 512), "out": (16, 512), "up": (16, 2048), "dn": (64, 512)}
     kinds = tuple(leads)
 
-    def half(shape):
-        return shape[:-1] + (shape[-1] // 2,)
-
-    def split_lead(lead, extra):
-        return lead[:-1] + extra + lead[-1:]
-
-    def low(shape):
+    def low(*shape):
         return pltpu.VMEM(shape, BF16)
 
-    full = [low(leads[k] + lines + shards[k]) for k in kinds]
-    across = [low(leads[k] + lines[1:] + shards[k]) for k in kinds]
-    part = [low(split_lead(leads[k], (2,)) + (PLANES, 2) + half(shards[k])) for k in kinds]
-    piece = [low(split_lead(leads[k], (2,)) + (PLANES,) + half(shards[k])) for k in kinds]
-    line = [low(split_lead(leads[k], (3,)) + shards[k]) for k in kinds]
-    local_rows = low((2, 64, 512))
-    one = low((GROUP, 64, 128))
-    many = lambda n: low((GROUP, n, 64, 128))
-    small = pltpu.VMEM((24, 512), F32)
-    attn = [low((64, 1024))] * 3 + [low((1024, 64))] * 2 + [low((1024, 1024))]
-    attn += [pltpu.VMEM((1, 1024), F32), pltpu.VMEM((64, 1024), F32)]
-    wide = pltpu.VMEM((128, 512), F32)
-    scratch = full + full + across + part + piece + line
-    scratch += [local_rows] * 3 + [pltpu.VMEM((2, 8, 128), jnp.int32), pltpu.VMEM((GROUP, 8, 128), jnp.int32)]
-    for n in (3, 2, 1, 1, 1, 1, 3, 1, 3):
-        scratch += [one if n == 1 else many(n)] * 2
-    scratch += [local_rows] * 3
-    scratch += [small] * 8 + [pltpu.VMEM((3, 24, 512), F32)]
-    scratch += [pltpu.VMEM((1024, 128), F32)] * 3 + [pltpu.VMEM((8, 1024), F32)]
-    scratch += attn + attn
-    scratch += [low((64, 1024))] + [pltpu.VMEM((64, 1024), F32)] * 3
-    scratch += [low((128, 2048)), pltpu.VMEM((128, 2048), F32)] + [wide] * 5
-    scratch += [pltpu.SemaphoreType.DMA((96,)), pltpu.SemaphoreType.DMA((96,))]
+    def full(*shape):
+        return pltpu.VMEM(shape, F32)
+
+    def whole(k):
+        return low(leads[k], *lines, *shards[k])
+
+    def halved(k, *middle):
+        return low(2, leads[k], *middle, shards[k][0], shards[k][1] // 2)
+
+    scratch = [whole(k) for k in kinds] * 2
+    scratch += [low(leads[k], *lines[1:], *shards[k]) for k in kinds]
+    scratch += [halved(k, PLANES, 2) for k in kinds] + [halved(k, PLANES) for k in kinds]
+    scratch += [low(3, leads[k], *shards[k]) for k in kinds]
+    scratch += [low(n, CORES, PLANES, 4, 16, 128) for n in (3, 2)] * 2
+    scratch += [low(n, PLANES, 4, 16, 128) for n in (3, 2)] + [low(3, n, 4, 16, 128) for n in (3, 2)]
+    scratch += [full(n, 4, 16, 128) for n in (3, 2)]
+    local_rows = low(2, 64, 512)
+    marks = [pltpu.VMEM((2, 1, n), jnp.int32) for n in (32, 32, 64, 64)] + [pltpu.VMEM((2, 8, 128), jnp.int32)] * 2
+    scratch += [low(GROUP, 2, 64, 512)] * 2 + [local_rows] + marks + [pltpu.VMEM((GROUP, 8, 128), jnp.int32)]
+    scratch += [low(GROUP, 2, 64, 512)] * 2 + [low(4, 2, 64, 512)] * 2 + [low(3, 2, 64, 512)] * 2
+    scratch += [low(GROUP, 64, 128)] * 12 + [local_rows] * 3
+    scratch += [full(24, 512)] * 8 + [full(3, 24, 512)]
+    scratch += [full(1024, 128)] * 3 + [full(8, 1024)]
+    scratch += ([low(64, 1024)] * 3 + [low(1024, 64)] * 2 + [low(1024, 1024), full(1, 1024), full(64, 1024)]) * 2
+    scratch += [low(64, 1024)] + [full(64, 1024)] * 3
+    scratch += [low(128, 2048), full(128, 2048), low(128, 2048)] + [full(128, 512)] * 5
+    scratch += [low(5, 128, 512), full(3, 512, 128), full(3, 128, 512), low(192, 1024), low(128, 1024), full(1, 64, 128)]
+    scratch += [pltpu.SemaphoreType.DMA((128,)), pltpu.SemaphoreType.DMA((128,))]
     rows = jax.ShapeDtypeStruct((2, 64, 512), BF16)
 
     def wide_out(*shape):
@@ -1232,15 +1369,23 @@
             rows, rows, rows, wide_out(2, 3, 16, 512), wide_out(2, 16, 512), wide_out(1, 16, 2048),
             wide_out(1, 64, 512), wide_out(7, 16), wide_out(1, 64), wide_out(3, 16), wide_out(3, 16), wide_out(3, 16),
         ),
-        in_specs=[any_space] * 3 + [any_space] + [any_space] * 4 + [vmem] * 5,
+        in_specs=[any_space] * 11 + [vmem] * 5,
         out_specs=(any_space,) * 3 + (vmem,) * 9,
         scratch_shapes=scratch,
         compiler_params=pltpu.CompilerParams(collective_id=0, has_side_effects=True, vmem_limit_bytes=60 * 1024 * 1024),
     )(
-        tokens.reshape(2, 64, 512), memory.reshape(2, 64, 512), cotangent.reshape(2, 64, 512), meta,
+        tokens.reshape(2, 64, 512), memory.reshape(2, 64, 512), cotangent.reshape(2, 64, 512),
+        tgt_lengths, src_lengths, jnp.transpose(tgt_mask, (0, 2, 1)), jnp.transpose(src_mask, (0, 2, 1)),
         attn_in, attn_out, w_up.reshape(1, 16, 2048), w_down.reshape(1, 64, 512),
         biases, up_bias.reshape(1, 2048), norm_gain, norm_shift, omega,
     )
+    outs = pl.pallas_call(
+        copy_kernel,
+        name="hand_over",
+        out_shape=tuple(jax.ShapeDtypeStruct(out.shape, out.dtype) for out in outs),
+        in_specs=[vmem] * len(outs),
+        out_specs=(vmem,) * len(outs),
+    )(*outs)
     shaped = [out.reshape(2, 64, 1, 512) for out in outs[:3]]
     return (
         *shaped, outs[3], outs[4], outs[5].reshape(16, 2048), outs[6].reshape(64, 512), outs[7], outs[8].reshape(64),

time: 158 us -> 128 us (0.81)
  Pallas kernels: 144 us -> 127 us
  local copies, waits for them, and re-layouts: 12.1 us -> 0 us
    pallas_call x1, Pallas kernels: 144 us -> 124 us  [fused_local(): pl.pallas_call(fused_kernel, name='layer', out_shape=(rows, rows, rows, w...]
    unnamed x42 -> x0, local copies, waits for them, and re-layouts: 11.5 us -> none
    pallas_call x0 -> x1, Pallas kernels: none -> 2.23 us  [fused_local(): pl.pallas_call(copy_kernel, name='hand_over', out_shape=tuple((jax.ShapeD...]
where the time goes in v2:
time: 128 us; the launch traced here: 127 us
  Pallas kernels  127 us (99%)
    pallas_call x1, Pallas kernels, fused_local(): pl.pallas_call(fused_kernel, name='layer', out_shape=(rows, rows, rows, w...  124 us

profile of v2, /device:TPU:0, one launch (start us, length us, event | category | flops | bytes accessed | tf_op | source)
XLA Modules:
  0.0 127.3 jit_solution(3364377667525915157)
XLA Ops:
  0.7 124.4 %layer.1 = (bf16[2,64,512]{2,1,0:T(8,128)(2,1)}, bf16[2,64,512]{2,1,0:T(8,128)(2,1)}, bf16[2,64,512]{2,1,0:T(8,128)(2,1)}, f32[2,3,16,512]{3,2,1,0:T(8,128)}, f3...) custom-call(bf16[2,64,512]{2,1,0:T(8,128)(2,1)} %bitcast.24, ...), custom_call_target="tpu_custom_call" | custom-call | tf_op jit(solution)/shard_map/layer/pallas_call | solution.py:1365
  125.1 2.2 %hand_over.1 = (bf16[2,64,512]{2,1,0:T(8,128)(2,1)}, bf16[2,64,512]{2,1,0:T(8,128)(2,1)}, bf16[2,64,512]{2,1,0:T(8,128)(2,1)}, f32[2,3,16,512]{3,2,1,0:T(8,128)}...) custom-call(bf16[2,64,512]{2,1,0:T(8,128)(2,1)} %get-tuple-element.3, ...), custom_call_target="tpu_custom_call" | custom-call | tf_op jit(solution)/shard_map/hand_over/pallas_call | solution.py:1382

commit v3 on v2

--- a/solution.py
+++ b/solution.py
@@ -513,6 +513,10 @@
 
 
 MESH = pl.DeviceIdType.MESH
+UNIT = 16 * 1024
+BINS = 16
+NAMES = 168
+ODD = ("marks", "w0p", "w1p", "u0p")
 F32 = jnp.float32
 BF16 = jnp.bfloat16
 PLANES, YS, XS, CORES = 4, 2, 2, 2
@@ -536,8 +540,9 @@
 
 
 def fused_kernel(
-    tok, mem, cot, tgt_len, src_len, tgt_msk, src_msk, s_in, s_out, s_up, s_dn, biases, up_bias, gain, shift, omega,
-    o_res, o_tok, o_mem, o_in, o_out, o_up, o_dn, o_bias, o_upb, o_gain, o_shift, o_omega,
+    tok, mem, cot, tgt_len, src_len, tgt_msk, src_msk, s_in, s_out, s_up, s_dn, h_biases, h_up_bias, h_gain, h_shift, h_omega,
+    o_res, o_tok, o_mem, h_in, h_out, h_up, h_dn, h_bias, h_upb, h_gain_o, h_shift_o, h_omega_o,
+    biases, up_bias, gain, shift, omega, o_in, o_out, o_up, o_dn, o_bias, o_upb, o_gain, o_shift, o_omega,
     w_q, w_out, w_up, w_dn, g_q, g_out, g_up, g_dn,
     c_q, c_out, c_up, c_dn,
     p_q, p_out, p_up, p_dn,
@@ -549,12 +554,13 @@
     a3, b3, a4, b4, a5, b5, a6, b6, a7, b7, a8, b8,
     out_res, out_tok, out_mem,
     sg0, sg1, sg2, sg3, sg4, sr0, sr1, sr2, sr3,
+    tg0, tg1, tg2, tg3, tr0, tr1, tr2, tr3,
     code_self, code_cross, key_pos, rows_f,
     qt0, kt0, vt0, k0, v0, pt0, l0, ot0,
     qt1, kt1, vt1, k1, v1, pt1, l1, ot1,
-    dnt, acc_k, acc_v, acc_q,
+    dnt, acc_k, acc_v,
     act, slope, gul, xh0, xh1, xh2, h1_f, h2_f,
-    wt, bias_cols, wz, dt0, dt1, col_sums,
+    wt, bias_cols, wz, dt0, dt1, gauge,
     ss, rs,
 ):
     c = lax.axis_index("rows")
@@ -585,8 +591,9 @@
     trio = [(1 - y, x), (y, 1 - x), (1 - y, 1 - x)]
     z_peers = [lax.rem(z + k, PLANES) for k in (1, 2, 3)]
 
-    names = {}
+    names, expected_bytes = {}, {}
     pending = []
+    edge = (z == 0) | (z == PLANES - 1)
 
     def sem(name):
         return names.setdefault(name, len(names))
@@ -594,10 +601,19 @@
     def wait(semaphore, ref):
         pltpu.make_async_copy(ref, ref, semaphore).wait()
 
-    def send(name, src, dst, device):
-        i = sem(name)
+    def size(ref):
+        return math.prod(ref.shape) * jnp.dtype(ref.dtype).itemsize
+
+    bins = [0]
+    odd = {}
+
+    def out_sem(name):
+        return ss.at[odd.setdefault(name, BINS + 1 + len(odd))] if name in ODD else ss.at[len(bins) - 1]
+
+    def send(name, src, dst, device, recv=None):
         pltpu.make_async_remote_copy(
-            src_ref=src, dst_ref=dst, send_sem=ss.at[i], recv_sem=rs.at[i], device_id=device, device_id_type=MESH
+            src_ref=src, dst_ref=dst, send_sem=out_sem(name), recv_sem=rs.at[sem(name)] if recv is None else recv,
+            device_id=device, device_id_type=MESH,
         ).start()
 
     def keep(name, src, dst):
@@ -607,52 +623,100 @@
         wait(rs.at[sem(name)], ref)
 
     def sent_later(name, ref):
-        pending.append((name, ref))
+        if name in ODD:
+            pending.append((ss.at[odd[name]], ref, None))
+            return
+        bins[-1] += size(ref)
+        assert size(ref) % UNIT == 0, (name, size(ref))
+        if bins[-1] > 1024 * UNIT // 16:
+            bins.append(0)
+
+    line_bytes = [0]
+
+    def along_z(name, src, block):
+        i, j = sem(name + "z"), sem(name + "f")
+        for step in (1, -1, 2, -2):
+            to = z + step
+            far = (z == 0) if step == 2 else (z == PLANES - 1) if step == -2 else None
+
+            @pl.when((to >= 0) & (to < PLANES))
+            def _():
+                pltpu.make_async_remote_copy(
+                    src_ref=src, dst_ref=block(z), send_sem=ss.at[BINS],
+                    recv_sem=rs.at[i] if far is None else rs.at[jnp.where(far, j, i)],
+                    device_id=(c, at(to, y, x)), device_id_type=MESH,
+                ).start()
+
+        line_bytes[0] += size(src)
+
+    def pass_on(name, block):
+        for mine, origin, to in ((1, 3, 0), (2, 0, 3)):
+
+            @pl.when(z == mine)
+            def _():
+                landed(name + "f", block(origin))
+                pltpu.make_async_remote_copy(
+                    src_ref=block(origin), dst_ref=block(origin), send_sem=ss.at[BINS], recv_sem=rs.at[sem(name + "z")],
+                    device_id=(c, at(to, y, x)), device_id_type=MESH,
+                ).start()
+
+    def line_landed(name, blocks, own):
+        @pl.when(edge)
+        def _():
+            landed(name + "z", blocks(3 + own))
+
+        @pl.when(jnp.logical_not(edge))
+        def _():
+            landed(name + "z", blocks(2 + own))
 
     def to_plane(name, src, dst, slotted=False):
+        half = lax.rem(z, 2)
+        core = z // 2
+        if slotted:
+            recv = rs.at[jnp.where(half == 0, sem(name + "h0"), sem(name + "h1"))]
+            part = dst.at[slot(core, y, x), half]
+        else:
+            recv = rs.at[sem(name)]
+            part = dst.at[half]
         for m in range(2):
             plane = 2 * m + c
-            core = z // 2
-            half = lax.rem(z, 2)
             own = (plane == z) & (core == c)
-            part = dst.at[slot(core, y, x), half] if slotted else dst.at[half]
+            out = ss.at[odd.setdefault(name + str(m), BINS + 1 + len(odd))]
 
             @pl.when(own)
             def _():
-                keep(name, src.at[m], part)
+                pltpu.make_async_copy(src.at[m], part, recv).start()
 
             @pl.when(jnp.logical_not(own))
             def _():
-                i = sem(name)
-                j = sem(name + str(m))
                 pltpu.make_async_remote_copy(
-                    src_ref=src.at[m], dst_ref=part, send_sem=ss.at[j], recv_sem=rs.at[i],
+                    src_ref=src.at[m], dst_ref=part, send_sem=out, recv_sem=recv,
                     device_id=(core, at(plane, y, x)), device_id_type=MESH,
                 ).start()
 
-            pending.append((name + str(m), src.at[m], jnp.logical_not(own)))
+            pending.append((out, src.at[m], jnp.logical_not(own)))
 
     def from_plane(name, src, dst):
         micro, core = z // 2, lax.rem(z, 2)
+        recv = rs.at[sem(name)]
         for half in range(2):
             zz = 2 * c + half
             own = (core == c) & (zz == z)
             part = dst.at[micro]
+            out = ss.at[odd.setdefault(name + str(half), BINS + 1 + len(odd))]
 
             @pl.when(own)
             def _():
-                keep(name, src.at[half], part)
+                pltpu.make_async_copy(src.at[half], part, recv).start()
 
             @pl.when(jnp.logical_not(own))
             def _():
-                i = sem(name)
-                j = sem(name + str(half))
                 pltpu.make_async_remote_copy(
-                    src_ref=src.at[half], dst_ref=part, send_sem=ss.at[j], recv_sem=rs.at[i],
+                    src_ref=src.at[half], dst_ref=part, send_sem=out, recv_sem=recv,
                     device_id=(core, at(zz, y, x)), device_id_type=MESH,
                 ).start()
 
-            pending.append((name + str(half), src.at[half], jnp.logical_not(own)))
+            pending.append((out, src.at[half], jnp.logical_not(own)))
 
     def to_heads(name, src, dst):
         keep(name, src.at[me_head], dst.at[me_slot])
@@ -660,18 +724,46 @@
             send(name, src.at[head(cc, yy, xx)], dst.at[me_slot], (cc, at(z, yy, xx)))
         sent_later(name, src.at[pl.ds(0, GROUP - 1)])
 
-    def to_slots(name, src, dst):
-        keep(name, src.at[me_slot], dst.at[me_head])
-        for cc, yy, xx in plane_peers:
-            send(name, src.at[slot(cc, yy, xx)], dst.at[me_head], (cc, at(z, yy, xx)))
-        sent_later(name, src.at[pl.ds(0, GROUP - 1)])
+    def to_slot(name, src, dst, s):
+        device = (s // 4, at(z, lax.rem(s, 4) // 2, lax.rem(s, 2)))
+        i = sem(name)
+        out = out_sem(name)
+
+        @pl.when(s == me_slot)
+        def _():
+            pltpu.make_async_copy(src.at[s], dst.at[me_head], rs.at[i]).start()
+
+        @pl.when(s != me_slot)
+        def _():
+            pltpu.make_async_remote_copy(
+                src_ref=src.at[s], dst_ref=dst.at[me_head], send_sem=out, recv_sem=rs.at[i],
+                device_id=device, device_id_type=MESH,
+            ).start()
 
     weights = {
         "q": (w_q, s_in.at[1, pl.ds(0, 1)], g_q, c_q, p_q, q_q, z_q, o_in.at[1, pl.ds(0, 1)]),
-        "out": (w_out, s_out, g_out, c_out, p_out, q_out, z_out, o_out),
-        "up": (w_up, s_up, g_up, c_up, p_up, q_up, z_up, o_up),
-        "dn": (w_dn, s_dn, g_dn, c_dn, p_dn, q_dn, z_dn, o_dn),
     }
+
+    for i in range(2):
+        one = pl.ds(i, 1)
+        refs = (w_out, s_out, g_out, c_out, p_out, q_out, z_out, o_out)
+        weights["out" + str(i)] = tuple(
+            ref.at[:, one] if ref is p_out or ref is q_out or ref is z_out else ref.at[one] for ref in refs
+        )
+        refs = (w_up, s_up, g_up, c_up, p_up, q_up, z_up, o_up)
+        cols = pl.ds(i * 1024, 1024)
+        weights["up" + str(i)] = tuple(
+            ref.at[:, one] if ref is p_up or ref is q_up or ref is z_up
+            else ref.at[:, :, cols] if ref is s_up or ref is o_up else ref.at[one]
+            for ref in refs
+        )
+        refs = (w_dn, s_dn, g_dn, c_dn, p_dn, q_dn, z_dn, o_dn)
+        cols = pl.ds(i * 256, 256)
+        weights["dn" + str(i)] = tuple(
+            ref.at[:, one] if ref is p_dn or ref is q_dn or ref is z_dn
+            else ref.at[:, :, cols] if ref is s_dn or ref is o_dn else ref.at[one]
+            for ref in refs
+        )
 
     def halves(ref):
         cols = ref.shape[-1] // 2
@@ -682,14 +774,16 @@
     def gather_z(g):
         full, shard = weights[g][:2]
         keep(g + "z", shard, full.at[:, c, z, y, x])
-        for zz in z_peers:
-            send(g + "z", shard, full.at[:, c, z, y, x], (c, at(zz, y, x)))
-        sent_later(g + "z", full.at[:, c, pl.ds(0, 3), y, x])
+        along_z(g, shard, lambda zz: full.at[:, c, zz, y, x])
+
+    def gather_f(g):
+        full = weights[g][0]
+        pass_on(g, lambda zz: full.at[:, c, zz, y, x])
 
     def gather_1(g):
         full = weights[g][0]
         first, second = halves(full)
-        landed(g + "z", full.at[:, c, :, y, x])
+        line_landed(g, lambda n: full.at[:, c, pl.ds(0, n), y, x], 1)
         part = full.at[:, c, :, y, x, :, first]
         send(g + "1a", part, part, x_next)
         sent_later(g + "1a", part)
@@ -784,20 +878,21 @@
             total = total + line[k].astype(F32)
         result[...] = total
 
-    def spread_1(name, full):
-        own = full.at[me_slot]
-        for yy, xx in trio:
-            send(name + "p", own, own, (c, at(z, yy, xx)))
-        sent_later(name + "p", full.at[pl.ds(0, 3)])
+    def spread_1(name, full, half):
+        own = full.at[me_slot, half]
+        landed(name + "h" + str(half), own)
+        for k, (yy, xx) in enumerate(trio):
+            send(name + "p" + str(half) + str(k), own, own, (c, at(z, yy, xx)))
+            sent_later(name + "p" + str(half) + str(k), own)
         send(name + "c", own, own, core_next)
         sent_later(name + "c", own)
 
-    def spread_2(name, full):
-        landed(name + "p", full.at[pl.ds(0, 3)])
-        for yy, xx in trio:
-            part = full.at[slot(c, yy, xx)]
+    def spread_2(name, full, half):
+        for k, (yy, xx) in enumerate(trio):
+            part = full.at[slot(c, yy, xx), half]
+            landed(name + "p" + str(half) + str(k), part)
             send(name + "d", part, part, core_next)
-        sent_later(name + "d", full.at[pl.ds(0, 3)])
+            sent_later(name + "d", part)
 
     def spread_3(name, full):
         landed(name + "c", full.at[0])
@@ -809,14 +904,12 @@
 
     def merge_1(name, full, across, parts):
         landed(name + "c", across)
-
-        @pl.loop(0, 4)
-        def _(i):
-            add(full.at[c * 4 + i], across.at[i])
-
         for k, (yy, xx) in enumerate(trio):
-            send(name + "p", full.at[slot(c, yy, xx)], parts.at[k], (c, at(z, yy, xx)))
+            place = slot(c, yy, xx)
+            add(full.at[place], across.at[yy * 2 + xx])
+            send(name + "p", full.at[place], parts.at[k], (c, at(z, yy, xx)))
         sent_later(name + "p", parts)
+        add(full.at[me_slot], across.at[yx])
 
     def merge_2(name, full, parts):
         landed(name + "p", parts)
@@ -836,12 +929,13 @@
 
     def slice_2(name, full):
         landed(name + "p", full.at[:, c, z])
-        for zz in z_peers:
-            send(name + "z", full.at[:, c, z], full.at[:, c, z], (c, at(zz, y, x)))
-        sent_later(name + "z", full.at[:, c, pl.ds(0, 3)])
+        along_z(name, full.at[:, c, z], lambda zz: full.at[:, c, zz])
+
+    def slice_f(name, full):
+        pass_on(name, lambda zz: full.at[:, c, zz])
 
     def slice_3(name, full):
-        landed(name + "z", full.at[:, c, pl.ds(0, 3)])
+        line_landed(name, lambda n: full.at[:, c, pl.ds(0, n)], 0)
         send(name + "c", full.at[:, c], full.at[:, c], core_next)
         sent_later(name + "c", full.at[:, c])
 
@@ -902,7 +996,7 @@
 
     BLOCK = 256
 
-    def attend(queries, keys, values_t, weights_t, sums, outputs, causal, target):
+    def attend(queries, keys, values_t, weights_t, sums, outputs, causal, name, target, arrives):
         def make(extent):
             def body(b):
                 cols = pl.ds(pl.multiple_of(b * BLOCK, BLOCK), BLOCK)
@@ -922,6 +1016,9 @@
                 out = nn(values_t[:, :extent], low) / total
                 sums[0:1, cols] = total
                 outputs[:, cols] = out
+                for k in range(2):
+                    target[2 * b + k] = out[:, k * here : (k + 1) * here].astype(BF16)
+                    to_slot(name, target, arrives, 2 * b + k)
 
             return body
 
@@ -930,10 +1027,9 @@
             pl.loop(2, 4)(make(1024))
         else:
             pl.loop(0, 4)(make(1024))
-        for s in range(GROUP):
-            target[s] = outputs[:, s * here : (s + 1) * here].astype(BF16)
-
-    def attend_back(buffer, queries, keys_t, values, weights_t, sums, outputs, causal):
+        sent_later(name, target.at[pl.ds(0, GROUP - 1)])
+
+    def attend_back(buffer, queries, keys_t, values, weights_t, sums, outputs, causal, name, target, arrives):
         acc_k[...] = jnp.zeros_like(acc_k)
         acc_v[...] = jnp.zeros_like(acc_v)
         for s in range(GROUP):
@@ -950,7 +1046,13 @@
                 dn = dnt[:, cols]
                 spread = nn(values[:extent, :], dn)
                 slopes = (low.astype(F32) * (spread + rows_f[2:3, cols])).astype(BF16)
-                acc_q[:, cols] = nn(keys_t[:, :extent], slopes) * 0.125
+                block = (nn(keys_t[:, :extent], slopes) * 0.125).astype(BF16)
+                if name is None:
+                    dt0[0:64, cols] = block
+                else:
+                    for k in range(2):
+                        target[2 * b + k] = block[:, k * here : (k + 1) * here]
+                        to_slot(name, target, arrives, 2 * b + k)
                 acc_k[:, :extent] += nt(queries[:, cols], slopes)
                 acc_v[:, :extent] += nt(dn, low)
 
@@ -961,6 +1063,9 @@
             pl.loop(2, 4)(make(1024))
         else:
             pl.loop(0, 4)(make(1024))
+        if name is not None:
+            sent_later(name, target.at[pl.ds(0, GROUP - 1)])
+
     def by_head(target, value):
         target[...] = flip(value).astype(BF16).reshape(GROUP, 64, here)
 
@@ -1013,17 +1118,126 @@
     def bias(i):
         return biases[i : i + 1, :]
 
+    def make_masks():
+        landed("marks", all_meta.at[pl.ds(0, 7)])
+        order = lax.broadcasted_iota(jnp.int32, (1, 1024), 1)
+        place = (order // 512) * 512 + lax.rem(order // 64, 2) * 256 + lax.rem(order // 128, 4) * 64 + lax.rem(order, 64)
+        place = place.astype(F32)
+        marks = [all_meta[s].astype(F32) for s in range(GROUP)]
+        tgt_real = jnp.concatenate([mark[0:1, :] for mark in marks], axis=1)
+        src_real = jnp.concatenate([mark[1:2, :] for mark in marks], axis=1)
+        lower = lax.broadcasted_iota(jnp.int32, (32, 128), 1)
+        later = lax.broadcasted_iota(jnp.int32, (32, 128), 0)
+
+        def ends_of(row):
+            lengths = jnp.broadcast_to(row, (32, 128))
+            ends = jnp.sum(jnp.where(lower <= later, lengths, 0.0), axis=1, keepdims=True)
+            starts = jnp.sum(jnp.where(lower < later, lengths, 0.0), axis=1, keepdims=True)
+            return ends, starts
+
+        def count(flags):
+            return jnp.sum(jnp.where(flags, 1.0, 0.0), axis=0, keepdims=True)
+
+        tgt_ends, _ = ends_of(marks[0][2:3, :])
+        src_ends, src_starts = ends_of(marks[0][3:4, :])
+        tgt_seg = count(tgt_ends <= place)
+        src_seg = count(src_ends <= place)
+        src_first = count(src_starts == place)
+        self_row = jnp.where(tgt_real > 0.5, tgt_seg, -1.0)
+        cross_row = jnp.where((src_real > 0.5) | (src_first > 0.5), src_seg, -1.0)
+        rows_f[0:1, :] = tgt_seg
+        rows_f[1:2, :] = place
+        code_self[...] = jnp.transpose(jnp.broadcast_to(self_row, (128, 1024)))
+        code_cross[...] = jnp.transpose(jnp.broadcast_to(cross_row, (128, 1024)))
+        key_pos[...] = jnp.transpose(jnp.broadcast_to(place, (128, 1024)))
+
+    def feed_up(rows, i):
+        for k in (2 * i, 2 * i + 1):
+            cols = slice(k * width, (k + 1) * width)
+            inner = slice((k % 2) * width, (k % 2 + 1) * width)
+            u = nn(rows, matrix(w_up.at[i, :, :, :, :, :, inner])) + up_bias[0:1, cols]
+            square = u * u
+            t = jnp.tanh(u * (0.7978845608028654 + 0.035677408136300125 * square))
+            act[:, cols] = (0.5 * u * (1.0 + t)).astype(BF16)
+            inner = 0.7978845608028654 + 0.10703222440890037 * square
+            slope[:, cols] = 0.5 * (1.0 + t) + 0.5 * u * (1.0 - t * t) * inner
+
+    def feed_back(gf, back):
+        for k in range(4):
+            cols = slice(k * width, (k + 1) * width)
+            inner = slice((k % 2) * width, (k % 2 + 1) * width)
+            rows = pl.ds(2 * (k % 2), 2)
+            gu = nt(gf[:, 0:256], matrix(w_dn.at[0, k // 2, rows]))
+            gu = gu + nt(gf[:, 256:512], matrix(w_dn.at[1, k // 2, rows]))
+            gu = (gu * slope[:, cols]).astype(BF16)
+            gul[:, cols] = gu
+            column(7 + k, gu.astype(F32))
+            back = back + nt(gu, matrix(w_up.at[k // 2, :, :, :, :, :, inner]))
+        return back
+
+    def value_sums(grads_t):
+        total = jnp.sum(grads_t[64:128, :].astype(F32), axis=1, keepdims=True)
+        bias_cols[0] = jnp.zeros((width, 128), F32)
+        bias_cols[0, own_head, :] = jnp.broadcast_to(total, (64, 128))
+        sg0[4:5, :] = jnp.transpose(bias_cols[0])[0:1, :]
+
+    def head_sums(grads_t):
+        lanes = lax.broadcasted_iota(jnp.int32, (64, 128), 1)
+        dq_sum = jnp.sum(grads_t[0:64, :].astype(F32), axis=1, keepdims=True)
+        dv_sum = jnp.sum(grads_t[128:192, :].astype(F32), axis=1, keepdims=True)
+        bias_cols[0] = jnp.zeros((width, 128), F32)
+        bias_cols[0, own_head, :] = jnp.where(lanes == 0, dq_sum, dv_sum)
+        tg0[...] = jnp.transpose(bias_cols[0])[0:8, :]
+
+    def small(name, src, dst, device):
+        send(name, src, dst, device)
+        sent_later(name, dst)
+
+    def small_add(name, arrived, mine, total):
+        landed(name, arrived)
+        total[...] = mine[...] + arrived[...]
+
+    def small_z(name, src, dst):
+        for k in range(3):
+            send(name, src, dst.at[2 - k], (c, at(z_peers[k], y, x)))
+        sent_later(name, dst)
+
+    def small_out():
+        landed("s3", sr3)
+        sg4[...] = sg3[...] + sr3[0] + sr3[1] + sr3[2]
+        landed("t3", tr3)
+        sg4[0:2, :] = (tg3[...] + tr3[0] + tr3[1] + tr3[2])[0:2, :]
+        block = c * 16 + seq
+        tile_of = sg4[:, pl.ds(pl.multiple_of((block // 8) * 128, 128), 128)]
+        turned = pltpu.roll(tile_of, lax.rem(128 - lax.rem(block, 8) * 16, 128), 1)
+        o_bias[...] = turned[0:7, 0:16]
+        o_gain[...] = turned[11:14, 0:16]
+        o_shift[...] = turned[14:17, 0:16]
+        o_omega[...] = turned[17:20, 0:16]
+        tile_of = sg4[:, pl.ds(pl.multiple_of((lax.rem(block, 8) // 2) * 128, 128), 128)]
+        turned = pltpu.roll(tile_of, lax.rem(block, 2) * 64, 1)
+        wanted = block // 8
+        row = jnp.zeros((1, 64), F32)
+        for k in range(4):
+            row = row + turned[7 + k : 8 + k, 0:64] * (wanted == k).astype(F32)
+        o_upb[...] = row
+        ends = ((o_bias, h_bias), (o_upb, h_upb), (o_gain, h_gain_o), (o_shift, h_shift_o), (o_omega, h_omega_o))
+        for i, (src, dst) in enumerate(ends):
+            keep("e" + str(4 + i), src, dst)
+
     raw = ((raw_tm, tgt_msk), (raw_sm, src_msk), (raw_tl, tgt_len), (raw_sl, src_len))
     for i, (ref, given) in enumerate(raw):
         keep("raw" + str(i), given, ref)
+    given = ((h_biases, biases), (h_up_bias, up_bias), (h_gain, gain), (h_shift, shift), (h_omega, omega))
+    for i, (src, ref) in enumerate(given):
+        keep("given" + str(i), src, ref)
     barrier = pltpu.get_barrier_semaphore()
     greet = [(cc, at(z, yy, xx)) for cc, yy, xx in plane_peers]
     greet += [(cc, at(zz, y, x)) for zz in z_peers for cc in (c, 1 - c)]
     for device in greet:
         pl.semaphore_signal(barrier, inc=1, device_id=device, device_id_type=MESH)
     pl.semaphore_wait(barrier, len(greet))
-
-    to_plane("tok", tok, all_tok, True)
+    to_plane("x", tok, all_tok, True)
     slice_1("w0", s_in.at[0], ws0)
     slice_1("w1", s_in.at[1, pl.ds(1, 2)], ws1)
     for i, (ref, _) in enumerate(raw):
@@ -1034,82 +1248,54 @@
                 meta[m, i : i + 1, start : start + span] = ref[m]
     to_plane("meta", meta, in_meta)
     slice_2("w0", ws0)
-    gather_z("out")
-    to_plane("mem", mem, all_mem, True)
-    landed("tok", all_tok.at[me_slot])
-    spread_1("x", all_tok)
+    gather_z("out0")
+    gather_z("q")
+    to_plane("m", mem, all_mem, True)
+    spread_1("x", all_tok, 0)
+    spread_1("x", all_tok, 1)
     slice_2("w1", ws1)
-    gather_z("q")
-    gather_z("up")
-    gather_z("dn")
+    gather_z("up0")
+    gather_z("up1")
+    gather_z("dn0")
+    gather_z("dn1")
+    gather_z("out1")
     to_plane("cot", cot, in_cot)
+    for i, (_, ref) in enumerate(given):
+        landed("given" + str(i), ref)
+    for i, row in enumerate((0, 1, 4)):
+        bias_cols[i] = jnp.transpose(jnp.broadcast_to(bias(row), (128, width)))
     landed("meta", in_meta)
     lane = lax.broadcasted_iota(jnp.int32, (8, 128), 1)
     all_meta[me_slot] = jnp.where(lane < 64, in_meta[0], in_meta[1])
     for cc, yy, xx in plane_peers:
         send("marks", all_meta.at[me_slot], all_meta.at[me_slot], (cc, at(z, yy, xx)))
     sent_later("marks", all_meta.at[pl.ds(0, 7)])
-    for i, row in enumerate((0, 1, 4)):
-        bias_cols[i] = jnp.transpose(jnp.broadcast_to(bias(row), (128, width)))
-
-    landed("marks", all_meta.at[pl.ds(0, 7)])
-    order = lax.broadcasted_iota(jnp.int32, (1, 1024), 1)
-    place = (order // 512) * 512 + lax.rem(order // 64, 2) * 256 + lax.rem(order // 128, 4) * 64 + lax.rem(order, 64)
-    place = place.astype(F32)
-    marks = [all_meta[s].astype(F32) for s in range(GROUP)]
-    tgt_real = jnp.concatenate([mark[0:1, :] for mark in marks], axis=1)
-    src_real = jnp.concatenate([mark[1:2, :] for mark in marks], axis=1)
-    lower = lax.broadcasted_iota(jnp.int32, (32, 128), 1)
-    later = lax.broadcasted_iota(jnp.int32, (32, 128), 0)
-
-    def ends_of(row):
-        lengths = jnp.broadcast_to(row, (32, 128))
-        ends = jnp.sum(jnp.where(lower <= later, lengths, 0.0), axis=1, keepdims=True)
-        starts = jnp.sum(jnp.where(lower < later, lengths, 0.0), axis=1, keepdims=True)
-        return ends, starts
-
-    def count(flags):
-        return jnp.sum(jnp.where(flags, 1.0, 0.0), axis=0, keepdims=True)
-
-    tgt_ends, _ = ends_of(marks[0][2:3, :])
-    src_ends, src_starts = ends_of(marks[0][3:4, :])
-    tgt_seg = count(tgt_ends <= place)
-    src_seg = count(src_ends <= place)
-    src_first = count(src_starts == place)
-    self_row = jnp.where(tgt_real > 0.5, tgt_seg, -1.0)
-    cross_row = jnp.where((src_real > 0.5) | (src_first > 0.5), src_seg, -1.0)
-    rows_f[0:1, :] = tgt_seg
-    rows_f[1:2, :] = place
-    code_self[...] = jnp.transpose(jnp.broadcast_to(self_row, (128, 1024)))
-    code_cross[...] = jnp.transpose(jnp.broadcast_to(cross_row, (128, 1024)))
-    key_pos[...] = jnp.transpose(jnp.broadcast_to(place, (128, 1024)))
-
+    spread_2("x", all_tok, 0)
+    slice_f("w0", ws0)
+    spread_2("x", all_tok, 1)
     slice_3("w0", ws0)
-    gather_1("out")
-    spread_2("x", all_tok)
+    gather_f("out0")
+    gather_f("q")
     slice_4("w0", ws0)
     heads_weights(0, ws0)
-    landed("mem", all_mem.at[me_slot])
-    spread_1("m", all_mem)
-    gather_2("out")
     spread_3("x", all_tok)
-
     project_heads(all_tok, 0, qt0, k0, kt0, v0, vt0)
-    attend(qt0, k0, vt0, pt0, l0, ot0, True, a3)
-    to_slots("x3", a3, b3)
-    gather_3("out")
+    gather_1("out0")
+    gather_1("q")
+    make_masks()
+    gather_2("out0")
+    gather_2("q")
+    attend(qt0, k0, vt0, pt0, l0, ot0, True, "x3", a3, b3)
+    slice_f("w1", ws1)
+    gather_3("out0")
+    gather_3("q")
+    spread_1("m", all_mem, 0)
+    spread_1("m", all_mem, 1)
     slice_3("w1", ws1)
-    gather_1("q")
-    spread_2("m", all_mem)
-    gather_2("q")
-    gather_1("up")
+    gather_f("up0")
     slice_4("w1", ws1)
     heads_weights(3, ws1)
-    spread_3("m", all_mem)
-    project_heads(all_mem, 3, None, k1, kt1, v1, vt1)
-    gather_3("q")
-    gathered("out")
-
+    gathered("out0")
     landed("x3", b3)
     words_f = all_tok[me_slot].reshape(here, width).astype(F32)
     branch = tn(b3[...].reshape(width, here), matrix(w_out.at[0])) + bias(2)
@@ -1119,87 +1305,85 @@
     gathered("q")
     by_head(a4, nn(h1_low, matrix(w_q.at[0])) + bias(3))
     to_heads("x4", a4, b4)
-    gather_1("dn")
-    gather_2("up")
-
+    spread_2("m", all_mem, 0)
+    gather_f("up1")
+    gather_1("up0")
+    spread_2("m", all_mem, 1)
+    gather_f("dn0")
+    gather_1("up1")
+    spread_3("m", all_mem)
+    project_heads(all_mem, 3, None, k1, kt1, v1, vt1)
     landed("x4", b4)
     for s in range(GROUP):
         qt1[:, s * here : (s + 1) * here] = (b4[s].astype(F32) * 0.125).astype(BF16)
-    attend(qt1, k1, vt1, pt1, l1, ot1, False, a5)
-    to_slots("x5", a5, b5)
-    gather_2("dn")
-    gather_3("up")
-
+    gather_2("up0")
+    gather_f("dn1")
+    gather_f("out1")
+    attend(qt1, k1, vt1, pt1, l1, ot1, False, "x5", a5, b5)
+    gather_1("out1")
+    gather_2("up1")
+    gather_1("dn0")
+    gather_3("up0")
+    gather_1("dn1")
+    gather_2("out1")
+    gather_3("up1")
+    gather_3("out1")
+    gathered("out1")
     landed("x5", b5)
     branch = tn(b5[...].reshape(width, here), matrix(w_out.at[1])) + bias(5)
     h2, scale1 = norm(h1_f[...] * omega[1:2, :] + branch, 1, xh1)
     h2_f[...] = h2
     h2_low = h2.astype(BF16)
-    gather_3("dn")
-
-    gathered("up")
-    for k in range(4):
-        cols = slice(k * width, (k + 1) * width)
-        u = nn(h2_low, matrix(w_up.at[0, :, :, :, :, :, cols])) + up_bias[0:1, cols]
-        square = u * u
-        t = jnp.tanh(u * (0.7978845608028654 + 0.035677408136300125 * square))
-        act[:, cols] = (0.5 * u * (1.0 + t)).astype(BF16)
-        inner = 0.7978845608028654 + 0.10703222440890037 * square
-        slope[:, cols] = 0.5 * (1.0 + t) + 0.5 * u * (1.0 - t * t) * inner
-    gathered("dn")
-    branch = bias(6)
-    for k in range(4):
-        rows = w_dn.at[0, k // 2, pl.ds(2 * (k % 2), 2)]
-        branch = branch + nn(act[:, k * width : (k + 1) * width], matrix(rows))
-    h3, scale2 = norm(h2_f[...] * omega[2:3, :] + branch, 2, xh2)
+    gather_2("dn0")
+    gather_2("dn1")
+    gathered("up0")
+    feed_up(h2_low, 0)
+    gathered("up1")
+    feed_up(h2_low, 1)
+    gather_3("dn0")
+    gather_3("dn1")
+    gathered("dn0")
+    first = nn(act[...], matrix(w_dn.at[0]))
+    gathered("dn1")
+    second = nn(act[...], matrix(w_dn.at[1]))
+    h3, scale2 = norm(h2_f[...] * omega[2:3, :] + jnp.concatenate([first, second], axis=1) + bias(6), 2, xh2)
     out_res[...] = h3.astype(BF16).reshape(2, 64, width)
     from_plane("res", out_res, o_res)
-
     landed("cot", in_cot)
     grad = in_cot[...].reshape(here, width).astype(F32)
     dr, skip = norm_back(grad, 2, xh2, scale2, h2_f[...])
     gf = dr.astype(BF16)
     column(6, gf.astype(F32))
-    back = skip
-    for k in range(4):
-        cols = slice(k * width, (k + 1) * width)
-        gu = nt(gf, matrix(w_dn.at[0, k // 2, pl.ds(2 * (k % 2), 2)])) * slope[:, cols]
-        gu = gu.astype(BF16)
-        gul[:, cols] = gu
-        column(7 + k, gu.astype(F32))
-        back = back + nt(gu, matrix(w_up.at[0, :, :, :, :, :, cols]))
-
+    put(g_dn.at[0], tn(act[...], gf[:, 0:256]))
+    scatter_0("dn0")
+    put(g_dn.at[1], tn(act[...], gf[:, 256:512]))
+    scatter_0("dn1")
+    back = feed_back(gf, skip)
     dr, skip = norm_back(back, 1, xh1, scale1, h1_f[...])
     gc = dr.astype(BF16)
     column(5, gc.astype(F32))
     by_head(a6, nt(gc, matrix(w_out.at[1])))
     to_heads("x6", a6, b6)
     back = skip
-    for k in range(4):
-        put(g_dn.at[0, k // 2, pl.ds(2 * (k % 2), 2)], tn(act[:, k * width : (k + 1) * width], gf))
-    scatter_0("dn")
-    for k in range(4):
-        cols = slice(k * width, (k + 1) * width)
-        put(g_up.at[0, :, :, :, :, :, cols], tn(h2_low, gul[:, cols]))
-    scatter_0("up")
-    scatter_1("dn")
-
+    scatter_1("dn0")
+    put(g_up.at[0], tn(h2_low, gul[:, 0:1024]))
+    scatter_0("up0")
+    scatter_1("dn1")
+    put(g_up.at[1], tn(h2_low, gul[:, 1024:2048]))
+    scatter_0("up1")
     landed("x6", b6)
-    attend_back(b6, qt1, kt1, v1, pt1, l1, ot1, False)
-    for s in range(GROUP):
-        a7[s] = acc_q[:, s * here : (s + 1) * here].astype(BF16)
-    to_slots("x7", a7, b7)
-    scatter_1("up")
+    attend_back(b6, qt1, kt1, v1, pt1, l1, ot1, False, "x7", a7, b7)
     dt1[0:64, :] = acc_k[...].astype(BF16)
     dt1[64:128, :] = acc_v[...].astype(BF16)
     rows_back(dt1, 3, dx1, 1 - c)
     merge_0("dm", dx1, dc1)
+    scatter_1("up0")
     rows_back(dt1, 3, dx1, c)
     slices_back(dt1, all_mem, gs1)
     unslice_0("u1", gs1, cs1)
-    col_sums[0] = jnp.broadcast_to(jnp.sum(dt1[64:128, :].astype(F32), axis=1, keepdims=True), (64, 128))
+    value_sums(dt1)
     put(g_out.at[1], nn(b5[...].reshape(width, here), gc))
-
+    scatter_0("out1")
     landed("x7", b7)
     dq = b7[...].reshape(width, here)
     dq_row = flip(dq)
@@ -1210,103 +1394,106 @@
     column(2, ga.astype(F32))
     by_head(a8, nt(ga, matrix(w_out.at[0])))
     to_heads("x8", a8, b8)
-    back = skip
-    scatter_2("dn")
+    last = skip
+    small("s0", sg0, sr0, core_next)
     merge_1("dm", dx1, dc1, dp1)
     put(g_out.at[0], nn(b3[...].reshape(width, here), ga))
-    scatter_0("out")
+    scatter_0("out0")
     put(g_q.at[0], nt(flip(h1_low).astype(BF16), dq))
     scatter_0("q")
+    small_add("s0", sr0, sg0, sg1)
+    small("s1", sg1, sr1, y_next)
     unslice_1("u1", gs1, cs1, zs1)
-    scatter_2("up")
-    scatter_3("dn")
-
     landed("x8", b8)
-    attend_back(b8, qt0, kt0, v0, pt0, l0, ot0, True)
-    dt0[0:64, :] = acc_q[...].astype(BF16)
+    scatter_1("up1")
+    scatter_2("dn0")
+    scatter_2("dn1")
+    attend_back(b8, qt0, kt0, v0, pt0, l0, ot0, True, None, None, None)
     dt0[64:128, :] = acc_k[...].astype(BF16)
     dt0[128:192, :] = acc_v[...].astype(BF16)
     rows_back(dt0, 0, dx0, 1 - c)
     merge_0("dx", dx0, dc0)
+    head_sums(dt0)
+    small("t0", tg0, tr0, core_next)
     rows_back(dt0, 0, dx0, c)
     merge_1("dx", dx0, dc0, dp0)
+    small_add("t0", tr0, tg0, tg1)
+    small("t1", tg1, tr1, y_next)
     slices_back(dt0, all_tok, gs0)
     unslice_0("u0", gs0, cs0)
-    lanes = lax.broadcasted_iota(jnp.int32, (64, 128), 1)
-    dq_sum = jnp.sum(dt0[0:64, :].astype(F32), axis=1, keepdims=True)
-    dv_sum = jnp.sum(dt0[128:192, :].astype(F32), axis=1, keepdims=True)
-    bias_cols[0] = jnp.zeros((width, 128), F32)
-    bias_cols[0, own_head, :] = jnp.where(lanes == 0, dq_sum, jnp.where(lanes == 1, dv_sum, col_sums[0]))
-    turned = jnp.transpose(bias_cols[0])
-    sg0[0:2, :] = turned[0:2, :]
-    sg0[4:5, :] = turned[2:3, :]
-
-    send("s0", sg0, sr0, core_next)
-    sent_later("s0", sr0)
-    scatter_1("out")
+    small_add("s1", sr1, sg1, sg2)
+    small("s2", sg2, sr2, x_next)
+    scatter_1("out1")
+    scatter_1("out0")
     scatter_1("q")
+    scatter_2("up0")
+    scatter_2("up1")
     out_mem[...] = merge_2("dm", dx1, dp1).astype(BF16).reshape(2, 64, width)
     from_plane("gmem", out_mem, o_mem)
+    scatter_3("dn0")
+    scatter_3("dn1")
+    unslice_1("u0", gs0, cs0, zs0)
+    small_add("t1", tr1, tg1, tg2)
+    small("t2", tg2, tr2, x_next)
+    out_tok[...] = (merge_2("dx", dx0, dp0) + last).astype(BF16).reshape(2, 64, width)
+    from_plane("gtok", out_tok, o_tok)
+    scatter_2("out1")
+    scatter_2("out0")
+    scatter_2("q")
     unslice_2("u1", gs1, zs1, fs1, o_in.at[1, pl.ds(1, 2)])
-    scatter_3("up")
-    unslice_1("u0", gs0, cs0, zs0)
-    landed("s0", sr0)
-    sg1[...] = sg0[...] + sr0[...]
-    send("s1", sg1, sr1, y_next)
-    sent_later("s1", sr1)
-    scatter_2("out")
-    scatter_2("q")
-    out_tok[...] = (merge_2("dx", dx0, dp0) + back).astype(BF16).reshape(2, 64, width)
-    from_plane("gtok", out_tok, o_tok)
-    landed("s1", sr1)
-    sg2[...] = sg1[...] + sr1[...]
-    send("s2", sg2, sr2, x_next)
-    sent_later("s2", sr2)
-    scatter_3("out")
+    small_add("s2", sr2, sg2, sg3)
+    small_z("s3", sg3, sr3)
+    small_add("t2", tr2, tg2, tg3)
+    small_z("t3", tg3, tr3)
+    unslice_2("u0", gs0, zs0, fs0, o_in.at[0])
+    scatter_3("up0")
+    scatter_3("up1")
+    scatter_3("out1")
+    scatter_3("out0")
     scatter_3("q")
-    unslice_2("u0", gs0, zs0, fs0, o_in.at[0])
-    scattered("dn")
-    scattered("up")
-    landed("s2", sr2)
-    sg3[...] = sg2[...] + sr2[...]
-    for k in range(3):
-        send("s3", sg3, sr3.at[2 - k], (c, at(z_peers[k], y, x)))
-    sent_later("s3", sr3)
-    scattered("out")
+    scattered("dn0")
+    scattered("dn1")
+    keep("e3", o_dn, h_dn)
+    small_out()
+    scattered("up0")
+    scattered("up1")
+    keep("e2", o_up, h_up)
+    scattered("out1")
+    scattered("out0")
     scattered("q")
+    keep("e1", o_out, h_out)
     unslice_3("u1", o_in.at[1, pl.ds(1, 2)])
     unslice_3("u0", o_in.at[0])
-    landed("s3", sr3)
-    sg0_total = sg3[...] + sr3[0] + sr3[1] + sr3[2]
-    sg4[...] = sg0_total
-    block = c * 16 + seq
-    tile = sg4[:, pl.ds(pl.multiple_of((block // 8) * 128, 128), 128)]
-    turned = pltpu.roll(tile, lax.rem(128 - lax.rem(block, 8) * 16, 128), 1)
-    o_bias[...] = turned[0:7, 0:16]
-    o_gain[...] = turned[11:14, 0:16]
-    o_shift[...] = turned[14:17, 0:16]
-    o_omega[...] = turned[17:20, 0:16]
-    tile = sg4[:, pl.ds(pl.multiple_of((lax.rem(block, 8) // 2) * 128, 128), 128)]
-    turned = pltpu.roll(tile, lax.rem(block, 2) * 64, 1)
-    wanted = block // 8
-    row = jnp.zeros((1, 64), F32)
-    for k in range(4):
-        row = row + turned[7 + k : 8 + k, 0:64] * (wanted == k).astype(F32)
-    o_upb[...] = row
-
+    keep("e0", o_in, h_in)
     landed("res", o_res)
     landed("gmem", o_mem)
     landed("gtok", o_tok)
-    for entry in pending:
-        if len(entry) == 2:
-            wait(ss.at[sem(entry[0])], entry[1])
+    for i, ref in enumerate((h_in, h_out, h_up, h_dn, h_bias, h_upb, h_gain_o, h_shift_o, h_omega_o)):
+        landed("e" + str(i), ref)
+    for semaphore, ref, when in pending:
+        if when is None:
+            wait(semaphore, ref)
         else:
 
-            @pl.when(entry[2])
+            @pl.when(when)
             def _():
-                wait(ss.at[sem(entry[0])], entry[1])
-
-    assert len(names) <= ss.shape[0], len(names)
+                wait(semaphore, ref)
+
+    for i, total in enumerate(bins):
+        if total:
+            wait(ss.at[i], gauge.at[pl.ds(0, total // 1024)])
+    units = line_bytes[0] // UNIT
+    assert line_bytes[0] % UNIT == 0
+
+    @pl.when(edge)
+    def _():
+        wait(ss.at[BINS], gauge.at[pl.ds(0, 2 * units * 16)])
+
+    @pl.when(jnp.logical_not(edge))
+    def _():
+        wait(ss.at[BINS], gauge.at[pl.ds(0, 4 * units * 16)])
+
+    assert len(names) <= NAMES and len(bins) <= BINS and BINS + 1 + len(odd) <= ss.shape[0]
 
 
 def copy_kernel(*refs):
@@ -1322,8 +1509,8 @@
     any_space = pl.BlockSpec(memory_space=pl.ANY)
     vmem = pl.BlockSpec(memory_space=pltpu.VMEM)
     lines = (CORES, PLANES, YS, XS)
-    leads = {"q": 1, "out": 2, "up": 1, "dn": 1}
-    shards = {"q": (16, 512), "out": (16, 512), "up": (16, 2048), "dn": (64, 512)}
+    leads = {"q": 1, "out": 2, "up": 2, "dn": 2}
+    shards = {"q": (16, 512), "out": (16, 512), "up": (16, 1024), "dn": (64, 256)}
     kinds = tuple(leads)
 
     def low(*shape):
@@ -1338,7 +1525,10 @@
     def halved(k, *middle):
         return low(2, leads[k], *middle, shards[k][0], shards[k][1] // 2)
 
-    scratch = [whole(k) for k in kinds] * 2
+    params = [full(7, 512), full(1, 2048), full(3, 512), full(3, 512), full(3, 512)]
+    results = [(2, 3, 16, 512), (2, 16, 512), (1, 16, 2048), (1, 64, 512), (7, 16), (1, 64), (3, 16), (3, 16), (3, 16)]
+    scratch = params + [full(*shape) for shape in results]
+    scratch += [whole(k) for k in kinds] * 2
     scratch += [low(leads[k], *lines[1:], *shards[k]) for k in kinds]
     scratch += [halved(k, PLANES, 2) for k in kinds] + [halved(k, PLANES) for k in kinds]
     scratch += [low(3, leads[k], *shards[k]) for k in kinds]
@@ -1351,12 +1541,13 @@
     scratch += [low(GROUP, 2, 64, 512)] * 2 + [low(4, 2, 64, 512)] * 2 + [low(3, 2, 64, 512)] * 2
     scratch += [low(GROUP, 64, 128)] * 12 + [local_rows] * 3
     scratch += [full(24, 512)] * 8 + [full(3, 24, 512)]
+    scratch += [full(8, 512)] * 7 + [full(3, 8, 512)]
     scratch += [full(1024, 128)] * 3 + [full(8, 1024)]
     scratch += ([low(64, 1024)] * 3 + [low(1024, 64)] * 2 + [low(1024, 1024), full(1, 1024), full(64, 1024)]) * 2
-    scratch += [low(64, 1024)] + [full(64, 1024)] * 3
+    scratch += [low(64, 1024)] + [full(64, 1024)] * 2
     scratch += [low(128, 2048), full(128, 2048), low(128, 2048)] + [full(128, 512)] * 5
-    scratch += [low(5, 128, 512), full(3, 512, 128), full(3, 128, 512), low(192, 1024), low(128, 1024), full(1, 64, 128)]
-    scratch += [pltpu.SemaphoreType.DMA((128,)), pltpu.SemaphoreType.DMA((128,))]
+    scratch += [low(5, 128, 512), full(3, 512, 128), full(3, 128, 512), low(192, 1024), low(128, 1024), low(2048, 512)]
+    scratch += [pltpu.SemaphoreType.DMA((36,)), pltpu.SemaphoreType.DMA((NAMES,))]
     rows = jax.ShapeDtypeStruct((2, 64, 512), BF16)
 
     def wide_out(*shape):
@@ -1365,12 +1556,9 @@
     outs = pl.pallas_call(
         fused_kernel,
         name="layer",
-        out_shape=(
-            rows, rows, rows, wide_out(2, 3, 16, 512), wide_out(2, 16, 512), wide_out(1, 16, 2048),
-            wide_out(1, 64, 512), wide_out(7, 16), wide_out(1, 64), wide_out(3, 16), wide_out(3, 16), wide_out(3, 16),
-        ),
-        in_specs=[any_space] * 11 + [vmem] * 5,
-        out_specs=(any_space,) * 3 + (vmem,) * 9,
+        out_shape=(rows, rows, rows, *(wide_out(*shape) for shape in results)),
+        in_specs=[any_space] * 16,
+        out_specs=(any_space,) * 12,
         scratch_shapes=scratch,
         compiler_params=pltpu.CompilerParams(collective_id=0, has_side_effects=True, vmem_limit_bytes=60 * 1024 * 1024),
     )(

time: 128 us -> 130 us (1.016)
  Pallas kernels: 127 us -> 129 us
    pallas_call x1, Pallas kernels: 124 us -> 127 us  [fused_local(): pl.pallas_call(fused_kernel, name='layer', out_shape=(rows, rows, rows, *...]
where the time goes in v3:
time: 130 us
  Pallas kernels  129 us (99%)
    pallas_call x1, Pallas kernels, fused_local(): pl.pallas_call(fused_kernel, name='layer', out_shape=(rows, rows, rows, *...  127 us

profile of v3, /device:TPU:0, one launch (start us, length us, event | category | flops | bytes accessed | tf_op | source)
XLA Modules:
  0.0 130.0 jit_solution(15549636832569172726)
XLA Ops:
  0.7 127.0 %layer.1 = (bf16[2,64,512]{2,1,0:T(8,128)(2,1)}, bf16[2,64,512]{2,1,0:T(8,128)(2,1)}, bf16[2,64,512]{2,1,0:T(8,128)(2,1)}, f32[2,3,16,512]{3,2,1,0:T(8,128)}, f3...) custom-call(bf16[2,64,512]{2,1,0:T(8,128)(2,1)} %bitcast.24, ...), custom_call_target="tpu_custom_call" | custom-call | tf_op jit(solution)/shard_map/layer/pallas_call | solution.py:1556
  127.6 2.2 %hand_over.1 = (bf16[2,64,512]{2,1,0:T(8,128)(2,1)}, bf16[2,64,512]{2,1,0:T(8,128)(2,1)}, bf16[2,64,512]{2,1,0:T(8,128)(2,1)}, f32[2,3,16,512]{3,2,1,0:T(8,128)}...) custom-call(bf16[2,64,512]{2,1,0:T(8,128)(2,1)} %get-tuple-element.3, ...), custom_call_target="tpu_custom_call" | custom-call | tf_op jit(solution)/shard_map/hand_over/pallas_call | solution.py:1570

commit v4 on v3

--- a/solution.py
+++ b/solution.py
@@ -1237,236 +1237,236 @@
     for device in greet:
         pl.semaphore_signal(barrier, inc=1, device_id=device, device_id_type=MESH)
     pl.semaphore_wait(barrier, len(greet))
-    to_plane("x", tok, all_tok, True)
-    slice_1("w0", s_in.at[0], ws0)
-    slice_1("w1", s_in.at[1, pl.ds(1, 2)], ws1)
+    to_plane("m", mem, all_mem, True)
     for i, (ref, _) in enumerate(raw):
         landed("raw" + str(i), ref)
         span = ref.shape[2]
         for m in range(2):
             for start in (0, 64):
                 meta[m, i : i + 1, start : start + span] = ref[m]
+    slice_1("w0", s_in.at[0], ws0)
     to_plane("meta", meta, in_meta)
+    for i, (_, ref) in enumerate(given):
+        landed("given" + str(i), ref)
+    gather_z("out0")
+    slice_1("w1", s_in.at[1, pl.ds(1, 2)], ws1)
+    gather_z("out1")
+    for i, row in enumerate((0, 1, 4)):
+        bias_cols[i] = jnp.transpose(jnp.broadcast_to(bias(row), (128, width)))
+    to_plane("x", tok, all_tok, True)
+    gather_z("up1")
+    spread_1("m", all_mem, 0)
+    gather_z("q")
+    gather_f("out0")
     slice_2("w0", ws0)
-    gather_z("out0")
-    gather_z("q")
-    to_plane("m", mem, all_mem, True)
+    spread_1("m", all_mem, 1)
     spread_1("x", all_tok, 0)
+    gather_f("out1")
     spread_1("x", all_tok, 1)
     slice_2("w1", ws1)
+    spread_2("m", all_mem, 0)
+    gather_f("up1")
+    landed("meta", in_meta)
+    gather_f("q")
+    spread_2("x", all_tok, 0)
+    slice_f("w0", ws0)
+    lane = lax.broadcasted_iota(jnp.int32, (8, 128), 1)
+    gather_z("dn0")
     gather_z("up0")
-    gather_z("up1")
-    gather_z("dn0")
-    gather_z("dn1")
-    gather_z("out1")
-    to_plane("cot", cot, in_cot)
-    for i, (_, ref) in enumerate(given):
-        landed("given" + str(i), ref)
-    for i, row in enumerate((0, 1, 4)):
-        bias_cols[i] = jnp.transpose(jnp.broadcast_to(bias(row), (128, width)))
-    landed("meta", in_meta)
-    lane = lax.broadcasted_iota(jnp.int32, (8, 128), 1)
+    gather_1("out1")
     all_meta[me_slot] = jnp.where(lane < 64, in_meta[0], in_meta[1])
+    gather_1("out0")
+    gather_1("up1")
     for cc, yy, xx in plane_peers:
         send("marks", all_meta.at[me_slot], all_meta.at[me_slot], (cc, at(z, yy, xx)))
+    spread_2("x", all_tok, 1)
+    gather_2("out0")
+    slice_3("w0", ws0)
+    slice_f("w1", ws1)
     sent_later("marks", all_meta.at[pl.ds(0, 7)])
-    spread_2("x", all_tok, 0)
-    slice_f("w0", ws0)
-    spread_2("x", all_tok, 1)
-    slice_3("w0", ws0)
-    gather_f("out0")
-    gather_f("q")
+    gather_f("dn0")
+    gather_1("q")
+    spread_2("m", all_mem, 1)
+    gather_2("out1")
+    gather_z("dn1")
+    make_masks()
+    gather_2("q")
+    gather_1("dn0")
+    gather_f("dn1")
     slice_4("w0", ws0)
     heads_weights(0, ws0)
+    slice_3("w1", ws1)
+    gather_3("out1")
     spread_3("x", all_tok)
+    to_plane("cot", cot, in_cot)
+    gather_2("up1")
     project_heads(all_tok, 0, qt0, k0, kt0, v0, vt0)
-    gather_1("out0")
-    gather_1("q")
-    make_masks()
-    gather_2("out0")
-    gather_2("q")
+    gather_3("out0")
+    gather_1("dn1")
     attend(qt0, k0, vt0, pt0, l0, ot0, True, "x3", a3, b3)
-    slice_f("w1", ws1)
-    gather_3("out0")
+    gather_3("up1")
+    gather_2("dn0")
+    gather_2("dn1")
+    gathered("out0")
+    spread_3("m", all_mem)
     gather_3("q")
-    spread_1("m", all_mem, 0)
-    spread_1("m", all_mem, 1)
-    slice_3("w1", ws1)
-    gather_f("up0")
-    slice_4("w1", ws1)
-    heads_weights(3, ws1)
-    gathered("out0")
+    gathered("q")
     landed("x3", b3)
     words_f = all_tok[me_slot].reshape(here, width).astype(F32)
+    gather_f("up0")
+    gather_3("dn0")
     branch = tn(b3[...].reshape(width, here), matrix(w_out.at[0])) + bias(2)
     h1, scale0 = norm(words_f * omega[0:1, :] + branch, 0, xh0)
     h1_f[...] = h1
+    slice_4("w1", ws1)
+    gathered("out1")
     h1_low = h1.astype(BF16)
-    gathered("q")
     by_head(a4, nn(h1_low, matrix(w_q.at[0])) + bias(3))
+    gather_1("up0")
+    heads_weights(3, ws1)
+    project_heads(all_mem, 3, None, k1, kt1, v1, vt1)
     to_heads("x4", a4, b4)
-    spread_2("m", all_mem, 0)
-    gather_f("up1")
-    gather_1("up0")
-    spread_2("m", all_mem, 1)
-    gather_f("dn0")
-    gather_1("up1")
-    spread_3("m", all_mem)
-    project_heads(all_mem, 3, None, k1, kt1, v1, vt1)
+    gather_3("dn1")
+    gathered("dn0")
+    gather_2("up0")
     landed("x4", b4)
     for s in range(GROUP):
         qt1[:, s * here : (s + 1) * here] = (b4[s].astype(F32) * 0.125).astype(BF16)
-    gather_2("up0")
-    gather_f("dn1")
-    gather_f("out1")
+    gathered("up1")
+    gathered("dn1")
     attend(qt1, k1, vt1, pt1, l1, ot1, False, "x5", a5, b5)
-    gather_1("out1")
-    gather_2("up1")
-    gather_1("dn0")
     gather_3("up0")
-    gather_1("dn1")
-    gather_2("out1")
-    gather_3("up1")
-    gather_3("out1")
-    gathered("out1")
     landed("x5", b5)
     branch = tn(b5[...].reshape(width, here), matrix(w_out.at[1])) + bias(5)
     h2, scale1 = norm(h1_f[...] * omega[1:2, :] + branch, 1, xh1)
+    gathered("up0")
     h2_f[...] = h2
     h2_low = h2.astype(BF16)
-    gather_2("dn0")
-    gather_2("dn1")
-    gathered("up0")
     feed_up(h2_low, 0)
-    gathered("up1")
     feed_up(h2_low, 1)
-    gather_3("dn0")
-    gather_3("dn1")
-    gathered("dn0")
     first = nn(act[...], matrix(w_dn.at[0]))
-    gathered("dn1")
     second = nn(act[...], matrix(w_dn.at[1]))
     h3, scale2 = norm(h2_f[...] * omega[2:3, :] + jnp.concatenate([first, second], axis=1) + bias(6), 2, xh2)
     out_res[...] = h3.astype(BF16).reshape(2, 64, width)
-    from_plane("res", out_res, o_res)
     landed("cot", in_cot)
     grad = in_cot[...].reshape(here, width).astype(F32)
     dr, skip = norm_back(grad, 2, xh2, scale2, h2_f[...])
     gf = dr.astype(BF16)
+    put(g_dn.at[0], tn(act[...], gf[:, 0:256]))
     column(6, gf.astype(F32))
-    put(g_dn.at[0], tn(act[...], gf[:, 0:256]))
     scatter_0("dn0")
-    put(g_dn.at[1], tn(act[...], gf[:, 256:512]))
-    scatter_0("dn1")
     back = feed_back(gf, skip)
+    scatter_1("dn0")
     dr, skip = norm_back(back, 1, xh1, scale1, h1_f[...])
     gc = dr.astype(BF16)
+    put(g_up.at[0], tn(h2_low, gul[:, 0:1024]))
+    put(g_out.at[1], nn(b5[...].reshape(width, here), gc))
+    scatter_0("up0")
+    scatter_0("out1")
     column(5, gc.astype(F32))
     by_head(a6, nt(gc, matrix(w_out.at[1])))
     to_heads("x6", a6, b6)
+    from_plane("res", out_res, o_res)
+    put(g_dn.at[1], tn(act[...], gf[:, 256:512]))
+    scatter_1("up0")
+    scatter_0("dn1")
+    scatter_2("dn0")
     back = skip
-    scatter_1("dn0")
-    put(g_up.at[0], tn(h2_low, gul[:, 0:1024]))
-    scatter_0("up0")
-    scatter_1("dn1")
     put(g_up.at[1], tn(h2_low, gul[:, 1024:2048]))
-    scatter_0("up1")
+    scatter_1("out1")
     landed("x6", b6)
     attend_back(b6, qt1, kt1, v1, pt1, l1, ot1, False, "x7", a7, b7)
     dt1[0:64, :] = acc_k[...].astype(BF16)
+    scatter_2("up0")
+    scatter_3("dn0")
     dt1[64:128, :] = acc_v[...].astype(BF16)
     rows_back(dt1, 3, dx1, 1 - c)
     merge_0("dm", dx1, dc1)
-    scatter_1("up0")
     rows_back(dt1, 3, dx1, c)
+    scatter_1("dn1")
     slices_back(dt1, all_mem, gs1)
+    landed("x7", b7)
+    scatter_2("out1")
+    dq = b7[...].reshape(width, here)
+    scatter_0("up1")
+    dq_row = flip(dq)
+    put(g_q.at[0], nt(flip(h1_low).astype(BF16), dq))
     unslice_0("u1", gs1, cs1)
+    scatter_3("up0")
     value_sums(dt1)
-    put(g_out.at[1], nn(b5[...].reshape(width, here), gc))
-    scatter_0("out1")
-    landed("x7", b7)
-    dq = b7[...].reshape(width, here)
-    dq_row = flip(dq)
     column(3, dq_row)
     back = back + nt(dq_row.astype(BF16), matrix(w_q.at[0]))
     dr, skip = norm_back(back, 0, xh0, scale0, words_f)
     ga = dr.astype(BF16)
     column(2, ga.astype(F32))
+    small("s0", sg0, sr0, core_next)
     by_head(a8, nt(ga, matrix(w_out.at[0])))
     to_heads("x8", a8, b8)
-    last = skip
-    small("s0", sg0, sr0, core_next)
-    merge_1("dm", dx1, dc1, dp1)
+    scatter_2("dn1")
     put(g_out.at[0], nn(b3[...].reshape(width, here), ga))
     scatter_0("out0")
-    put(g_q.at[0], nt(flip(h1_low).astype(BF16), dq))
+    scatter_3("out1")
+    last = skip
+    scatter_1("up1")
+    unslice_1("u1", gs1, cs1, zs1)
+    small_add("s0", sr0, sg0, sg1)
+    landed("x8", b8)
     scatter_0("q")
-    small_add("s0", sr0, sg0, sg1)
+    scatter_1("out0")
     small("s1", sg1, sr1, y_next)
-    unslice_1("u1", gs1, cs1, zs1)
-    landed("x8", b8)
-    scatter_1("up1")
-    scatter_2("dn0")
-    scatter_2("dn1")
     attend_back(b8, qt0, kt0, v0, pt0, l0, ot0, True, None, None, None)
+    scattered("dn0")
     dt0[64:128, :] = acc_k[...].astype(BF16)
+    scatter_1("q")
+    scatter_3("dn1")
     dt0[128:192, :] = acc_v[...].astype(BF16)
-    rows_back(dt0, 0, dx0, 1 - c)
-    merge_0("dx", dx0, dc0)
-    head_sums(dt0)
-    small("t0", tg0, tr0, core_next)
-    rows_back(dt0, 0, dx0, c)
-    merge_1("dx", dx0, dc0, dp0)
-    small_add("t0", tr0, tg0, tg1)
-    small("t1", tg1, tr1, y_next)
     slices_back(dt0, all_tok, gs0)
     unslice_0("u0", gs0, cs0)
+    rows_back(dt0, 0, dx0, 1 - c)
+    landed("res", o_res)
+    scatter_2("up1")
+    head_sums(dt0)
     small_add("s1", sr1, sg1, sg2)
+    unslice_1("u0", gs0, cs0, zs0)
     small("s2", sg2, sr2, x_next)
-    scatter_1("out1")
-    scatter_1("out0")
-    scatter_1("q")
-    scatter_2("up0")
-    scatter_2("up1")
+    small("t0", tg0, tr0, core_next)
+    merge_0("dx", dx0, dc0)
+    scatter_2("q")
+    small_add("t0", tr0, tg0, tg1)
+    scatter_2("out0")
+    scattered("up0")
+    rows_back(dt0, 0, dx0, c)
+    small("t1", tg1, tr1, y_next)
+    merge_1("dm", dx1, dc1, dp1)
+    merge_1("dx", dx0, dc0, dp0)
+    scatter_3("out0")
+    scatter_3("up1")
+    scatter_3("q")
+    small_add("s2", sr2, sg2, sg3)
+    small_z("s3", sg3, sr3)
+    scattered("up1")
     out_mem[...] = merge_2("dm", dx1, dp1).astype(BF16).reshape(2, 64, width)
     from_plane("gmem", out_mem, o_mem)
-    scatter_3("dn0")
-    scatter_3("dn1")
-    unslice_1("u0", gs0, cs0, zs0)
+    unslice_2("u0", gs0, zs0, fs0, o_in.at[0])
+    scattered("dn1")
+    keep("e3", o_dn, h_dn)
     small_add("t1", tr1, tg1, tg2)
     small("t2", tg2, tr2, x_next)
+    unslice_2("u1", gs1, zs1, fs1, o_in.at[1, pl.ds(1, 2)])
+    small_add("t2", tr2, tg2, tg3)
+    small_z("t3", tg3, tr3)
     out_tok[...] = (merge_2("dx", dx0, dp0) + last).astype(BF16).reshape(2, 64, width)
     from_plane("gtok", out_tok, o_tok)
-    scatter_2("out1")
-    scatter_2("out0")
-    scatter_2("q")
-    unslice_2("u1", gs1, zs1, fs1, o_in.at[1, pl.ds(1, 2)])
-    small_add("s2", sr2, sg2, sg3)
-    small_z("s3", sg3, sr3)
-    small_add("t2", tr2, tg2, tg3)
-    small_z("t3", tg3, tr3)
-    unslice_2("u0", gs0, zs0, fs0, o_in.at[0])
-    scatter_3("up0")
-    scatter_3("up1")
-    scatter_3("out1")
-    scatter_3("out0")
-    scatter_3("q")
-    scattered("dn0")
-    scattered("dn1")
-    keep("e3", o_dn, h_dn)
     small_out()
-    scattered("up0")
-    scattered("up1")
+    scattered("out0")
+    landed("gmem", o_mem)
     keep("e2", o_up, h_up)
+    unslice_3("u0", o_in.at[0])
     scattered("out1")
-    scattered("out0")
+    keep("e1", o_out, h_out)
     scattered("q")
-    keep("e1", o_out, h_out)
     unslice_3("u1", o_in.at[1, pl.ds(1, 2)])
-    unslice_3("u0", o_in.at[0])
     keep("e0", o_in, h_in)
-    landed("res", o_res)
-    landed("gmem", o_mem)
     landed("gtok", o_tok)
     for i, ref in enumerate((h_in, h_out, h_up, h_dn, h_bias, h_upb, h_gain_o, h_shift_o, h_omega_o)):
         landed("e" + str(i), ref)

time: 130 us -> 114 us (0.88)
  Pallas kernels: 129 us -> 113 us
    pallas_call x1, Pallas kernels: 127 us -> 110 us  [fused_local(): pl.pallas_call(fused_kernel, name='layer', out_shape=(rows, rows, rows, *...]
where the time goes in v4:
time: 114 us; the launch traced here: 113 us
  Pallas kernels  113 us (99%)
    pallas_call x1, Pallas kernels, fused_local(): pl.pallas_call(fused_kernel, name='layer', out_shape=(rows, rows, rows, *...  110 us

profile of v4, /device:TPU:0, one launch (start us, length us, event | category | flops | bytes accessed | tf_op | source)
XLA Modules:
  0.0 113.4 jit_solution(13362650398971256629)
XLA Ops:
  0.7 110.3 %layer.1 = (bf16[2,64,512]{2,1,0:T(8,128)(2,1)}, bf16[2,64,512]{2,1,0:T(8,128)(2,1)}, bf16[2,64,512]{2,1,0:T(8,128)(2,1)}, f32[2,3,16,512]{3,2,1,0:T(8,128)}, f3...) custom-call(bf16[2,64,512]{2,1,0:T(8,128)(2,1)} %bitcast.24, ...), custom_call_target="tpu_custom_call" | custom-call | tf_op jit(solution)/shard_map/layer/pallas_call | solution.py:1556
  111.0 2.2 %hand_over.1 = (bf16[2,64,512]{2,1,0:T(8,128)(2,1)}, bf16[2,64,512]{2,1,0:T(8,128)(2,1)}, bf16[2,64,512]{2,1,0:T(8,128)(2,1)}, f32[2,3,16,512]{3,2,1,0:T(8,128)}...) custom-call(bf16[2,64,512]{2,1,0:T(8,128)(2,1)} %get-tuple-element.3, ...), custom_call_target="tpu_custom_call" | custom-call | tf_op jit(solution)/shard_map/hand_over/pallas_call | solution.py:1570

commit v5 on v4

--- a/solution.py
+++ b/solution.py
@@ -515,8 +515,8 @@
 MESH = pl.DeviceIdType.MESH
 UNIT = 16 * 1024
 BINS = 16
-NAMES = 168
-ODD = ("marks", "w0p", "w1p", "u0p")
+NAMES = 192
+ODD = ("marks", "w0p", "w1p", "u0p", "x3", "x5", "x7")
 F32 = jnp.float32
 BF16 = jnp.bfloat16
 PLANES, YS, XS, CORES = 4, 2, 2, 2
@@ -725,15 +725,15 @@
         sent_later(name, src.at[pl.ds(0, GROUP - 1)])
 
     def to_slot(name, src, dst, s):
-        device = (s // 4, at(z, lax.rem(s, 4) // 2, lax.rem(s, 2)))
+        device = (s // 4, at(z, (s % 4) // 2, s % 2))
         i = sem(name)
         out = out_sem(name)
 
-        @pl.when(s == me_slot)
+        @pl.when(me_slot == s)
         def _():
             pltpu.make_async_copy(src.at[s], dst.at[me_head], rs.at[i]).start()
 
-        @pl.when(s != me_slot)
+        @pl.when(me_slot != s)
         def _():
             pltpu.make_async_remote_copy(
                 src_ref=src.at[s], dst_ref=dst.at[me_head], send_sem=out, recv_sem=rs.at[i],
@@ -878,21 +878,33 @@
             total = total + line[k].astype(F32)
         result[...] = total
 
+    left, right = pl.ds(0, 256), pl.ds(256, 256)
+    y_slot, x_slot, far_slot = slot(c, 1 - y, x), slot(c, y, 1 - x), slot(c, 1 - y, 1 - x)
+
     def spread_1(name, full, half):
         own = full.at[me_slot, half]
         landed(name + "h" + str(half), own)
-        for k, (yy, xx) in enumerate(trio):
-            send(name + "p" + str(half) + str(k), own, own, (c, at(z, yy, xx)))
-            sent_later(name + "p" + str(half) + str(k), own)
-        send(name + "c", own, own, core_next)
-        sent_later(name + "c", own)
+        for which, device in (("y", y_next), ("x", x_next), ("c", core_next)):
+            which = which if which == "c" else which + str(half)
+            send(name + which, own, own, device)
+            sent_later(name + which, own)
 
     def spread_2(name, full, half):
-        for k, (yy, xx) in enumerate(trio):
-            part = full.at[slot(c, yy, xx), half]
-            landed(name + "p" + str(half) + str(k), part)
+        for which, place, cols, device in (("y", y_slot, right, x_next), ("x", x_slot, left, y_next)):
+            part = full.at[place, half]
+            landed(name + which + str(half), part)
+            half_of = full.at[place, half, :, cols]
+            send(name + "q" + which + str(half), half_of, half_of, device)
+            sent_later(name + "q" + which + str(half), half_of)
             send(name + "d", part, part, core_next)
             sent_later(name + "d", part)
+
+    def spread_4(name, full, half):
+        part = full.at[far_slot, half]
+        landed(name + "qy" + str(half), full.at[far_slot, half, :, right])
+        landed(name + "qx" + str(half), full.at[far_slot, half, :, left])
+        send(name + "d", part, part, core_next)
+        sent_later(name + "d", part)
 
     def spread_3(name, full):
         landed(name + "c", full.at[0])
@@ -904,17 +916,29 @@
 
     def merge_1(name, full, across, parts):
         landed(name + "c", across)
-        for k, (yy, xx) in enumerate(trio):
-            place = slot(c, yy, xx)
-            add(full.at[place], across.at[yy * 2 + xx])
-            send(name + "p", full.at[place], parts.at[k], (c, at(z, yy, xx)))
-        sent_later(name + "p", parts)
+        add(full.at[far_slot], across.at[(1 - y) * 2 + 1 - x])
+        send(name + "qx", full.at[far_slot, :, :, left], parts.at[2, :, :, left], y_next)
+        send(name + "qy", full.at[far_slot, :, :, right], parts.at[2, :, :, right], x_next)
+        sent_later(name + "q", parts.at[2])
+        add(full.at[x_slot], across.at[y * 2 + 1 - x])
+        add(full.at[y_slot], across.at[(1 - y) * 2 + x])
         add(full.at[me_slot], across.at[yx])
 
+    def merge_3(name, full, parts):
+        landed(name + "qx", parts.at[2, :, :, left])
+        add(full.at[x_slot, :, :, left], parts.at[2, :, :, left])
+        send(name + "px", full.at[x_slot], parts.at[0], x_next)
+        sent_later(name + "px", parts.at[0])
+        landed(name + "qy", parts.at[2, :, :, right])
+        add(full.at[y_slot, :, :, right], parts.at[2, :, :, right])
+        send(name + "py", full.at[y_slot], parts.at[1], y_next)
+        sent_later(name + "py", parts.at[1])
+
     def merge_2(name, full, parts):
-        landed(name + "p", parts)
+        landed(name + "px", parts.at[0])
+        landed(name + "py", parts.at[1])
         total = full[me_slot].astype(F32)
-        for k in range(3):
+        for k in range(2):
             total = total + parts[k].astype(F32)
         return total.reshape(here, width)
 
@@ -996,40 +1020,32 @@
 
     BLOCK = 256
 
-    def attend(queries, keys, values_t, weights_t, sums, outputs, causal, name, target, arrives):
-        def make(extent):
-            def body(b):
-                cols = pl.ds(pl.multiple_of(b * BLOCK, BLOCK), BLOCK)
-                scores = nn(keys[:extent, :], queries[:, cols])
-                seg = rows_f[0:1, cols]
-                code = (code_self if causal else code_cross)[:extent, :]
-                permit = jnp.concatenate([code, code], axis=1) == seg
-                if causal:
-                    pos = key_pos[:extent, :]
-                    pos = jnp.concatenate([pos, pos], axis=1)
-                    mine = rows_f[1:2, cols]
-                    permit = (permit & (pos <= mine)) | (pos == mine)
-                weight = jnp.where(permit, jnp.exp(scores), 0.0)
-                total = jnp.sum(weight, axis=0, keepdims=True)
-                low = weight.astype(BF16)
-                weights_t[:extent, cols] = low
-                out = nn(values_t[:, :extent], low) / total
-                sums[0:1, cols] = total
-                outputs[:, cols] = out
-                for k in range(2):
-                    target[2 * b + k] = out[:, k * here : (k + 1) * here].astype(BF16)
-                    to_slot(name, target, arrives, 2 * b + k)
-
-            return body
-
+    def attend(b, queries, keys, values_t, weights_t, sums, outputs, causal, name, target, arrives):
+        extent = 512 if causal and b < 2 else 1024
+        cols = slice(b * BLOCK, (b + 1) * BLOCK)
+        scores = nn(keys[:extent, :], queries[:, cols])
+        seg = rows_f[0:1, cols]
+        code = (code_self if causal else code_cross)[:extent, :]
+        permit = jnp.concatenate([code, code], axis=1) == seg
         if causal:
-            pl.loop(0, 2)(make(512))
-            pl.loop(2, 4)(make(1024))
-        else:
-            pl.loop(0, 4)(make(1024))
-        sent_later(name, target.at[pl.ds(0, GROUP - 1)])
-
-    def attend_back(buffer, queries, keys_t, values, weights_t, sums, outputs, causal, name, target, arrives):
+            pos = key_pos[:extent, :]
+            pos = jnp.concatenate([pos, pos], axis=1)
+            mine = rows_f[1:2, cols]
+            permit = (permit & (pos <= mine)) | (pos == mine)
+        weight = jnp.where(permit, jnp.exp(scores), 0.0)
+        total = jnp.sum(weight, axis=0, keepdims=True)
+        low = weight.astype(BF16)
+        weights_t[:extent, cols] = low
+        out = nn(values_t[:, :extent], low) / total
+        sums[0:1, cols] = total
+        outputs[:, cols] = out
+        for k in range(2):
+            target[2 * b + k] = out[:, k * here : (k + 1) * here].astype(BF16)
+            to_slot(name, target, arrives, 2 * b + k)
+        if b == 3:
+            sent_later(name, target.at[pl.ds(0, GROUP - 1)])
+
+    def attend_start(buffer, sums, outputs):
         acc_k[...] = jnp.zeros_like(acc_k)
         acc_v[...] = jnp.zeros_like(acc_v)
         for s in range(GROUP):
@@ -1039,32 +1055,24 @@
             dnt[:, cols] = (grad * inverse).astype(BF16)
             rows_f[2:3, cols] = -jnp.sum(grad * outputs[:, cols], axis=0, keepdims=True) * inverse
 
-        def make(extent):
-            def body(b):
-                cols = pl.ds(pl.multiple_of(b * BLOCK, BLOCK), BLOCK)
-                low = weights_t[:extent, cols]
-                dn = dnt[:, cols]
-                spread = nn(values[:extent, :], dn)
-                slopes = (low.astype(F32) * (spread + rows_f[2:3, cols])).astype(BF16)
-                block = (nn(keys_t[:, :extent], slopes) * 0.125).astype(BF16)
-                if name is None:
-                    dt0[0:64, cols] = block
-                else:
-                    for k in range(2):
-                        target[2 * b + k] = block[:, k * here : (k + 1) * here]
-                        to_slot(name, target, arrives, 2 * b + k)
-                acc_k[:, :extent] += nt(queries[:, cols], slopes)
-                acc_v[:, :extent] += nt(dn, low)
-
-            return body
-
-        if causal:
-            pl.loop(0, 2)(make(512))
-            pl.loop(2, 4)(make(1024))
+    def attend_back(b, queries, keys_t, values, weights_t, causal, name, target, arrives):
+        extent = 512 if causal and b < 2 else 1024
+        cols = slice(b * BLOCK, (b + 1) * BLOCK)
+        low = weights_t[:extent, cols]
+        dn = dnt[:, cols]
+        spread = nn(values[:extent, :], dn)
+        slopes = (low.astype(F32) * (spread + rows_f[2:3, cols])).astype(BF16)
+        block = (nn(keys_t[:, :extent], slopes) * 0.125).astype(BF16)
+        if name is None:
+            dt0[0:64, cols] = block
         else:
-            pl.loop(0, 4)(make(1024))
-        if name is not None:
-            sent_later(name, target.at[pl.ds(0, GROUP - 1)])
+            for k in range(2):
+                target[2 * b + k] = block[:, k * here : (k + 1) * here]
+                to_slot(name, target, arrives, 2 * b + k)
+            if b == 3:
+                sent_later(name, target.at[pl.ds(0, GROUP - 1)])
+        acc_k[:, :extent] += nt(queries[:, cols], slopes)
+        acc_v[:, :extent] += nt(dn, low)
 
     def by_head(target, value):
         target[...] = flip(value).astype(BF16).reshape(GROUP, 64, here)
@@ -1237,6 +1245,7 @@
     for device in greet:
         pl.semaphore_signal(barrier, inc=1, device_id=device, device_id_type=MESH)
     pl.semaphore_wait(barrier, len(greet))
+    gather_z("q")
     to_plane("m", mem, all_mem, True)
     for i, (ref, _) in enumerate(raw):
         landed("raw" + str(i), ref)
@@ -1244,102 +1253,111 @@
         for m in range(2):
             for start in (0, 64):
                 meta[m, i : i + 1, start : start + span] = ref[m]
+    gather_f("q")
     slice_1("w0", s_in.at[0], ws0)
     to_plane("meta", meta, in_meta)
+    gather_z("out0")
+    slice_1("w1", s_in.at[1, pl.ds(1, 2)], ws1)
+    to_plane("x", tok, all_tok, True)
+    gather_1("q")
+    gather_z("up0")
+    spread_1("m", all_mem, 0)
+    spread_1("m", all_mem, 1)
+    gather_z("out1")
+    gather_f("out0")
+    gather_z("dn1")
+    landed("meta", in_meta)
+    lane = lax.broadcasted_iota(jnp.int32, (8, 128), 1)
+    slice_2("w0", ws0)
+    gather_2("q")
+    all_meta[me_slot] = jnp.where(lane < 64, in_meta[0], in_meta[1])
+    spread_2("m", all_mem, 0)
+    spread_1("x", all_tok, 0)
+    spread_1("x", all_tok, 1)
+    spread_2("m", all_mem, 1)
+    gather_f("up0")
+    gather_f("out1")
+    gather_z("up1")
+    gather_3("q")
     for i, (_, ref) in enumerate(given):
         landed("given" + str(i), ref)
-    gather_z("out0")
-    slice_1("w1", s_in.at[1, pl.ds(1, 2)], ws1)
-    gather_z("out1")
+    gather_1("out0")
+    spread_2("x", all_tok, 0)
+    slice_2("w1", ws1)
+    gather_1("up0")
+    spread_4("m", all_mem, 0)
+    spread_2("x", all_tok, 1)
+    gather_2("out0")
+    gather_f("dn1")
+    for cc, yy, xx in plane_peers:
+        send("marks", all_meta.at[me_slot], all_meta.at[me_slot], (cc, at(z, yy, xx)))
+    slice_f("w0", ws0)
+    gather_z("dn0")
     for i, row in enumerate((0, 1, 4)):
         bias_cols[i] = jnp.transpose(jnp.broadcast_to(bias(row), (128, width)))
-    to_plane("x", tok, all_tok, True)
-    gather_z("up1")
-    spread_1("m", all_mem, 0)
-    gather_z("q")
-    gather_f("out0")
-    slice_2("w0", ws0)
-    spread_1("m", all_mem, 1)
-    spread_1("x", all_tok, 0)
-    gather_f("out1")
-    spread_1("x", all_tok, 1)
-    slice_2("w1", ws1)
-    spread_2("m", all_mem, 0)
+    gather_1("out1")
+    gather_2("up0")
     gather_f("up1")
-    landed("meta", in_meta)
-    gather_f("q")
-    spread_2("x", all_tok, 0)
-    slice_f("w0", ws0)
-    lane = lax.broadcasted_iota(jnp.int32, (8, 128), 1)
-    gather_z("dn0")
-    gather_z("up0")
-    gather_1("out1")
-    all_meta[me_slot] = jnp.where(lane < 64, in_meta[0], in_meta[1])
-    gather_1("out0")
+    spread_4("x", all_tok, 0)
+    slice_f("w1", ws1)
+    spread_4("x", all_tok, 1)
+    sent_later("marks", all_meta.at[pl.ds(0, 7)])
+    gather_1("dn1")
+    slice_3("w0", ws0)
+    gather_2("out1")
+    make_masks()
     gather_1("up1")
-    for cc, yy, xx in plane_peers:
-        send("marks", all_meta.at[me_slot], all_meta.at[me_slot], (cc, at(z, yy, xx)))
-    spread_2("x", all_tok, 1)
-    gather_2("out0")
-    slice_3("w0", ws0)
-    slice_f("w1", ws1)
-    sent_later("marks", all_meta.at[pl.ds(0, 7)])
+    slice_4("w0", ws0)
+    gather_3("out0")
+    heads_weights(0, ws0)
+    gather_3("up0")
+    spread_4("m", all_mem, 1)
+    gather_2("dn1")
+    spread_3("x", all_tok)
+    project_heads(all_tok, 0, qt0, k0, kt0, v0, vt0)
+    attend(0, qt0, k0, vt0, pt0, l0, ot0, True, "x3", a3, b3)
+    slice_3("w1", ws1)
     gather_f("dn0")
-    gather_1("q")
-    spread_2("m", all_mem, 1)
-    gather_2("out1")
-    gather_z("dn1")
-    make_masks()
-    gather_2("q")
+    attend(1, qt0, k0, vt0, pt0, l0, ot0, True, "x3", a3, b3)
+    attend(2, qt0, k0, vt0, pt0, l0, ot0, True, "x3", a3, b3)
+    spread_3("m", all_mem)
+    attend(3, qt0, k0, vt0, pt0, l0, ot0, True, "x3", a3, b3)
     gather_1("dn0")
-    gather_f("dn1")
-    slice_4("w0", ws0)
-    heads_weights(0, ws0)
-    slice_3("w1", ws1)
-    gather_3("out1")
-    spread_3("x", all_tok)
+    slice_4("w1", ws1)
     to_plane("cot", cot, in_cot)
     gather_2("up1")
-    project_heads(all_tok, 0, qt0, k0, kt0, v0, vt0)
-    gather_3("out0")
-    gather_1("dn1")
-    attend(qt0, k0, vt0, pt0, l0, ot0, True, "x3", a3, b3)
-    gather_3("up1")
-    gather_2("dn0")
-    gather_2("dn1")
     gathered("out0")
-    spread_3("m", all_mem)
-    gather_3("q")
     gathered("q")
+    heads_weights(3, ws1)
+    project_heads(all_mem, 3, None, k1, kt1, v1, vt1)
     landed("x3", b3)
     words_f = all_tok[me_slot].reshape(here, width).astype(F32)
-    gather_f("up0")
-    gather_3("dn0")
     branch = tn(b3[...].reshape(width, here), matrix(w_out.at[0])) + bias(2)
     h1, scale0 = norm(words_f * omega[0:1, :] + branch, 0, xh0)
     h1_f[...] = h1
-    slice_4("w1", ws1)
-    gathered("out1")
     h1_low = h1.astype(BF16)
     by_head(a4, nn(h1_low, matrix(w_q.at[0])) + bias(3))
-    gather_1("up0")
-    heads_weights(3, ws1)
-    project_heads(all_mem, 3, None, k1, kt1, v1, vt1)
     to_heads("x4", a4, b4)
     gather_3("dn1")
-    gathered("dn0")
-    gather_2("up0")
+    gather_2("dn0")
+    gathered("up0")
+    gather_3("out1")
+    gather_3("up1")
+    gathered("out1")
     landed("x4", b4)
     for s in range(GROUP):
         qt1[:, s * here : (s + 1) * here] = (b4[s].astype(F32) * 0.125).astype(BF16)
+    attend(0, qt1, k1, vt1, pt1, l1, ot1, False, "x5", a5, b5)
+    attend(1, qt1, k1, vt1, pt1, l1, ot1, False, "x5", a5, b5)
+    attend(2, qt1, k1, vt1, pt1, l1, ot1, False, "x5", a5, b5)
+    attend(3, qt1, k1, vt1, pt1, l1, ot1, False, "x5", a5, b5)
+    gather_3("dn0")
+    gathered("dn0")
     gathered("up1")
     gathered("dn1")
-    attend(qt1, k1, vt1, pt1, l1, ot1, False, "x5", a5, b5)
-    gather_3("up0")
     landed("x5", b5)
     branch = tn(b5[...].reshape(width, here), matrix(w_out.at[1])) + bias(5)
     h2, scale1 = norm(h1_f[...] * omega[1:2, :] + branch, 1, xh1)
-    gathered("up0")
     h2_f[...] = h2
     h2_low = h2.astype(BF16)
     feed_up(h2_low, 0)
@@ -1352,120 +1370,130 @@
     grad = in_cot[...].reshape(here, width).astype(F32)
     dr, skip = norm_back(grad, 2, xh2, scale2, h2_f[...])
     gf = dr.astype(BF16)
-    put(g_dn.at[0], tn(act[...], gf[:, 0:256]))
     column(6, gf.astype(F32))
-    scatter_0("dn0")
     back = feed_back(gf, skip)
-    scatter_1("dn0")
+    put(g_up.at[0], tn(h2_low, gul[:, 0:1024]))
+    scatter_0("up0")
     dr, skip = norm_back(back, 1, xh1, scale1, h1_f[...])
     gc = dr.astype(BF16)
-    put(g_up.at[0], tn(h2_low, gul[:, 0:1024]))
-    put(g_out.at[1], nn(b5[...].reshape(width, here), gc))
-    scatter_0("up0")
-    scatter_0("out1")
     column(5, gc.astype(F32))
     by_head(a6, nt(gc, matrix(w_out.at[1])))
     to_heads("x6", a6, b6)
+    put(g_up.at[1], tn(h2_low, gul[:, 1024:2048]))
+    scatter_1("up0")
+    scatter_0("up1")
     from_plane("res", out_res, o_res)
+    put(g_dn.at[0], tn(act[...], gf[:, 0:256]))
     put(g_dn.at[1], tn(act[...], gf[:, 256:512]))
-    scatter_1("up0")
+    scatter_1("up1")
+    back = skip
+    landed("x6", b6)
+    attend_start(b6, l1, ot1)
+    attend_back(0, qt1, kt1, v1, pt1, False, "x7", a7, b7)
     scatter_0("dn1")
-    scatter_2("dn0")
-    back = skip
-    put(g_up.at[1], tn(h2_low, gul[:, 1024:2048]))
-    scatter_1("out1")
-    landed("x6", b6)
-    attend_back(b6, qt1, kt1, v1, pt1, l1, ot1, False, "x7", a7, b7)
+    attend_back(1, qt1, kt1, v1, pt1, False, "x7", a7, b7)
+    attend_back(2, qt1, kt1, v1, pt1, False, "x7", a7, b7)
+    attend_back(3, qt1, kt1, v1, pt1, False, "x7", a7, b7)
+    scatter_2("up0")
     dt1[0:64, :] = acc_k[...].astype(BF16)
-    scatter_2("up0")
-    scatter_3("dn0")
     dt1[64:128, :] = acc_v[...].astype(BF16)
+    scatter_2("up1")
+    put(g_out.at[1], nn(b5[...].reshape(width, here), gc))
     rows_back(dt1, 3, dx1, 1 - c)
     merge_0("dm", dx1, dc1)
     rows_back(dt1, 3, dx1, c)
+    slices_back(dt1, all_mem, gs1)
+    unslice_0("u1", gs1, cs1)
     scatter_1("dn1")
-    slices_back(dt1, all_mem, gs1)
+    value_sums(dt1)
     landed("x7", b7)
-    scatter_2("out1")
     dq = b7[...].reshape(width, here)
-    scatter_0("up1")
     dq_row = flip(dq)
-    put(g_q.at[0], nt(flip(h1_low).astype(BF16), dq))
-    unslice_0("u1", gs1, cs1)
+    column(3, dq_row)
     scatter_3("up0")
-    value_sums(dt1)
-    column(3, dq_row)
     back = back + nt(dq_row.astype(BF16), matrix(w_q.at[0]))
     dr, skip = norm_back(back, 0, xh0, scale0, words_f)
     ga = dr.astype(BF16)
     column(2, ga.astype(F32))
+    scatter_0("out1")
+    by_head(a8, nt(ga, matrix(w_out.at[0])))
+    put(g_q.at[0], nt(flip(h1_low).astype(BF16), dq))
+    to_heads("x8", a8, b8)
+    scatter_0("q")
+    merge_1("dm", dx1, dc1, dp1)
+    put(g_out.at[0], nn(b3[...].reshape(width, here), ga))
+    scatter_3("up1")
     small("s0", sg0, sr0, core_next)
-    by_head(a8, nt(ga, matrix(w_out.at[0])))
-    to_heads("x8", a8, b8)
+    scatter_0("out0")
+    scatter_0("dn0")
     scatter_2("dn1")
-    put(g_out.at[0], nn(b3[...].reshape(width, here), ga))
-    scatter_0("out0")
-    scatter_3("out1")
-    last = skip
-    scatter_1("up1")
     unslice_1("u1", gs1, cs1, zs1)
     small_add("s0", sr0, sg0, sg1)
-    landed("x8", b8)
-    scatter_0("q")
     scatter_1("out0")
     small("s1", sg1, sr1, y_next)
-    attend_back(b8, qt0, kt0, v0, pt0, l0, ot0, True, None, None, None)
-    scattered("dn0")
+    last = skip
+    landed("x8", b8)
+    attend_start(b8, l0, ot0)
+    attend_back(0, qt0, kt0, v0, pt0, True, None, None, None)
+    attend_back(1, qt0, kt0, v0, pt0, True, None, None, None)
+    merge_3("dm", dx1, dp1)
+    attend_back(2, qt0, kt0, v0, pt0, True, None, None, None)
+    scatter_3("dn1")
+    attend_back(3, qt0, kt0, v0, pt0, True, None, None, None)
     dt0[64:128, :] = acc_k[...].astype(BF16)
-    scatter_1("q")
-    scatter_3("dn1")
     dt0[128:192, :] = acc_v[...].astype(BF16)
     slices_back(dt0, all_tok, gs0)
     unslice_0("u0", gs0, cs0)
+    scattered("up0")
     rows_back(dt0, 0, dx0, 1 - c)
-    landed("res", o_res)
-    scatter_2("up1")
+    small_add("s1", sr1, sg1, sg2)
+    small("s2", sg2, sr2, x_next)
     head_sums(dt0)
-    small_add("s1", sr1, sg1, sg2)
+    scatter_1("q")
     unslice_1("u0", gs0, cs0, zs0)
-    small("s2", sg2, sr2, x_next)
+    merge_0("dx", dx0, dc0)
+    scatter_1("dn0")
+    scatter_1("out1")
+    rows_back(dt0, 0, dx0, c)
     small("t0", tg0, tr0, core_next)
-    merge_0("dx", dx0, dc0)
-    scatter_2("q")
     small_add("t0", tr0, tg0, tg1)
     scatter_2("out0")
-    scattered("up0")
-    rows_back(dt0, 0, dx0, c)
     small("t1", tg1, tr1, y_next)
-    merge_1("dm", dx1, dc1, dp1)
     merge_1("dx", dx0, dc0, dp0)
-    scatter_3("out0")
-    scatter_3("up1")
-    scatter_3("q")
     small_add("s2", sr2, sg2, sg3)
     small_z("s3", sg3, sr3)
-    scattered("up1")
+    scatter_2("q")
     out_mem[...] = merge_2("dm", dx1, dp1).astype(BF16).reshape(2, 64, width)
     from_plane("gmem", out_mem, o_mem)
+    scatter_2("dn0")
+    small_add("t1", tr1, tg1, tg2)
+    scatter_2("out1")
+    unslice_2("u1", gs1, zs1, fs1, o_in.at[1, pl.ds(1, 2)])
+    scatter_3("out0")
+    small("t2", tg2, tr2, x_next)
+    merge_3("dx", dx0, dp0)
+    scatter_3("dn0")
+    scatter_3("q")
+    scatter_3("out1")
+    unslice_3("u1", o_in.at[1, pl.ds(1, 2)])
+    scattered("out0")
+    out_tok[...] = (merge_2("dx", dx0, dp0) + last).astype(BF16).reshape(2, 64, width)
     unslice_2("u0", gs0, zs0, fs0, o_in.at[0])
+    small_add("t2", tr2, tg2, tg3)
+    scattered("up1")
+    small_z("t3", tg3, tr3)
+    landed("res", o_res)
+    from_plane("gtok", out_tok, o_tok)
     scattered("dn1")
+    scattered("dn0")
+    unslice_3("u0", o_in.at[0])
+    landed("gmem", o_mem)
+    scattered("out1")
     keep("e3", o_dn, h_dn)
-    small_add("t1", tr1, tg1, tg2)
-    small("t2", tg2, tr2, x_next)
-    unslice_2("u1", gs1, zs1, fs1, o_in.at[1, pl.ds(1, 2)])
-    small_add("t2", tr2, tg2, tg3)
-    small_z("t3", tg3, tr3)
-    out_tok[...] = (merge_2("dx", dx0, dp0) + last).astype(BF16).reshape(2, 64, width)
-    from_plane("gtok", out_tok, o_tok)
     small_out()
-    scattered("out0")
-    landed("gmem", o_mem)
     keep("e2", o_up, h_up)
-    unslice_3("u0", o_in.at[0])
-    scattered("out1")
     keep("e1", o_out, h_out)
     scattered("q")
-    unslice_3("u1", o_in.at[1, pl.ds(1, 2)])
     keep("e0", o_in, h_in)
     landed("gtok", o_tok)
     for i, ref in enumerate((h_in, h_out, h_up, h_dn, h_bias, h_upb, h_gain_o, h_shift_o, h_omega_o)):
@@ -1547,7 +1575,7 @@
     scratch += [low(64, 1024)] + [full(64, 1024)] * 2
     scratch += [low(128, 2048), full(128, 2048), low(128, 2048)] + [full(128, 512)] * 5
     scratch += [low(5, 128, 512), full(3, 512, 128), full(3, 128, 512), low(192, 1024), low(128, 1024), low(2048, 512)]
-    scratch += [pltpu.SemaphoreType.DMA((36,)), pltpu.SemaphoreType.DMA((NAMES,))]
+    scratch += [pltpu.SemaphoreType.DMA((40,)), pltpu.SemaphoreType.DMA((NAMES,))]
     rows = jax.ShapeDtypeStruct((2, 64, 512), BF16)
 
     def wide_out(*shape):

time: 114 us -> 107 us (0.939)
  Pallas kernels: 113 us -> 106 us
    pallas_call x1, Pallas kernels: 110 us -> 104 us  [fused_local(): pl.pallas_call(fused_kernel, name='layer', out_shape=(rows, rows, rows, *...]
where the time goes in v5:
time: 107 us
  Pallas kernels  106 us (99%)
    pallas_call x1, Pallas kernels, fused_local(): pl.pallas_call(fused_kernel, name='layer', out_shape=(rows, rows, rows, *...  104 us
    pallas_call x1, Pallas kernels, fused_local(): pl.pallas_call(copy_kernel, name='hand_over', out_shape=tuple((jax.ShapeD...  2.23 us

profile of v5, /device:TPU:0, one launch (start us, length us, event | category | flops | bytes accessed | tf_op | source)
XLA Modules:
  0.0 107.3 jit_solution(80662455247532021)
XLA Ops:
  0.7 104.3 %layer.1 = (bf16[2,64,512]{2,1,0:T(8,128)(2,1)}, bf16[2,64,512]{2,1,0:T(8,128)(2,1)}, bf16[2,64,512]{2,1,0:T(8,128)(2,1)}, f32[2,3,16,512]{3,2,1,0:T(8,128)}, f3...) custom-call(bf16[2,64,512]{2,1,0:T(8,128)(2,1)} %bitcast.24, ...), custom_call_target="tpu_custom_call" | custom-call | tf_op jit(solution)/shard_map/layer/pallas_call | solution.py:1584
  104.9 2.2 %hand_over.1 = (bf16[2,64,512]{2,1,0:T(8,128)(2,1)}, bf16[2,64,512]{2,1,0:T(8,128)(2,1)}, bf16[2,64,512]{2,1,0:T(8,128)(2,1)}, f32[2,3,16,512]{3,2,1,0:T(8,128)}...) custom-call(bf16[2,64,512]{2,1,0:T(8,128)(2,1)} %get-tuple-element.3, ...), custom_call_target="tpu_custom_call" | custom-call | tf_op jit(solution)/shard_map/hand_over/pallas_call | solution.py:1598

commit v6 on v5

--- a/solution.py
+++ b/solution.py
@@ -516,7 +516,7 @@
 UNIT = 16 * 1024
 BINS = 16
 NAMES = 192
-ODD = ("marks", "w0p", "w1p", "u0p", "x3", "x5", "x7")
+ODD = ("marks", "w0p", "w1p", "u0p", "x3", "x5", "x7", "sa", "sb", "ta")
 F32 = jnp.float32
 BF16 = jnp.bfloat16
 PLANES, YS, XS, CORES = 4, 2, 2, 2
@@ -553,14 +553,15 @@
     dx0, dx1, dc0, dc1, dp0, dp1,
     a3, b3, a4, b4, a5, b5, a6, b6, a7, b7, a8, b8,
     out_res, out_tok, out_mem,
-    sg0, sg1, sg2, sg3, sg4, sr0, sr1, sr2, sr3,
-    tg0, tg1, tg2, tg3, tr0, tr1, tr2, tr3,
+    sg0, sg1, sg2, sg3, sr0, sr1, sr2, sra, srb,
+    tg0, tg1, tg2, tg3, tr0, tr1, tr2, tra,
     code_self, code_cross, key_pos, rows_f,
     qt0, kt0, vt0, k0, v0, pt0, l0, ot0,
     qt1, kt1, vt1, k1, v1, pt1, l1, ot1,
     dnt, acc_k, acc_v,
     act, slope, gul, xh0, xh1, xh2, h1_f, h2_f,
     wt, bias_cols, wz, dt0, dt1, gauge,
+    f_q, f_out, f_up, f_dn, f_u0, f_u1,
     ss, rs,
 ):
     c = lax.axis_index("rows")
@@ -659,6 +660,57 @@
                     src_ref=block(origin), dst_ref=block(origin), send_sem=ss.at[BINS], recv_sem=rs.at[sem(name + "z")],
                     device_id=(c, at(to, y, x)), device_id_type=MESH,
                 ).start()
+
+    fold_bytes = [0]
+
+    def fold_send(name, block, target, to):
+        pltpu.make_async_remote_copy(
+            src_ref=block, dst_ref=target, send_sem=ss.at[BINS], recv_sem=rs.at[sem(name)],
+            device_id=(c, at(to, y, x)), device_id_type=MESH,
+        ).start()
+
+    def fold_z(name, block, far, line):
+        inner = jnp.where(edge, 0, 1)
+        for origin, step, hops in ((0, 3, 1), (3, -3, -1)):
+
+            @pl.when(z == origin)
+            def _():
+                fold_send(name + "a", block(origin + step), far, origin + hops)
+                fold_send(name + "l", block(origin + 2 * hops), line.at[2], origin + 2 * hops)
+
+        for step in (1, -1):
+            to = z + step
+
+            @pl.when((to >= 0) & (to < PLANES))
+            def _():
+                between = jnp.where((to == 0) | (to == PLANES - 1), 0, inner)
+                fold_send(name + "l", block(to), line.at[between], to)
+
+        fold_bytes[0] += size(far)
+
+    def fold_f(name, block, far, line):
+        for mine, to in ((1, 3), (2, 0)):
+
+            @pl.when(z == mine)
+            def _():
+                landed(name + "a", far)
+                add(block(to), far)
+                fold_send(name + "l", block(to), line.at[1], to)
+
+    def fold_sum(name, own, line, result):
+        @pl.when(edge)
+        def _():
+            landed(name + "l", line.at[pl.ds(0, 2)])
+
+        @pl.when(jnp.logical_not(edge))
+        def _():
+            landed(name + "l", line)
+
+        result[...] = own.astype(F32) + line[0].astype(F32) + line[1].astype(F32)
+
+        @pl.when(jnp.logical_not(edge))
+        def _():
+            result[...] += line[2].astype(F32)
 
     def line_landed(name, blocks, own):
         @pl.when(edge)
@@ -765,6 +817,11 @@
             for ref in refs
         )
 
+    fars = {"q": f_q, "u0": f_u0, "u1": f_u1}
+    for i in range(2):
+        one = pl.ds(i, 1)
+        fars["out" + str(i)], fars["up" + str(i)], fars["dn" + str(i)] = f_out.at[one], f_up.at[one], f_dn.at[one]
+
     def halves(ref):
         cols = ref.shape[-1] // 2
         return pl.ds(0, cols), pl.ds(cols, cols)
@@ -866,17 +923,15 @@
                 add(grad.at[lead, c, zz, y, x, :, first], piece.at[0, lead, zz])
                 add(grad.at[lead, c, zz, y, x, :, second], piece.at[1, lead, zz])
 
-        for k in range(3):
-            send(g + "r3", grad.at[:, c, z_peers[k], y, x], line.at[2 - k], (c, at(z_peers[k], y, x)))
-        sent_later(g + "r3", line)
+        fold_z(g, lambda zz: grad.at[:, c, zz, y, x], fars[g], line)
+
+    def scatter_f(g):
+        grad, line = weights[g][2], weights[g][6]
+        fold_f(g, lambda zz: grad.at[:, c, zz, y, x], fars[g], line)
 
     def scattered(g):
         grad, _, _, _, line, result = weights[g][2:8]
-        landed(g + "r3", line)
-        total = grad[:, c, z, y, x].astype(F32)
-        for k in range(3):
-            total = total + line[k].astype(F32)
-        result[...] = total
+        fold_sum(g, grad[:, c, z, y, x], line, result)
 
     left, right = pl.ds(0, 256), pl.ds(256, 256)
     y_slot, x_slot, far_slot = slot(c, 1 - y, x), slot(c, y, 1 - x), slot(c, 1 - y, 1 - x)
@@ -974,16 +1029,13 @@
         landed(name + "c", across)
         for lead in range(grad.shape[0]):
             add(grad.at[lead, c], across.at[lead])
-        for k in range(3):
-            send(name + "z", grad.at[:, c, z_peers[k]], line.at[2 - k], (c, at(z_peers[k], y, x)))
-        sent_later(name + "z", line)
+        fold_z(name, lambda zz: grad.at[:, c, zz], fars[name], line)
+
+    def unslice_f(name, grad, line):
+        fold_f(name, lambda zz: grad.at[:, c, zz], fars[name], line)
 
     def unslice_2(name, grad, line, total, result):
-        landed(name + "z", line)
-        value = grad[:, c, z].astype(F32)
-        for k in range(3):
-            value = value + line[k].astype(F32)
-        total[...] = value
+        fold_sum(name, grad[:, c, z], line, total)
         for yy, xx in trio:
             send(name + "p", total.at[:, yy * 2 + xx], result.at[:, :, tile(yx)], (c, at(z, yy, xx)))
         sent_later(name + "p", total.at[:, pl.ds(0, 3)])
@@ -1010,12 +1062,12 @@
 
     def norm_back(grad, i, kept, scale, skip):
         xhat = kept[...]
-        column(11 + i, grad * xhat)
-        column(14 + i, grad)
+        column(12 + i, grad * xhat)
+        column(15 + i, grad)
         dxhat = grad * gain[i : i + 1, :]
         dr = dxhat - jnp.mean(dxhat, axis=1, keepdims=True)
         dr = (dr - xhat * jnp.mean(dxhat * xhat, axis=1, keepdims=True)) * scale
-        column(17 + i, dr * skip)
+        column(18 + i, dr * skip)
         return dr, dr * omega[i : i + 1, :]
 
     BLOCK = 256
@@ -1179,7 +1231,7 @@
             gu = gu + nt(gf[:, 256:512], matrix(w_dn.at[1, k // 2, rows]))
             gu = (gu * slope[:, cols]).astype(BF16)
             gul[:, cols] = gu
-            column(7 + k, gu.astype(F32))
+            column(8 + k, gu.astype(F32))
             back = back + nt(gu, matrix(w_up.at[k // 2, :, :, :, :, :, inner]))
         return back
 
@@ -1205,29 +1257,36 @@
         landed(name, arrived)
         total[...] = mine[...] + arrived[...]
 
-    def small_z(name, src, dst):
-        for k in range(3):
-            send(name, src, dst.at[2 - k], (c, at(z_peers[k], y, x)))
+    def small_z(name, src, rows, tile_at, dst):
+        for k, zz in enumerate(z_peers):
+            send(name, src.at[rows, tile(tile_at(zz))], dst.at[2 - k], (c, at(zz, y, x)))
         sent_later(name, dst)
 
+    def tile_own(zz):
+        return c * 2 + zz // 2
+
+    def tile_up(zz):
+        return lax.rem(zz, 2) * 2 + y
+
+    def small_sum(name, src, rows, tile_at, dst):
+        landed(name, dst)
+        return src[rows, tile(tile_at(z))] + dst[0] + dst[1] + dst[2]
+
     def small_out():
-        landed("s3", sr3)
-        sg4[...] = sg3[...] + sr3[0] + sr3[1] + sr3[2]
-        landed("t3", tr3)
-        sg4[0:2, :] = (tg3[...] + tr3[0] + tr3[1] + tr3[2])[0:2, :]
         block = c * 16 + seq
-        tile_of = sg4[:, pl.ds(pl.multiple_of((block // 8) * 128, 128), 128)]
-        turned = pltpu.roll(tile_of, lax.rem(128 - lax.rem(block, 8) * 16, 128), 1)
+        shift_by = lax.rem(128 - lax.rem(block, 8) * 16, 128)
+        turned = pltpu.roll(small_sum("sa", sg3, slice(None), tile_own, sra), shift_by, 1)
         o_bias[...] = turned[0:7, 0:16]
-        o_gain[...] = turned[11:14, 0:16]
-        o_shift[...] = turned[14:17, 0:16]
-        o_omega[...] = turned[17:20, 0:16]
-        tile_of = sg4[:, pl.ds(pl.multiple_of((lax.rem(block, 8) // 2) * 128, 128), 128)]
-        turned = pltpu.roll(tile_of, lax.rem(block, 2) * 64, 1)
+        o_gain[...] = turned[12:15, 0:16]
+        o_shift[...] = turned[15:18, 0:16]
+        o_omega[...] = turned[18:21, 0:16]
+        turned = pltpu.roll(small_sum("ta", tg3, slice(None), tile_own, tra), shift_by, 1)
+        o_bias[0:2, :] = turned[0:2, 0:16]
+        turned = pltpu.roll(small_sum("sb", sg3, pl.ds(8, 8), tile_up, srb), lax.rem(block, 2) * 64, 1)
         wanted = block // 8
         row = jnp.zeros((1, 64), F32)
         for k in range(4):
-            row = row + turned[7 + k : 8 + k, 0:64] * (wanted == k).astype(F32)
+            row = row + turned[k : k + 1, 0:64] * (wanted == k).astype(F32)
         o_upb[...] = row
         ends = ((o_bias, h_bias), (o_upb, h_upb), (o_gain, h_gain_o), (o_shift, h_shift_o), (o_omega, h_omega_o))
         for i, (src, dst) in enumerate(ends):
@@ -1245,7 +1304,11 @@
     for device in greet:
         pl.semaphore_signal(barrier, inc=1, device_id=device, device_id_type=MESH)
     pl.semaphore_wait(barrier, len(greet))
-    gather_z("q")
+    to_plane("x", tok, all_tok, True)
+    slice_1("w1", s_in.at[1, pl.ds(1, 2)], ws1)
+    slice_1("w0", s_in.at[0], ws0)
+    for i, (_, ref) in enumerate(given):
+        landed("given" + str(i), ref)
     to_plane("m", mem, all_mem, True)
     for i, (ref, _) in enumerate(raw):
         landed("raw" + str(i), ref)
@@ -1253,108 +1316,104 @@
         for m in range(2):
             for start in (0, 64):
                 meta[m, i : i + 1, start : start + span] = ref[m]
-    gather_f("q")
-    slice_1("w0", s_in.at[0], ws0)
+    gather_z("q")
+    spread_1("x", all_tok, 0)
+    spread_1("x", all_tok, 1)
+    gather_z("out0")
     to_plane("meta", meta, in_meta)
-    gather_z("out0")
-    slice_1("w1", s_in.at[1, pl.ds(1, 2)], ws1)
-    to_plane("x", tok, all_tok, True)
-    gather_1("q")
-    gather_z("up0")
+    gather_z("dn0")
     spread_1("m", all_mem, 0)
+    gather_z("out1")
     spread_1("m", all_mem, 1)
-    gather_z("out1")
-    gather_f("out0")
-    gather_z("dn1")
+    spread_2("x", all_tok, 0)
+    slice_2("w0", ws0)
     landed("meta", in_meta)
     lane = lax.broadcasted_iota(jnp.int32, (8, 128), 1)
-    slice_2("w0", ws0)
-    gather_2("q")
+    gather_f("q")
     all_meta[me_slot] = jnp.where(lane < 64, in_meta[0], in_meta[1])
-    spread_2("m", all_mem, 0)
-    spread_1("x", all_tok, 0)
-    spread_1("x", all_tok, 1)
-    spread_2("m", all_mem, 1)
-    gather_f("up0")
-    gather_f("out1")
-    gather_z("up1")
-    gather_3("q")
-    for i, (_, ref) in enumerate(given):
-        landed("given" + str(i), ref)
-    gather_1("out0")
-    spread_2("x", all_tok, 0)
-    slice_2("w1", ws1)
-    gather_1("up0")
-    spread_4("m", all_mem, 0)
-    spread_2("x", all_tok, 1)
-    gather_2("out0")
-    gather_f("dn1")
+    gather_f("out0")
     for cc, yy, xx in plane_peers:
         send("marks", all_meta.at[me_slot], all_meta.at[me_slot], (cc, at(z, yy, xx)))
-    slice_f("w0", ws0)
-    gather_z("dn0")
+    sent_later("marks", all_meta.at[pl.ds(0, 7)])
+    spread_2("m", all_mem, 0)
+    spread_2("m", all_mem, 1)
+    gather_f("dn0")
+    gather_z("up1")
+    spread_2("x", all_tok, 1)
     for i, row in enumerate((0, 1, 4)):
         bias_cols[i] = jnp.transpose(jnp.broadcast_to(bias(row), (128, width)))
+    gather_z("dn1")
+    gather_1("q")
+    gather_1("out0")
+    gather_1("dn0")
+    gather_2("q")
+    spread_4("x", all_tok, 0)
+    spread_4("m", all_mem, 0)
+    gather_2("out0")
+    slice_f("w0", ws0)
+    make_masks()
+    gather_f("out1")
+    gather_2("dn0")
+    gather_f("up1")
+    slice_3("w0", ws0)
+    spread_4("x", all_tok, 1)
+    gather_z("up0")
+    gather_f("dn1")
+    spread_4("m", all_mem, 1)
+    to_plane("cot", cot, in_cot)
+    gather_3("q")
+    gather_1("up1")
+    spread_3("x", all_tok)
+    slice_4("w0", ws0)
+    slice_2("w1", ws1)
+    gather_3("out0")
     gather_1("out1")
-    gather_2("up0")
-    gather_f("up1")
-    spread_4("x", all_tok, 0)
-    slice_f("w1", ws1)
-    spread_4("x", all_tok, 1)
-    sent_later("marks", all_meta.at[pl.ds(0, 7)])
+    heads_weights(0, ws0)
+    project_heads(all_tok, 0, qt0, k0, kt0, v0, vt0)
     gather_1("dn1")
-    slice_3("w0", ws0)
-    gather_2("out1")
-    make_masks()
-    gather_1("up1")
-    slice_4("w0", ws0)
-    gather_3("out0")
-    heads_weights(0, ws0)
-    gather_3("up0")
-    spread_4("m", all_mem, 1)
-    gather_2("dn1")
-    spread_3("x", all_tok)
-    project_heads(all_tok, 0, qt0, k0, kt0, v0, vt0)
+    gather_f("up0")
+    gathered("out0")
     attend(0, qt0, k0, vt0, pt0, l0, ot0, True, "x3", a3, b3)
-    slice_3("w1", ws1)
-    gather_f("dn0")
+    gather_2("up1")
     attend(1, qt0, k0, vt0, pt0, l0, ot0, True, "x3", a3, b3)
     attend(2, qt0, k0, vt0, pt0, l0, ot0, True, "x3", a3, b3)
+    attend(3, qt0, k0, vt0, pt0, l0, ot0, True, "x3", a3, b3)
+    slice_f("w1", ws1)
+    gather_2("dn1")
+    gather_1("up0")
+    landed("x3", b3)
+    gathered("q")
+    words_f = all_tok[me_slot].reshape(here, width).astype(F32)
     spread_3("m", all_mem)
-    attend(3, qt0, k0, vt0, pt0, l0, ot0, True, "x3", a3, b3)
-    gather_1("dn0")
-    slice_4("w1", ws1)
-    to_plane("cot", cot, in_cot)
-    gather_2("up1")
-    gathered("out0")
-    gathered("q")
-    heads_weights(3, ws1)
-    project_heads(all_mem, 3, None, k1, kt1, v1, vt1)
-    landed("x3", b3)
-    words_f = all_tok[me_slot].reshape(here, width).astype(F32)
+    gather_3("dn0")
     branch = tn(b3[...].reshape(width, here), matrix(w_out.at[0])) + bias(2)
     h1, scale0 = norm(words_f * omega[0:1, :] + branch, 0, xh0)
     h1_f[...] = h1
     h1_low = h1.astype(BF16)
     by_head(a4, nn(h1_low, matrix(w_q.at[0])) + bias(3))
+    slice_3("w1", ws1)
     to_heads("x4", a4, b4)
-    gather_3("dn1")
-    gather_2("dn0")
-    gathered("up0")
-    gather_3("out1")
+    gather_2("out1")
+    slice_4("w1", ws1)
     gather_3("up1")
-    gathered("out1")
+    gather_2("up0")
+    heads_weights(3, ws1)
+    project_heads(all_mem, 3, None, k1, kt1, v1, vt1)
+    gathered("up1")
     landed("x4", b4)
     for s in range(GROUP):
         qt1[:, s * here : (s + 1) * here] = (b4[s].astype(F32) * 0.125).astype(BF16)
     attend(0, qt1, k1, vt1, pt1, l1, ot1, False, "x5", a5, b5)
+    gather_3("dn1")
+    gather_3("out1")
     attend(1, qt1, k1, vt1, pt1, l1, ot1, False, "x5", a5, b5)
     attend(2, qt1, k1, vt1, pt1, l1, ot1, False, "x5", a5, b5)
     attend(3, qt1, k1, vt1, pt1, l1, ot1, False, "x5", a5, b5)
-    gather_3("dn0")
+    gather_3("up0")
+    gathered("dn1")
+    gathered("up0")
     gathered("dn0")
-    gathered("up1")
-    gathered("dn1")
+    gathered("out1")
     landed("x5", b5)
     branch = tn(b5[...].reshape(width, here), matrix(w_out.at[1])) + bias(5)
     h2, scale1 = norm(h1_f[...] * omega[1:2, :] + branch, 1, xh1)
@@ -1370,130 +1429,140 @@
     grad = in_cot[...].reshape(here, width).astype(F32)
     dr, skip = norm_back(grad, 2, xh2, scale2, h2_f[...])
     gf = dr.astype(BF16)
+    put(g_dn.at[0], tn(act[...], gf[:, 0:256]))
+    scatter_0("dn0")
     column(6, gf.astype(F32))
     back = feed_back(gf, skip)
-    put(g_up.at[0], tn(h2_low, gul[:, 0:1024]))
-    scatter_0("up0")
     dr, skip = norm_back(back, 1, xh1, scale1, h1_f[...])
     gc = dr.astype(BF16)
     column(5, gc.astype(F32))
     by_head(a6, nt(gc, matrix(w_out.at[1])))
     to_heads("x6", a6, b6)
+    scatter_1("dn0")
+    put(g_up.at[0], tn(h2_low, gul[:, 0:1024]))
+    scatter_0("up0")
     put(g_up.at[1], tn(h2_low, gul[:, 1024:2048]))
     scatter_1("up0")
     scatter_0("up1")
-    from_plane("res", out_res, o_res)
-    put(g_dn.at[0], tn(act[...], gf[:, 0:256]))
-    put(g_dn.at[1], tn(act[...], gf[:, 256:512]))
-    scatter_1("up1")
     back = skip
     landed("x6", b6)
     attend_start(b6, l1, ot1)
     attend_back(0, qt1, kt1, v1, pt1, False, "x7", a7, b7)
-    scatter_0("dn1")
     attend_back(1, qt1, kt1, v1, pt1, False, "x7", a7, b7)
     attend_back(2, qt1, kt1, v1, pt1, False, "x7", a7, b7)
     attend_back(3, qt1, kt1, v1, pt1, False, "x7", a7, b7)
-    scatter_2("up0")
+    put(g_dn.at[1], tn(act[...], gf[:, 256:512]))
+    scatter_2("dn0")
+    scatter_1("up1")
     dt1[0:64, :] = acc_k[...].astype(BF16)
     dt1[64:128, :] = acc_v[...].astype(BF16)
-    scatter_2("up1")
-    put(g_out.at[1], nn(b5[...].reshape(width, here), gc))
     rows_back(dt1, 3, dx1, 1 - c)
+    scatter_2("up0")
     merge_0("dm", dx1, dc1)
     rows_back(dt1, 3, dx1, c)
     slices_back(dt1, all_mem, gs1)
-    unslice_0("u1", gs1, cs1)
-    scatter_1("dn1")
-    value_sums(dt1)
     landed("x7", b7)
+    put(g_out.at[1], nn(b5[...].reshape(width, here), gc))
+    scatter_0("dn1")
+    scatter_3("dn0")
+    from_plane("res", out_res, o_res)
     dq = b7[...].reshape(width, here)
     dq_row = flip(dq)
     column(3, dq_row)
-    scatter_3("up0")
     back = back + nt(dq_row.astype(BF16), matrix(w_q.at[0]))
     dr, skip = norm_back(back, 0, xh0, scale0, words_f)
+    value_sums(dt1)
     ga = dr.astype(BF16)
+    unslice_0("u1", gs1, cs1)
     column(2, ga.astype(F32))
-    scatter_0("out1")
+    small("s0", sg0, sr0, core_next)
     by_head(a8, nt(ga, matrix(w_out.at[0])))
     put(g_q.at[0], nt(flip(h1_low).astype(BF16), dq))
     to_heads("x8", a8, b8)
+    small_add("s0", sr0, sg0, sg1)
+    small("s1", sg1, sr1, y_next)
     scatter_0("q")
-    merge_1("dm", dx1, dc1, dp1)
+    scatter_0("out1")
     put(g_out.at[0], nn(b3[...].reshape(width, here), ga))
-    scatter_3("up1")
-    small("s0", sg0, sr0, core_next)
-    scatter_0("out0")
-    scatter_0("dn0")
-    scatter_2("dn1")
-    unslice_1("u1", gs1, cs1, zs1)
-    small_add("s0", sr0, sg0, sg1)
-    scatter_1("out0")
-    small("s1", sg1, sr1, y_next)
+    scatter_2("up1")
     last = skip
+    scatter_1("dn1")
+    scatter_f("dn0")
+    scatter_3("up0")
     landed("x8", b8)
     attend_start(b8, l0, ot0)
+    scatter_0("out0")
     attend_back(0, qt0, kt0, v0, pt0, True, None, None, None)
+    unslice_1("u1", gs1, cs1, zs1)
+    merge_1("dm", dx1, dc1, dp1)
     attend_back(1, qt0, kt0, v0, pt0, True, None, None, None)
-    merge_3("dm", dx1, dp1)
+    small_add("s1", sr1, sg1, sg2)
+    scatter_f("up0")
+    small("s2", sg2, sr2, x_next)
     attend_back(2, qt0, kt0, v0, pt0, True, None, None, None)
-    scatter_3("dn1")
     attend_back(3, qt0, kt0, v0, pt0, True, None, None, None)
+    scatter_1("out1")
+    scatter_3("up1")
+    scattered("dn0")
+    unslice_f("u1", gs1, zs1)
     dt0[64:128, :] = acc_k[...].astype(BF16)
+    scatter_1("q")
     dt0[128:192, :] = acc_v[...].astype(BF16)
     slices_back(dt0, all_tok, gs0)
+    rows_back(dt0, 0, dx0, 1 - c)
     unslice_0("u0", gs0, cs0)
+    head_sums(dt0)
+    scatter_2("dn1")
+    merge_3("dm", dx1, dp1)
+    small("t0", tg0, tr0, core_next)
+    unslice_1("u0", gs0, cs0, zs0)
+    small_add("s2", sr2, sg2, sg3)
+    scatter_f("up1")
+    merge_0("dx", dx0, dc0)
+    scatter_2("out1")
+    small_z("sa", sg3, slice(None), tile_own, sra)
+    small_z("sb", sg3, pl.ds(8, 8), tile_up, srb)
+    small_add("t0", tr0, tg0, tg1)
+    scatter_3("dn1")
+    small("t1", tg1, tr1, y_next)
+    rows_back(dt0, 0, dx0, c)
     scattered("up0")
-    rows_back(dt0, 0, dx0, 1 - c)
-    small_add("s1", sr1, sg1, sg2)
-    small("s2", sg2, sr2, x_next)
-    head_sums(dt0)
-    scatter_1("q")
-    unslice_1("u0", gs0, cs0, zs0)
-    merge_0("dx", dx0, dc0)
-    scatter_1("dn0")
-    scatter_1("out1")
-    rows_back(dt0, 0, dx0, c)
-    small("t0", tg0, tr0, core_next)
-    small_add("t0", tr0, tg0, tg1)
-    scatter_2("out0")
-    small("t1", tg1, tr1, y_next)
+    scatter_1("out0")
     merge_1("dx", dx0, dc0, dp0)
-    small_add("s2", sr2, sg2, sg3)
-    small_z("s3", sg3, sr3)
     scatter_2("q")
     out_mem[...] = merge_2("dm", dx1, dp1).astype(BF16).reshape(2, 64, width)
     from_plane("gmem", out_mem, o_mem)
-    scatter_2("dn0")
     small_add("t1", tr1, tg1, tg2)
-    scatter_2("out1")
+    small("t2", tg2, tr2, x_next)
+    scatter_f("dn1")
+    scatter_3("out1")
+    scatter_2("out0")
+    merge_3("dx", dx0, dp0)
+    unslice_f("u0", gs0, zs0)
+    scatter_3("q")
+    small_add("t2", tr2, tg2, tg3)
+    scatter_3("out0")
+    scattered("dn1")
+    landed("res", o_res)
     unslice_2("u1", gs1, zs1, fs1, o_in.at[1, pl.ds(1, 2)])
-    scatter_3("out0")
-    small("t2", tg2, tr2, x_next)
-    merge_3("dx", dx0, dp0)
-    scatter_3("dn0")
-    scatter_3("q")
-    scatter_3("out1")
+    scatter_f("q")
+    scatter_f("out1")
+    small_z("ta", tg3, slice(None), tile_own, tra)
+    unslice_2("u0", gs0, zs0, fs0, o_in.at[0])
+    keep("e3", o_dn, h_dn)
+    scatter_f("out0")
+    out_tok[...] = (merge_2("dx", dx0, dp0) + last).astype(BF16).reshape(2, 64, width)
+    from_plane("gtok", out_tok, o_tok)
+    landed("gmem", o_mem)
+    small_out()
+    scattered("up1")
     unslice_3("u1", o_in.at[1, pl.ds(1, 2)])
+    scattered("out1")
+    scattered("q")
+    keep("e2", o_up, h_up)
     scattered("out0")
-    out_tok[...] = (merge_2("dx", dx0, dp0) + last).astype(BF16).reshape(2, 64, width)
-    unslice_2("u0", gs0, zs0, fs0, o_in.at[0])
-    small_add("t2", tr2, tg2, tg3)
-    scattered("up1")
-    small_z("t3", tg3, tr3)
-    landed("res", o_res)
-    from_plane("gtok", out_tok, o_tok)
-    scattered("dn1")
-    scattered("dn0")
+    keep("e1", o_out, h_out)
     unslice_3("u0", o_in.at[0])
-    landed("gmem", o_mem)
-    scattered("out1")
-    keep("e3", o_dn, h_dn)
-    small_out()
-    keep("e2", o_up, h_up)
-    keep("e1", o_out, h_out)
-    scattered("q")
     keep("e0", o_in, h_in)
     landed("gtok", o_tok)
     for i, ref in enumerate((h_in, h_out, h_up, h_dn, h_bias, h_upb, h_gain_o, h_shift_o, h_omega_o)):
@@ -1510,16 +1579,16 @@
     for i, total in enumerate(bins):
         if total:
             wait(ss.at[i], gauge.at[pl.ds(0, total // 1024)])
-    units = line_bytes[0] // UNIT
-    assert line_bytes[0] % UNIT == 0
+    spans = [2 * line_bytes[0] + 3 * fold_bytes[0], 4 * line_bytes[0] + 3 * fold_bytes[0]]
+    assert spans[0] % UNIT == 0 and spans[1] % UNIT == 0
 
     @pl.when(edge)
     def _():
-        wait(ss.at[BINS], gauge.at[pl.ds(0, 2 * units * 16)])
+        wait(ss.at[BINS], gauge.at[pl.ds(0, spans[0] // 1024)])
 
     @pl.when(jnp.logical_not(edge))
     def _():
-        wait(ss.at[BINS], gauge.at[pl.ds(0, 4 * units * 16)])
+        wait(ss.at[BINS], gauge.at[pl.ds(0, spans[1] // 1024)])
 
     assert len(names) <= NAMES and len(bins) <= BINS and BINS + 1 + len(odd) <= ss.shape[0]
 
@@ -1568,14 +1637,15 @@
     scratch += [low(GROUP, 2, 64, 512)] * 2 + [local_rows] + marks + [pltpu.VMEM((GROUP, 8, 128), jnp.int32)]
     scratch += [low(GROUP, 2, 64, 512)] * 2 + [low(4, 2, 64, 512)] * 2 + [low(3, 2, 64, 512)] * 2
     scratch += [low(GROUP, 64, 128)] * 12 + [local_rows] * 3
-    scratch += [full(24, 512)] * 8 + [full(3, 24, 512)]
-    scratch += [full(8, 512)] * 7 + [full(3, 8, 512)]
+    scratch += [full(24, 512)] * 7 + [full(3, 24, 128), full(3, 8, 128)]
+    scratch += [full(8, 512)] * 7 + [full(3, 8, 128)]
     scratch += [full(1024, 128)] * 3 + [full(8, 1024)]
     scratch += ([low(64, 1024)] * 3 + [low(1024, 64)] * 2 + [low(1024, 1024), full(1, 1024), full(64, 1024)]) * 2
     scratch += [low(64, 1024)] + [full(64, 1024)] * 2
     scratch += [low(128, 2048), full(128, 2048), low(128, 2048)] + [full(128, 512)] * 5
     scratch += [low(5, 128, 512), full(3, 512, 128), full(3, 128, 512), low(192, 1024), low(128, 1024), low(2048, 512)]
-    scratch += [pltpu.SemaphoreType.DMA((40,)), pltpu.SemaphoreType.DMA((NAMES,))]
+    scratch += [low(leads[k], *shards[k]) for k in kinds] + [low(n, 4, 16, 128) for n in (3, 2)]
+    scratch += [pltpu.SemaphoreType.DMA((44,)), pltpu.SemaphoreType.DMA((NAMES,))]
     rows = jax.ShapeDtypeStruct((2, 64, 512), BF16)
 
     def wide_out(*shape):

time: 107 us -> 105 us (0.981)
  Pallas kernels: 106 us -> 104 us
    pallas_call x1, Pallas kernels: 104 us -> 101 us  [fused_local(): pl.pallas_call(fused_kernel, name='layer', out_shape=(rows, rows, rows, *...]
where the time goes in v6:
time: 105 us; the launch traced here: 104 us
  Pallas kernels  104 us (99%)
    pallas_call x1, Pallas kernels, fused_local(): pl.pallas_call(fused_kernel, name='layer', out_shape=(rows, rows, rows, *...  101 us
    pallas_call x1, Pallas kernels, fused_local(): pl.pallas_call(copy_kernel, name='hand_over', out_shape=tuple((jax.ShapeD...  2.23 us

profile of v6, /device:TPU:0, one launch (start us, length us, event | category | flops | bytes accessed | tf_op | source)
XLA Modules:
  0.0 104.5 jit_solution(12865392907186040165)
XLA Ops:
  0.7 101.4 %layer.1 = (bf16[2,64,512]{2,1,0:T(8,128)(2,1)}, bf16[2,64,512]{2,1,0:T(8,128)(2,1)}, bf16[2,64,512]{2,1,0:T(8,128)(2,1)}, f32[2,3,16,512]{3,2,1,0:T(8,128)}, f3...) custom-call(bf16[2,64,512]{2,1,0:T(8,128)(2,1)} %bitcast.24, ...), custom_call_target="tpu_custom_call" | custom-call | tf_op jit(solution)/shard_map/layer/pallas_call | solution.py:1654
  102.1 2.2 %hand_over.1 = (bf16[2,64,512]{2,1,0:T(8,128)(2,1)}, bf16[2,64,512]{2,1,0:T(8,128)(2,1)}, bf16[2,64,512]{2,1,0:T(8,128)(2,1)}, f32[2,3,16,512]{3,2,1,0:T(8,128)}...) custom-call(bf16[2,64,512]{2,1,0:T(8,128)(2,1)} %get-tuple-element.3, ...), custom_call_target="tpu_custom_call" | custom-call | tf_op jit(solution)/shard_map/hand_over/pallas_call | solution.py:1668

commit v7 on v6

--- a/solution.py
+++ b/solution.py
@@ -515,7 +515,8 @@
 MESH = pl.DeviceIdType.MESH
 UNIT = 16 * 1024
 BINS = 16
-NAMES = 192
+NAMES = 200
+BETWEEN = ("dn0", "dn1")
 ODD = ("marks", "w0p", "w1p", "u0p", "x3", "x5", "x7", "sa", "sb", "ta")
 F32 = jnp.float32
 BF16 = jnp.bfloat16
@@ -561,7 +562,7 @@
     dnt, acc_k, acc_v,
     act, slope, gul, xh0, xh1, xh2, h1_f, h2_f,
     wt, bias_cols, wz, dt0, dt1, gauge,
-    f_q, f_out, f_up, f_dn, f_u0, f_u1,
+    f_q, f_out, f_up, f_dn, f_u0, f_u1, mid_far, mid_line,
     ss, rs,
 ):
     c = lax.axis_index("rows")
@@ -706,11 +707,15 @@
         def _():
             landed(name + "l", line)
 
-        result[...] = own.astype(F32) + line[0].astype(F32) + line[1].astype(F32)
+        total = own.astype(F32) + line[0].astype(F32) + line[1].astype(F32)
+
+        @pl.when(edge)
+        def _():
+            result[...] = total.astype(result.dtype)
 
         @pl.when(jnp.logical_not(edge))
         def _():
-            result[...] += line[2].astype(F32)
+            result[...] = (total + line[2].astype(F32)).astype(result.dtype)
 
     def line_landed(name, blocks, own):
         @pl.when(edge)
@@ -817,6 +822,7 @@
             for ref in refs
         )
 
+    mids = {g: (mid_far.at[i], mid_line.at[i]) for i, g in enumerate(BETWEEN)}
     fars = {"q": f_q, "u0": f_u0, "u1": f_u1}
     for i in range(2):
         one = pl.ds(i, 1)
@@ -830,16 +836,37 @@
 
     def gather_z(g):
         full, shard = weights[g][:2]
+        if g in BETWEEN:
+            first, second = halves(full)
+            whole = s_dn if g[:2] == "dn" else s_up
+            keep(g + "o", shard, full.at[:, c, z, y, x])
+            for which, cols, device in (("1a", first, x_next), ("1b", second, y_next)):
+                part = full.at[:, c, z, y, x, :, cols]
+                send(g + which, whole.at[:, :, shard_cols(g, cols)], part, device)
+                sent_later(g + which, part)
+            return
         keep(g + "z", shard, full.at[:, c, z, y, x])
         along_z(g, shard, lambda zz: full.at[:, c, zz, y, x])
 
     def gather_f(g):
         full = weights[g][0]
+        if g in BETWEEN:
+            first, second = halves(full)
+            pass_on(g + "A", lambda zz: full.at[:, c, zz, y, :, :, first])
+            pass_on(g + "B", lambda zz: full.at[:, c, zz, :, x, :, second])
+            return
         pass_on(g, lambda zz: full.at[:, c, zz, y, x])
 
     def gather_1(g):
         full = weights[g][0]
         first, second = halves(full)
+        if g in BETWEEN:
+            landed(g + "o", full.at[:, c, z, y, x])
+            landed(g + "1a", full.at[:, c, z, y, 1 - x, :, first])
+            along_z(g + "A", full.at[:, c, z, y, :, :, first], lambda zz: full.at[:, c, zz, y, :, :, first])
+            landed(g + "1b", full.at[:, c, z, 1 - y, x, :, second])
+            along_z(g + "B", full.at[:, c, z, :, x, :, second], lambda zz: full.at[:, c, zz, :, x, :, second])
+            return
         line_landed(g, lambda n: full.at[:, c, pl.ds(0, n), y, x], 1)
         part = full.at[:, c, :, y, x, :, first]
         send(g + "1a", part, part, x_next)
@@ -851,14 +878,24 @@
     def gather_2(g):
         full = weights[g][0]
         first, second = halves(full)
-        landed(g + "1a", full.at[:, c, :, y, 1 - x, :, first])
+        if g in BETWEEN:
+            line_landed(g + "A", lambda n: full.at[:, c, pl.ds(0, n), y, :, :, first], 0)
+        else:
+            landed(g + "1a", full.at[:, c, :, y, 1 - x, :, first])
         part = full.at[:, c, :, y, :, :, first]
         send(g + "2a", part, part, y_next)
         sent_later(g + "2a", part)
-        landed(g + "1b", full.at[:, c, :, 1 - y, x, :, second])
+        if g in BETWEEN:
+            line_landed(g + "B", lambda n: full.at[:, c, pl.ds(0, n), :, x, :, second], 0)
+        else:
+            landed(g + "1b", full.at[:, c, :, 1 - y, x, :, second])
         part = full.at[:, c, :, :, x, :, second]
         send(g + "2b", part, part, x_next)
         sent_later(g + "2b", part)
+
+    def shard_cols(g, cols):
+        start = 256 * int(g[-1]) if g[:2] == "dn" else 1024 * int(g[-1])
+        return pl.ds(start + cols.start, cols.size)
 
     def gather_3(g):
         full = weights[g][0]
@@ -906,6 +943,10 @@
                 add(grad.at[lead, c, zz, y, :, :, first], part.at[0, lead, zz])
                 add(grad.at[lead, c, zz, :, x, :, second], part.at[1, lead, zz])
 
+        if g in BETWEEN:
+            fold_z(g + "A", lambda zz: grad.at[:, c, zz, y, :, :, first], mids[g][0].at[0, 0], mids[g][1].at[:, 0])
+            fold_z(g + "B", lambda zz: grad.at[:, c, zz, :, x, :, second], mids[g][0].at[1, 0], mids[g][1].at[:, 1])
+            return
         send(g + "r2a", grad.at[:, c, :, y, 1 - x, :, first], piece.at[0], x_next)
         sent_later(g + "r2a", piece.at[0])
         send(g + "r2b", grad.at[:, c, :, 1 - y, x, :, second], piece.at[1], y_next)
@@ -914,6 +955,14 @@
     def scatter_3(g):
         grad, _, _, piece, line = weights[g][2:7]
         first, second = halves(grad)
+        if g in BETWEEN:
+            fold_sum(g + "A", grad[:, c, z, y, :, :, first], mids[g][1].at[:, 0], grad.at[:, c, z, y, :, :, first])
+            send(g + "r2a", grad.at[:, c, z, y, 1 - x, :, first], piece.at[0, :, 0], x_next)
+            sent_later(g + "r2a", piece.at[0, :, 0])
+            fold_sum(g + "B", grad[:, c, z, :, x, :, second], mids[g][1].at[:, 1], grad.at[:, c, z, :, x, :, second])
+            send(g + "r2b", grad.at[:, c, z, 1 - y, x, :, second], piece.at[1, :, 0], y_next)
+            sent_later(g + "r2b", piece.at[1, :, 0])
+            return
         landed(g + "r2a", piece.at[0])
         landed(g + "r2b", piece.at[1])
         for lead in range(grad.shape[0]):
@@ -927,10 +976,21 @@
 
     def scatter_f(g):
         grad, line = weights[g][2], weights[g][6]
+        if g in BETWEEN:
+            first, second = halves(grad)
+            fold_f(g + "A", lambda zz: grad.at[:, c, zz, y, :, :, first], mids[g][0].at[0, 0], mids[g][1].at[:, 0])
+            fold_f(g + "B", lambda zz: grad.at[:, c, zz, :, x, :, second], mids[g][0].at[1, 0], mids[g][1].at[:, 1])
+            return
         fold_f(g, lambda zz: grad.at[:, c, zz, y, x], fars[g], line)
 
     def scattered(g):
-        grad, _, _, _, line, result = weights[g][2:8]
+        grad, _, _, piece, line, result = weights[g][2:8]
+        if g in BETWEEN:
+            landed(g + "r2a", piece.at[0, :, 0])
+            landed(g + "r2b", piece.at[1, :, 0])
+            across = jnp.concatenate([piece[0, :, 0], piece[1, :, 0]], axis=-1)
+            result[...] = grad[:, c, z, y, x].astype(F32) + across.astype(F32)
+            return
         fold_sum(g, grad[:, c, z, y, x], line, result)
 
     left, right = pl.ds(0, 256), pl.ds(256, 256)
@@ -1305,115 +1365,115 @@
         pl.semaphore_signal(barrier, inc=1, device_id=device, device_id_type=MESH)
     pl.semaphore_wait(barrier, len(greet))
     to_plane("x", tok, all_tok, True)
-    slice_1("w1", s_in.at[1, pl.ds(1, 2)], ws1)
-    slice_1("w0", s_in.at[0], ws0)
+    gather_z("out0")
+    gather_z("dn0")
+    gather_z("dn1")
     for i, (_, ref) in enumerate(given):
         landed("given" + str(i), ref)
-    to_plane("m", mem, all_mem, True)
     for i, (ref, _) in enumerate(raw):
         landed("raw" + str(i), ref)
         span = ref.shape[2]
         for m in range(2):
             for start in (0, 64):
                 meta[m, i : i + 1, start : start + span] = ref[m]
-    gather_z("q")
+    gather_z("up0")
+    to_plane("meta", meta, in_meta)
+    slice_1("w0", s_in.at[0], ws0)
     spread_1("x", all_tok, 0)
     spread_1("x", all_tok, 1)
-    gather_z("out0")
-    to_plane("meta", meta, in_meta)
-    gather_z("dn0")
-    spread_1("m", all_mem, 0)
-    gather_z("out1")
-    spread_1("m", all_mem, 1)
+    slice_1("w1", s_in.at[1, pl.ds(1, 2)], ws1)
+    to_plane("m", mem, all_mem, True)
+    gather_f("out0")
     spread_2("x", all_tok, 0)
+    gather_f("up0")
+    gather_z("up1")
+    spread_2("x", all_tok, 1)
     slice_2("w0", ws0)
+    gather_z("q")
+    gather_1("out0")
+    spread_4("x", all_tok, 0)
     landed("meta", in_meta)
     lane = lax.broadcasted_iota(jnp.int32, (8, 128), 1)
-    gather_f("q")
     all_meta[me_slot] = jnp.where(lane < 64, in_meta[0], in_meta[1])
-    gather_f("out0")
     for cc, yy, xx in plane_peers:
         send("marks", all_meta.at[me_slot], all_meta.at[me_slot], (cc, at(z, yy, xx)))
+    gather_1("up0")
     sent_later("marks", all_meta.at[pl.ds(0, 7)])
-    spread_2("m", all_mem, 0)
-    spread_2("m", all_mem, 1)
-    gather_f("dn0")
-    gather_z("up1")
-    spread_2("x", all_tok, 1)
+    spread_1("m", all_mem, 0)
+    slice_2("w1", ws1)
+    gather_2("out0")
+    gather_2("up0")
+    gather_f("up1")
+    spread_4("x", all_tok, 1)
+    slice_f("w0", ws0)
+    gather_z("out1")
+    gather_1("up1")
+    gather_3("out0")
+    spread_1("m", all_mem, 1)
+    make_masks()
+    gather_f("q")
     for i, row in enumerate((0, 1, 4)):
         bias_cols[i] = jnp.transpose(jnp.broadcast_to(bias(row), (128, width)))
-    gather_z("dn1")
-    gather_1("q")
-    gather_1("out0")
-    gather_1("dn0")
-    gather_2("q")
-    spread_4("x", all_tok, 0)
-    spread_4("m", all_mem, 0)
-    gather_2("out0")
-    slice_f("w0", ws0)
-    make_masks()
-    gather_f("out1")
-    gather_2("dn0")
-    gather_f("up1")
+    spread_2("m", all_mem, 0)
     slice_3("w0", ws0)
-    spread_4("x", all_tok, 1)
-    gather_z("up0")
-    gather_f("dn1")
-    spread_4("m", all_mem, 1)
-    to_plane("cot", cot, in_cot)
-    gather_3("q")
-    gather_1("up1")
+    gather_1("dn1")
     spread_3("x", all_tok)
     slice_4("w0", ws0)
-    slice_2("w1", ws1)
-    gather_3("out0")
-    gather_1("out1")
+    gather_3("up0")
+    gather_1("q")
+    gather_2("up1")
     heads_weights(0, ws0)
     project_heads(all_tok, 0, qt0, k0, kt0, v0, vt0)
-    gather_1("dn1")
-    gather_f("up0")
+    attend(0, qt0, k0, vt0, pt0, l0, ot0, True, "x3", a3, b3)
+    spread_2("m", all_mem, 1)
+    gather_2("q")
+    attend(1, qt0, k0, vt0, pt0, l0, ot0, True, "x3", a3, b3)
+    gather_f("out1")
+    gather_f("dn1")
+    spread_4("m", all_mem, 0)
+    gather_1("dn0")
+    slice_f("w1", ws1)
+    gather_1("out1")
+    attend(2, qt0, k0, vt0, pt0, l0, ot0, True, "x3", a3, b3)
     gathered("out0")
-    attend(0, qt0, k0, vt0, pt0, l0, ot0, True, "x3", a3, b3)
-    gather_2("up1")
-    attend(1, qt0, k0, vt0, pt0, l0, ot0, True, "x3", a3, b3)
-    attend(2, qt0, k0, vt0, pt0, l0, ot0, True, "x3", a3, b3)
     attend(3, qt0, k0, vt0, pt0, l0, ot0, True, "x3", a3, b3)
-    slice_f("w1", ws1)
+    spread_4("m", all_mem, 1)
     gather_2("dn1")
-    gather_1("up0")
+    gather_3("q")
+    gather_2("out1")
+    slice_3("w1", ws1)
+    gathered("q")
     landed("x3", b3)
-    gathered("q")
     words_f = all_tok[me_slot].reshape(here, width).astype(F32)
-    spread_3("m", all_mem)
-    gather_3("dn0")
+    gather_3("up1")
+    gather_f("dn0")
     branch = tn(b3[...].reshape(width, here), matrix(w_out.at[0])) + bias(2)
     h1, scale0 = norm(words_f * omega[0:1, :] + branch, 0, xh0)
     h1_f[...] = h1
     h1_low = h1.astype(BF16)
+    spread_3("m", all_mem)
     by_head(a4, nn(h1_low, matrix(w_q.at[0])) + bias(3))
-    slice_3("w1", ws1)
     to_heads("x4", a4, b4)
-    gather_2("out1")
     slice_4("w1", ws1)
-    gather_3("up1")
-    gather_2("up0")
+    gather_2("dn0")
+    gather_3("out1")
     heads_weights(3, ws1)
+    to_plane("cot", cot, in_cot)
+    gather_3("dn1")
     project_heads(all_mem, 3, None, k1, kt1, v1, vt1)
-    gathered("up1")
     landed("x4", b4)
     for s in range(GROUP):
         qt1[:, s * here : (s + 1) * here] = (b4[s].astype(F32) * 0.125).astype(BF16)
     attend(0, qt1, k1, vt1, pt1, l1, ot1, False, "x5", a5, b5)
-    gather_3("dn1")
-    gather_3("out1")
     attend(1, qt1, k1, vt1, pt1, l1, ot1, False, "x5", a5, b5)
     attend(2, qt1, k1, vt1, pt1, l1, ot1, False, "x5", a5, b5)
     attend(3, qt1, k1, vt1, pt1, l1, ot1, False, "x5", a5, b5)
-    gather_3("up0")
+    gathered("out1")
+    gathered("up1")
     gathered("dn1")
     gathered("up0")
+    gather_3("dn0")
     gathered("dn0")
-    gathered("out1")
     landed("x5", b5)
     branch = tn(b5[...].reshape(width, here), matrix(w_out.at[1])) + bias(5)
     h2, scale1 = norm(h1_f[...] * omega[1:2, :] + branch, 1, xh1)
@@ -1429,140 +1489,140 @@
     grad = in_cot[...].reshape(here, width).astype(F32)
     dr, skip = norm_back(grad, 2, xh2, scale2, h2_f[...])
     gf = dr.astype(BF16)
+    column(6, gf.astype(F32))
     put(g_dn.at[0], tn(act[...], gf[:, 0:256]))
+    back = feed_back(gf, skip)
     scatter_0("dn0")
-    column(6, gf.astype(F32))
-    back = feed_back(gf, skip)
     dr, skip = norm_back(back, 1, xh1, scale1, h1_f[...])
     gc = dr.astype(BF16)
     column(5, gc.astype(F32))
     by_head(a6, nt(gc, matrix(w_out.at[1])))
     to_heads("x6", a6, b6)
+    put(g_up.at[0], tn(h2_low, gul[:, 0:1024]))
     scatter_1("dn0")
-    put(g_up.at[0], tn(h2_low, gul[:, 0:1024]))
     scatter_0("up0")
     put(g_up.at[1], tn(h2_low, gul[:, 1024:2048]))
     scatter_1("up0")
+    back = skip
     scatter_0("up1")
-    back = skip
     landed("x6", b6)
     attend_start(b6, l1, ot1)
     attend_back(0, qt1, kt1, v1, pt1, False, "x7", a7, b7)
+    from_plane("res", out_res, o_res)
+    put(g_out.at[1], nn(b5[...].reshape(width, here), gc))
     attend_back(1, qt1, kt1, v1, pt1, False, "x7", a7, b7)
     attend_back(2, qt1, kt1, v1, pt1, False, "x7", a7, b7)
     attend_back(3, qt1, kt1, v1, pt1, False, "x7", a7, b7)
-    put(g_dn.at[1], tn(act[...], gf[:, 256:512]))
-    scatter_2("dn0")
-    scatter_1("up1")
     dt1[0:64, :] = acc_k[...].astype(BF16)
     dt1[64:128, :] = acc_v[...].astype(BF16)
+    scatter_1("up1")
+    put(g_dn.at[1], tn(act[...], gf[:, 256:512]))
+    scatter_0("dn1")
+    scatter_2("dn0")
     rows_back(dt1, 3, dx1, 1 - c)
     scatter_2("up0")
     merge_0("dm", dx1, dc1)
     rows_back(dt1, 3, dx1, c)
     slices_back(dt1, all_mem, gs1)
+    value_sums(dt1)
     landed("x7", b7)
-    put(g_out.at[1], nn(b5[...].reshape(width, here), gc))
-    scatter_0("dn1")
-    scatter_3("dn0")
-    from_plane("res", out_res, o_res)
     dq = b7[...].reshape(width, here)
+    unslice_0("u1", gs1, cs1)
     dq_row = flip(dq)
     column(3, dq_row)
     back = back + nt(dq_row.astype(BF16), matrix(w_q.at[0]))
     dr, skip = norm_back(back, 0, xh0, scale0, words_f)
-    value_sums(dt1)
     ga = dr.astype(BF16)
-    unslice_0("u1", gs1, cs1)
     column(2, ga.astype(F32))
+    by_head(a8, nt(ga, matrix(w_out.at[0])))
+    to_heads("x8", a8, b8)
+    put(g_out.at[0], nn(b3[...].reshape(width, here), ga))
+    scatter_1("dn1")
+    put(g_q.at[0], nt(flip(h1_low).astype(BF16), dq))
+    last = skip
+    unslice_1("u1", gs1, cs1, zs1)
+    scatter_0("out1")
+    scatter_1("out1")
+    scatter_3("up0")
+    scatter_2("up1")
+    scatter_0("q")
     small("s0", sg0, sr0, core_next)
-    by_head(a8, nt(ga, matrix(w_out.at[0])))
-    put(g_q.at[0], nt(flip(h1_low).astype(BF16), dq))
-    to_heads("x8", a8, b8)
-    small_add("s0", sr0, sg0, sg1)
-    small("s1", sg1, sr1, y_next)
-    scatter_0("q")
-    scatter_0("out1")
-    put(g_out.at[0], nn(b3[...].reshape(width, here), ga))
-    scatter_2("up1")
-    last = skip
-    scatter_1("dn1")
-    scatter_f("dn0")
-    scatter_3("up0")
+    scatter_0("out0")
     landed("x8", b8)
     attend_start(b8, l0, ot0)
-    scatter_0("out0")
     attend_back(0, qt0, kt0, v0, pt0, True, None, None, None)
-    unslice_1("u1", gs1, cs1, zs1)
-    merge_1("dm", dx1, dc1, dp1)
+    scatter_f("dn0")
     attend_back(1, qt0, kt0, v0, pt0, True, None, None, None)
-    small_add("s1", sr1, sg1, sg2)
-    scatter_f("up0")
-    small("s2", sg2, sr2, x_next)
+    small_add("s0", sr0, sg0, sg1)
+    scatter_2("dn1")
+    scatter_1("q")
     attend_back(2, qt0, kt0, v0, pt0, True, None, None, None)
     attend_back(3, qt0, kt0, v0, pt0, True, None, None, None)
-    scatter_1("out1")
+    scatter_2("out1")
+    merge_1("dm", dx1, dc1, dp1)
     scatter_3("up1")
-    scattered("dn0")
-    unslice_f("u1", gs1, zs1)
     dt0[64:128, :] = acc_k[...].astype(BF16)
-    scatter_1("q")
     dt0[128:192, :] = acc_v[...].astype(BF16)
+    scatter_f("up0")
     slices_back(dt0, all_tok, gs0)
-    rows_back(dt0, 0, dx0, 1 - c)
+    scatter_1("out0")
     unslice_0("u0", gs0, cs0)
     head_sums(dt0)
-    scatter_2("dn1")
+    scatter_3("out1")
+    scatter_2("q")
+    unslice_1("u0", gs0, cs0, zs0)
+    small("t0", tg0, tr0, core_next)
+    small("s1", sg1, sr1, y_next)
+    rows_back(dt0, 0, dx0, 1 - c)
+    small_add("t0", tr0, tg0, tg1)
+    small("t1", tg1, tr1, y_next)
+    merge_0("dx", dx0, dc0)
+    rows_back(dt0, 0, dx0, c)
     merge_3("dm", dx1, dp1)
-    small("t0", tg0, tr0, core_next)
-    unslice_1("u0", gs0, cs0, zs0)
+    scatter_f("dn1")
+    unslice_f("u1", gs1, zs1)
+    merge_1("dx", dx0, dc0, dp0)
+    scatter_f("out1")
+    small_add("t1", tr1, tg1, tg2)
+    small("t2", tg2, tr2, x_next)
+    scatter_3("q")
+    scatter_f("up1")
+    small_add("s1", sr1, sg1, sg2)
+    small("s2", sg2, sr2, x_next)
+    landed("res", o_res)
+    unslice_f("u0", gs0, zs0)
+    scatter_2("out0")
+    scatter_3("dn1")
+    scatter_f("q")
+    out_mem[...] = merge_2("dm", dx1, dp1).astype(BF16).reshape(2, 64, width)
+    from_plane("gmem", out_mem, o_mem)
+    small_add("t2", tr2, tg2, tg3)
+    merge_3("dx", dx0, dp0)
     small_add("s2", sr2, sg2, sg3)
-    scatter_f("up1")
-    merge_0("dx", dx0, dc0)
-    scatter_2("out1")
+    scattered("up0")
+    scatter_3("out0")
     small_z("sa", sg3, slice(None), tile_own, sra)
     small_z("sb", sg3, pl.ds(8, 8), tile_up, srb)
-    small_add("t0", tr0, tg0, tg1)
-    scatter_3("dn1")
-    small("t1", tg1, tr1, y_next)
-    rows_back(dt0, 0, dx0, c)
-    scattered("up0")
-    scatter_1("out0")
-    merge_1("dx", dx0, dc0, dp0)
-    scatter_2("q")
-    out_mem[...] = merge_2("dm", dx1, dp1).astype(BF16).reshape(2, 64, width)
-    from_plane("gmem", out_mem, o_mem)
-    small_add("t1", tr1, tg1, tg2)
-    small("t2", tg2, tr2, x_next)
-    scatter_f("dn1")
-    scatter_3("out1")
-    scatter_2("out0")
-    merge_3("dx", dx0, dp0)
-    unslice_f("u0", gs0, zs0)
-    scatter_3("q")
-    small_add("t2", tr2, tg2, tg3)
-    scatter_3("out0")
+    unslice_2("u0", gs0, zs0, fs0, o_in.at[0])
+    unslice_2("u1", gs1, zs1, fs1, o_in.at[1, pl.ds(1, 2)])
+    small_z("ta", tg3, slice(None), tile_own, tra)
+    scattered("up1")
+    scattered("out1")
     scattered("dn1")
-    landed("res", o_res)
-    unslice_2("u1", gs1, zs1, fs1, o_in.at[1, pl.ds(1, 2)])
-    scatter_f("q")
-    scatter_f("out1")
-    small_z("ta", tg3, slice(None), tile_own, tra)
-    unslice_2("u0", gs0, zs0, fs0, o_in.at[0])
-    keep("e3", o_dn, h_dn)
+    scatter_3("dn0")
     scatter_f("out0")
     out_tok[...] = (merge_2("dx", dx0, dp0) + last).astype(BF16).reshape(2, 64, width)
     from_plane("gtok", out_tok, o_tok)
+    unslice_3("u1", o_in.at[1, pl.ds(1, 2)])
+    unslice_3("u0", o_in.at[0])
+    scattered("q")
     landed("gmem", o_mem)
+    scattered("dn0")
+    keep("e3", o_dn, h_dn)
     small_out()
-    scattered("up1")
-    unslice_3("u1", o_in.at[1, pl.ds(1, 2)])
-    scattered("out1")
-    scattered("q")
     keep("e2", o_up, h_up)
     scattered("out0")
     keep("e1", o_out, h_out)
-    unslice_3("u0", o_in.at[0])
     keep("e0", o_in, h_in)
     landed("gtok", o_tok)
     for i, ref in enumerate((h_in, h_out, h_up, h_dn, h_bias, h_upb, h_gain_o, h_shift_o, h_omega_o)):
@@ -1643,8 +1703,9 @@
     scratch += ([low(64, 1024)] * 3 + [low(1024, 64)] * 2 + [low(1024, 1024), full(1, 1024), full(64, 1024)]) * 2
     scratch += [low(64, 1024)] + [full(64, 1024)] * 2
     scratch += [low(128, 2048), full(128, 2048), low(128, 2048)] + [full(128, 512)] * 5
-    scratch += [low(5, 128, 512), full(3, 512, 128), full(3, 128, 512), low(192, 1024), low(128, 1024), low(2048, 512)]
+    scratch += [low(5, 128, 512), full(3, 512, 128), full(3, 128, 512), low(192, 1024), low(128, 1024), low(2304, 512)]
     scratch += [low(leads[k], *shards[k]) for k in kinds] + [low(n, 4, 16, 128) for n in (3, 2)]
+    scratch += [low(2, 2, 1, 1, 2, 64, 128), low(2, 3, 2, 1, 2, 64, 128)]
     scratch += [pltpu.SemaphoreType.DMA((44,)), pltpu.SemaphoreType.DMA((NAMES,))]
     rows = jax.ShapeDtypeStruct((2, 64, 512), BF16)
 

time: 105 us -> 101 us (0.962)
  Pallas kernels: 104 us -> 99 us
    pallas_call x1, Pallas kernels: 101 us -> 96.8 us  [fused_local(): pl.pallas_call(fused_kernel, name='layer', out_shape=(rows, rows, rows, *...]
where the time goes in v7:
time: 101 us; the launch traced here: 99.9 us
  Pallas kernels  99 us (98%)
    pallas_call x1, Pallas kernels, fused_local(): pl.pallas_call(fused_kernel, name='layer', out_shape=(rows, rows, rows, *...  96.8 us
    pallas_call x1, Pallas kernels, fused_local(): pl.pallas_call(copy_kernel, name='hand_over', out_shape=tuple((jax.ShapeD...  2.23 us

profile of v7, /device:TPU:0, one launch (start us, length us, event | category | flops | bytes accessed | tf_op | source)
XLA Modules:
  0.0 99.9 jit_solution(7017276048706065568)
XLA Ops:
  0.7 96.8 %layer.1 = (bf16[2,64,512]{2,1,0:T(8,128)(2,1)}, bf16[2,64,512]{2,1,0:T(8,128)(2,1)}, bf16[2,64,512]{2,1,0:T(8,128)(2,1)}, f32[2,3,16,512]{3,2,1,0:T(8,128)}, f3...) custom-call(bf16[2,64,512]{2,1,0:T(8,128)(2,1)} %bitcast.24, ...), custom_call_target="tpu_custom_call" | custom-call | tf_op jit(solution)/shard_map/layer/pallas_call | solution.py:1715
  97.5 2.2 %hand_over.1 = (bf16[2,64,512]{2,1,0:T(8,128)(2,1)}, bf16[2,64,512]{2,1,0:T(8,128)(2,1)}, bf16[2,64,512]{2,1,0:T(8,128)(2,1)}, f32[2,3,16,512]{3,2,1,0:T(8,128)}...) custom-call(bf16[2,64,512]{2,1,0:T(8,128)(2,1)} %get-tuple-element.3, ...), custom_call_target="tpu_custom_call" | custom-call | tf_op jit(solution)/shard_map/hand_over/pallas_call | solution.py:1729

commit v8 on v7

--- a/solution.py
+++ b/solution.py
@@ -515,9 +515,10 @@
 MESH = pl.DeviceIdType.MESH
 UNIT = 16 * 1024
 BINS = 16
-NAMES = 200
+NAMES = 208
 BETWEEN = ("dn0", "dn1")
-ODD = ("marks", "w0p", "w1p", "u0p", "x3", "x5", "x7", "sa", "sb", "ta")
+BETWEEN_OUT = BETWEEN + ("up1", "out1")
+ODD = ("marks", "w0p", "w1p", "u0p", "x3", "x5", "x7", "sa", "sb", "ta", "out11a", "out11b")
 F32 = jnp.float32
 BF16 = jnp.bfloat16
 PLANES, YS, XS, CORES = 4, 2, 2, 2
@@ -836,9 +837,9 @@
 
     def gather_z(g):
         full, shard = weights[g][:2]
-        if g in BETWEEN:
+        if g in BETWEEN_OUT:
             first, second = halves(full)
-            whole = s_dn if g[:2] == "dn" else s_up
+            whole = s_dn if g[:2] == "dn" else s_up if g[:2] == "up" else shard
             keep(g + "o", shard, full.at[:, c, z, y, x])
             for which, cols, device in (("1a", first, x_next), ("1b", second, y_next)):
                 part = full.at[:, c, z, y, x, :, cols]
@@ -850,7 +851,7 @@
 
     def gather_f(g):
         full = weights[g][0]
-        if g in BETWEEN:
+        if g in BETWEEN_OUT:
             first, second = halves(full)
             pass_on(g + "A", lambda zz: full.at[:, c, zz, y, :, :, first])
             pass_on(g + "B", lambda zz: full.at[:, c, zz, :, x, :, second])
@@ -860,7 +861,7 @@
     def gather_1(g):
         full = weights[g][0]
         first, second = halves(full)
-        if g in BETWEEN:
+        if g in BETWEEN_OUT:
             landed(g + "o", full.at[:, c, z, y, x])
             landed(g + "1a", full.at[:, c, z, y, 1 - x, :, first])
             along_z(g + "A", full.at[:, c, z, y, :, :, first], lambda zz: full.at[:, c, zz, y, :, :, first])
@@ -878,14 +879,14 @@
     def gather_2(g):
         full = weights[g][0]
         first, second = halves(full)
-        if g in BETWEEN:
+        if g in BETWEEN_OUT:
             line_landed(g + "A", lambda n: full.at[:, c, pl.ds(0, n), y, :, :, first], 0)
         else:
             landed(g + "1a", full.at[:, c, :, y, 1 - x, :, first])
         part = full.at[:, c, :, y, :, :, first]
         send(g + "2a", part, part, y_next)
         sent_later(g + "2a", part)
-        if g in BETWEEN:
+        if g in BETWEEN_OUT:
             line_landed(g + "B", lambda n: full.at[:, c, pl.ds(0, n), :, x, :, second], 0)
         else:
             landed(g + "1b", full.at[:, c, :, 1 - y, x, :, second])
@@ -894,7 +895,7 @@
         sent_later(g + "2b", part)
 
     def shard_cols(g, cols):
-        start = 256 * int(g[-1]) if g[:2] == "dn" else 1024 * int(g[-1])
+        start = int(g[-1]) * {"dn": 256, "up": 1024, "ou": 0}[g[:2]]
         return pl.ds(start + cols.start, cols.size)
 
     def gather_3(g):
@@ -1364,116 +1365,116 @@
     for device in greet:
         pl.semaphore_signal(barrier, inc=1, device_id=device, device_id_type=MESH)
     pl.semaphore_wait(barrier, len(greet))
+    gather_z("out0")
+    gather_z("dn1")
+    gather_z("up1")
     to_plane("x", tok, all_tok, True)
-    gather_z("out0")
+    slice_1("w0", s_in.at[0], ws0)
     gather_z("dn0")
-    gather_z("dn1")
-    for i, (_, ref) in enumerate(given):
-        landed("given" + str(i), ref)
+    gather_z("out1")
+    gather_z("q")
+    gather_z("up0")
     for i, (ref, _) in enumerate(raw):
         landed("raw" + str(i), ref)
         span = ref.shape[2]
         for m in range(2):
             for start in (0, 64):
                 meta[m, i : i + 1, start : start + span] = ref[m]
-    gather_z("up0")
+    slice_1("w1", s_in.at[1, pl.ds(1, 2)], ws1)
+    gather_f("out0")
+    spread_1("x", all_tok, 0)
+    slice_2("w0", ws0)
+    gather_1("out0")
+    gather_f("q")
     to_plane("meta", meta, in_meta)
-    slice_1("w0", s_in.at[0], ws0)
-    spread_1("x", all_tok, 0)
     spread_1("x", all_tok, 1)
-    slice_1("w1", s_in.at[1, pl.ds(1, 2)], ws1)
-    to_plane("m", mem, all_mem, True)
-    gather_f("out0")
     spread_2("x", all_tok, 0)
     gather_f("up0")
-    gather_z("up1")
+    gather_2("out0")
+    gather_1("q")
+    gather_1("out1")
+    slice_f("w0", ws0)
+    gather_1("up0")
+    to_plane("m", mem, all_mem, True)
+    for i, (_, ref) in enumerate(given):
+        landed("given" + str(i), ref)
     spread_2("x", all_tok, 1)
-    slice_2("w0", ws0)
-    gather_z("q")
-    gather_1("out0")
-    spread_4("x", all_tok, 0)
     landed("meta", in_meta)
     lane = lax.broadcasted_iota(jnp.int32, (8, 128), 1)
+    gather_2("q")
+    slice_3("w0", ws0)
+    gather_1("dn0")
     all_meta[me_slot] = jnp.where(lane < 64, in_meta[0], in_meta[1])
     for cc, yy, xx in plane_peers:
         send("marks", all_meta.at[me_slot], all_meta.at[me_slot], (cc, at(z, yy, xx)))
-    gather_1("up0")
+    gather_3("out0")
+    gather_2("up0")
+    spread_4("x", all_tok, 0)
+    spread_4("x", all_tok, 1)
+    slice_2("w1", ws1)
+    slice_4("w0", ws0)
+    spread_3("x", all_tok)
+    gather_3("q")
+    spread_1("m", all_mem, 0)
+    gathered("out0")
+    spread_1("m", all_mem, 1)
+    gather_f("out1")
+    heads_weights(0, ws0)
     sent_later("marks", all_meta.at[pl.ds(0, 7)])
-    spread_1("m", all_mem, 0)
-    slice_2("w1", ws1)
-    gather_2("out0")
-    gather_2("up0")
-    gather_f("up1")
-    spread_4("x", all_tok, 1)
-    slice_f("w0", ws0)
-    gather_z("out1")
     gather_1("up1")
-    gather_3("out0")
-    spread_1("m", all_mem, 1)
     make_masks()
-    gather_f("q")
     for i, row in enumerate((0, 1, 4)):
         bias_cols[i] = jnp.transpose(jnp.broadcast_to(bias(row), (128, width)))
-    spread_2("m", all_mem, 0)
-    slice_3("w0", ws0)
-    gather_1("dn1")
-    spread_3("x", all_tok)
-    slice_4("w0", ws0)
-    gather_3("up0")
-    gather_1("q")
-    gather_2("up1")
-    heads_weights(0, ws0)
     project_heads(all_tok, 0, qt0, k0, kt0, v0, vt0)
     attend(0, qt0, k0, vt0, pt0, l0, ot0, True, "x3", a3, b3)
+    gather_f("dn0")
+    gather_2("out1")
+    attend(1, qt0, k0, vt0, pt0, l0, ot0, True, "x3", a3, b3)
+    spread_2("m", all_mem, 0)
+    slice_f("w1", ws1)
     spread_2("m", all_mem, 1)
-    gather_2("q")
-    attend(1, qt0, k0, vt0, pt0, l0, ot0, True, "x3", a3, b3)
-    gather_f("out1")
-    gather_f("dn1")
-    spread_4("m", all_mem, 0)
-    gather_1("dn0")
-    slice_f("w1", ws1)
-    gather_1("out1")
     attend(2, qt0, k0, vt0, pt0, l0, ot0, True, "x3", a3, b3)
-    gathered("out0")
+    gather_1("dn1")
     attend(3, qt0, k0, vt0, pt0, l0, ot0, True, "x3", a3, b3)
-    spread_4("m", all_mem, 1)
-    gather_2("dn1")
-    gather_3("q")
-    gather_2("out1")
     slice_3("w1", ws1)
+    gather_3("up0")
+    gather_2("dn0")
     gathered("q")
+    gather_f("up1")
     landed("x3", b3)
     words_f = all_tok[me_slot].reshape(here, width).astype(F32)
-    gather_3("up1")
-    gather_f("dn0")
     branch = tn(b3[...].reshape(width, here), matrix(w_out.at[0])) + bias(2)
     h1, scale0 = norm(words_f * omega[0:1, :] + branch, 0, xh0)
     h1_f[...] = h1
+    gather_3("out1")
     h1_low = h1.astype(BF16)
-    spread_3("m", all_mem)
+    slice_4("w1", ws1)
     by_head(a4, nn(h1_low, matrix(w_q.at[0])) + bias(3))
     to_heads("x4", a4, b4)
-    slice_4("w1", ws1)
-    gather_2("dn0")
-    gather_3("out1")
+    gather_2("up1")
+    gather_f("dn1")
+    spread_4("m", all_mem, 0)
+    spread_4("m", all_mem, 1)
+    landed("x4", b4)
+    spread_3("m", all_mem)
+    gathered("out1")
     heads_weights(3, ws1)
-    to_plane("cot", cot, in_cot)
-    gather_3("dn1")
+    gather_2("dn1")
     project_heads(all_mem, 3, None, k1, kt1, v1, vt1)
-    landed("x4", b4)
     for s in range(GROUP):
         qt1[:, s * here : (s + 1) * here] = (b4[s].astype(F32) * 0.125).astype(BF16)
+    gather_3("dn0")
+    gathered("up0")
+    gather_3("up1")
     attend(0, qt1, k1, vt1, pt1, l1, ot1, False, "x5", a5, b5)
     attend(1, qt1, k1, vt1, pt1, l1, ot1, False, "x5", a5, b5)
     attend(2, qt1, k1, vt1, pt1, l1, ot1, False, "x5", a5, b5)
     attend(3, qt1, k1, vt1, pt1, l1, ot1, False, "x5", a5, b5)
-    gathered("out1")
+    gathered("dn0")
+    gather_3("dn1")
+    to_plane("cot", cot, in_cot)
+    gathered("dn1")
     gathered("up1")
-    gathered("dn1")
-    gathered("up0")
-    gather_3("dn0")
-    gathered("dn0")
     landed("x5", b5)
     branch = tn(b5[...].reshape(width, here), matrix(w_out.at[1])) + bias(5)
     h2, scale1 = norm(h1_f[...] * omega[1:2, :] + branch, 1, xh1)
@@ -1498,130 +1499,130 @@
     column(5, gc.astype(F32))
     by_head(a6, nt(gc, matrix(w_out.at[1])))
     to_heads("x6", a6, b6)
+    put(g_out.at[1], nn(b5[...].reshape(width, here), gc))
+    scatter_1("dn0")
+    put(g_dn.at[1], tn(act[...], gf[:, 256:512]))
+    scatter_0("dn1")
+    from_plane("res", out_res, o_res)
     put(g_up.at[0], tn(h2_low, gul[:, 0:1024]))
-    scatter_1("dn0")
-    scatter_0("up0")
     put(g_up.at[1], tn(h2_low, gul[:, 1024:2048]))
-    scatter_1("up0")
     back = skip
-    scatter_0("up1")
     landed("x6", b6)
     attend_start(b6, l1, ot1)
+    scatter_0("up0")
+    scatter_1("dn1")
     attend_back(0, qt1, kt1, v1, pt1, False, "x7", a7, b7)
-    from_plane("res", out_res, o_res)
-    put(g_out.at[1], nn(b5[...].reshape(width, here), gc))
     attend_back(1, qt1, kt1, v1, pt1, False, "x7", a7, b7)
     attend_back(2, qt1, kt1, v1, pt1, False, "x7", a7, b7)
+    scatter_2("dn0")
     attend_back(3, qt1, kt1, v1, pt1, False, "x7", a7, b7)
     dt1[0:64, :] = acc_k[...].astype(BF16)
     dt1[64:128, :] = acc_v[...].astype(BF16)
+    scatter_1("up0")
+    scatter_0("out1")
+    scatter_0("up1")
+    rows_back(dt1, 3, dx1, 1 - c)
     scatter_1("up1")
-    put(g_dn.at[1], tn(act[...], gf[:, 256:512]))
-    scatter_0("dn1")
-    scatter_2("dn0")
-    rows_back(dt1, 3, dx1, 1 - c)
-    scatter_2("up0")
+    landed("x7", b7)
     merge_0("dm", dx1, dc1)
     rows_back(dt1, 3, dx1, c)
-    slices_back(dt1, all_mem, gs1)
-    value_sums(dt1)
-    landed("x7", b7)
     dq = b7[...].reshape(width, here)
-    unslice_0("u1", gs1, cs1)
     dq_row = flip(dq)
+    scatter_2("dn1")
     column(3, dq_row)
     back = back + nt(dq_row.astype(BF16), matrix(w_q.at[0]))
+    slices_back(dt1, all_mem, gs1)
     dr, skip = norm_back(back, 0, xh0, scale0, words_f)
     ga = dr.astype(BF16)
+    value_sums(dt1)
     column(2, ga.astype(F32))
+    small("s0", sg0, sr0, core_next)
     by_head(a8, nt(ga, matrix(w_out.at[0])))
     to_heads("x8", a8, b8)
+    last = skip
+    scatter_f("dn0")
+    merge_1("dm", dx1, dc1, dp1)
+    unslice_0("u1", gs1, cs1)
     put(g_out.at[0], nn(b3[...].reshape(width, here), ga))
-    scatter_1("dn1")
+    scatter_2("up1")
+    scatter_2("up0")
+    scatter_1("out1")
     put(g_q.at[0], nt(flip(h1_low).astype(BF16), dq))
-    last = skip
     unslice_1("u1", gs1, cs1, zs1)
-    scatter_0("out1")
-    scatter_1("out1")
-    scatter_3("up0")
-    scatter_2("up1")
-    scatter_0("q")
-    small("s0", sg0, sr0, core_next)
     scatter_0("out0")
+    scatter_f("dn1")
     landed("x8", b8)
+    small_add("s0", sr0, sg0, sg1)
+    small("s1", sg1, sr1, y_next)
     attend_start(b8, l0, ot0)
     attend_back(0, qt0, kt0, v0, pt0, True, None, None, None)
-    scatter_f("dn0")
     attend_back(1, qt0, kt0, v0, pt0, True, None, None, None)
-    small_add("s0", sr0, sg0, sg1)
-    scatter_2("dn1")
-    scatter_1("q")
     attend_back(2, qt0, kt0, v0, pt0, True, None, None, None)
+    merge_3("dm", dx1, dp1)
+    scatter_0("q")
+    scatter_3("up1")
     attend_back(3, qt0, kt0, v0, pt0, True, None, None, None)
-    scatter_2("out1")
-    merge_1("dm", dx1, dc1, dp1)
-    scatter_3("up1")
     dt0[64:128, :] = acc_k[...].astype(BF16)
     dt0[128:192, :] = acc_v[...].astype(BF16)
-    scatter_f("up0")
+    rows_back(dt0, 0, dx0, 1 - c)
+    unslice_f("u1", gs1, zs1)
+    scatter_3("up0")
+    scatter_1("q")
+    head_sums(dt0)
+    scatter_1("out0")
     slices_back(dt0, all_tok, gs0)
-    scatter_1("out0")
     unslice_0("u0", gs0, cs0)
-    head_sums(dt0)
-    scatter_3("out1")
-    scatter_2("q")
+    scatter_f("up1")
+    scatter_2("out1")
+    small_add("s1", sr1, sg1, sg2)
+    merge_0("dx", dx0, dc0)
+    small("s2", sg2, sr2, x_next)
     unslice_1("u0", gs0, cs0, zs0)
     small("t0", tg0, tr0, core_next)
-    small("s1", sg1, sr1, y_next)
-    rows_back(dt0, 0, dx0, 1 - c)
+    landed("res", o_res)
     small_add("t0", tr0, tg0, tg1)
+    out_mem[...] = merge_2("dm", dx1, dp1).astype(BF16).reshape(2, 64, width)
+    from_plane("gmem", out_mem, o_mem)
+    rows_back(dt0, 0, dx0, c)
+    merge_1("dx", dx0, dc0, dp0)
+    scatter_2("out0")
+    unslice_f("u0", gs0, zs0)
+    small_add("s2", sr2, sg2, sg3)
+    scatter_f("up0")
+    scatter_2("q")
+    scatter_3("out1")
     small("t1", tg1, tr1, y_next)
-    merge_0("dx", dx0, dc0)
-    rows_back(dt0, 0, dx0, c)
-    merge_3("dm", dx1, dp1)
-    scatter_f("dn1")
-    unslice_f("u1", gs1, zs1)
-    merge_1("dx", dx0, dc0, dp0)
+    merge_3("dx", dx0, dp0)
+    scatter_3("out0")
+    scatter_3("q")
+    small_add("t1", tr1, tg1, tg2)
+    small_z("sa", sg3, slice(None), tile_own, sra)
+    small("t2", tg2, tr2, x_next)
+    unslice_2("u1", gs1, zs1, fs1, o_in.at[1, pl.ds(1, 2)])
+    scatter_f("out0")
+    unslice_2("u0", gs0, zs0, fs0, o_in.at[0])
+    scattered("up0")
+    small_z("sb", sg3, pl.ds(8, 8), tile_up, srb)
     scatter_f("out1")
-    small_add("t1", tr1, tg1, tg2)
-    small("t2", tg2, tr2, x_next)
-    scatter_3("q")
-    scatter_f("up1")
-    small_add("s1", sr1, sg1, sg2)
-    small("s2", sg2, sr2, x_next)
-    landed("res", o_res)
-    unslice_f("u0", gs0, zs0)
-    scatter_2("out0")
     scatter_3("dn1")
     scatter_f("q")
-    out_mem[...] = merge_2("dm", dx1, dp1).astype(BF16).reshape(2, 64, width)
-    from_plane("gmem", out_mem, o_mem)
     small_add("t2", tr2, tg2, tg3)
-    merge_3("dx", dx0, dp0)
-    small_add("s2", sr2, sg2, sg3)
-    scattered("up0")
-    scatter_3("out0")
-    small_z("sa", sg3, slice(None), tile_own, sra)
-    small_z("sb", sg3, pl.ds(8, 8), tile_up, srb)
-    unslice_2("u0", gs0, zs0, fs0, o_in.at[0])
-    unslice_2("u1", gs1, zs1, fs1, o_in.at[1, pl.ds(1, 2)])
     small_z("ta", tg3, slice(None), tile_own, tra)
-    scattered("up1")
-    scattered("out1")
-    scattered("dn1")
-    scatter_3("dn0")
-    scatter_f("out0")
     out_tok[...] = (merge_2("dx", dx0, dp0) + last).astype(BF16).reshape(2, 64, width)
     from_plane("gtok", out_tok, o_tok)
     unslice_3("u1", o_in.at[1, pl.ds(1, 2)])
-    unslice_3("u0", o_in.at[0])
+    scattered("up1")
+    scatter_3("dn0")
     scattered("q")
+    scattered("out0")
     landed("gmem", o_mem)
+    scattered("dn1")
+    scattered("out1")
     scattered("dn0")
     keep("e3", o_dn, h_dn)
     small_out()
     keep("e2", o_up, h_up)
-    scattered("out0")
+    unslice_3("u0", o_in.at[0])
     keep("e1", o_out, h_out)
     keep("e0", o_in, h_in)
     landed("gtok", o_tok)
@@ -1703,10 +1704,10 @@
     scratch += ([low(64, 1024)] * 3 + [low(1024, 64)] * 2 + [low(1024, 1024), full(1, 1024), full(64, 1024)]) * 2
     scratch += [low(64, 1024)] + [full(64, 1024)] * 2
     scratch += [low(128, 2048), full(128, 2048), low(128, 2048)] + [full(128, 512)] * 5
-    scratch += [low(5, 128, 512), full(3, 512, 128), full(3, 128, 512), low(192, 1024), low(128, 1024), low(2304, 512)]
+    scratch += [low(5, 128, 512), full(3, 512, 128), full(3, 128, 512), low(192, 1024), low(128, 1024), low(2560, 512)]
     scratch += [low(leads[k], *shards[k]) for k in kinds] + [low(n, 4, 16, 128) for n in (3, 2)]
     scratch += [low(2, 2, 1, 1, 2, 64, 128), low(2, 3, 2, 1, 2, 64, 128)]
-    scratch += [pltpu.SemaphoreType.DMA((44,)), pltpu.SemaphoreType.DMA((NAMES,))]
+    scratch += [pltpu.SemaphoreType.DMA((46,)), pltpu.SemaphoreType.DMA((NAMES,))]
     rows = jax.ShapeDtypeStruct((2, 64, 512), BF16)
 
     def wide_out(*shape):

time: 101 us -> 99.7 us (0.987)
  no operation moved by 1% of the time
where the time goes in v8:
time: 99.7 us; the launch traced here: 99.5 us
  Pallas kernels  98.7 us (99%)
    pallas_call x1, Pallas kernels, fused_local(): pl.pallas_call(fused_kernel, name='layer', out_shape=(rows, rows, rows, *...  96.5 us
    pallas_call x1, Pallas kernels, fused_local(): pl.pallas_call(copy_kernel, name='hand_over', out_shape=tuple((jax.ShapeD...  2.23 us

profile of v8, /device:TPU:0, one launch (start us, length us, event | category | flops | bytes accessed | tf_op | source)
XLA Modules:
  0.0 99.5 jit_solution(9658819631849748687)
XLA Ops:
  0.7 96.5 %layer.1 = (bf16[2,64,512]{2,1,0:T(8,128)(2,1)}, bf16[2,64,512]{2,1,0:T(8,128)(2,1)}, bf16[2,64,512]{2,1,0:T(8,128)(2,1)}, f32[2,3,16,512]{3,2,1,0:T(8,128)}, f3...) custom-call(bf16[2,64,512]{2,1,0:T(8,128)(2,1)} %bitcast.24, ...), custom_call_target="tpu_custom_call" | custom-call | tf_op jit(solution)/shard_map/layer/pallas_call | solution.py:1716
  97.1 2.2 %hand_over.1 = (bf16[2,64,512]{2,1,0:T(8,128)(2,1)}, bf16[2,64,512]{2,1,0:T(8,128)(2,1)}, bf16[2,64,512]{2,1,0:T(8,128)(2,1)}, f32[2,3,16,512]{3,2,1,0:T(8,128)}...) custom-call(bf16[2,64,512]{2,1,0:T(8,128)(2,1)} %get-tuple-element.3, ...), custom_call_target="tpu_custom_call" | custom-call | tf_op jit(solution)/shard_map/hand_over/pallas_call | solution.py:1730

commit v9 on v8

--- a/solution.py
+++ b/solution.py
@@ -1366,115 +1366,115 @@
         pl.semaphore_signal(barrier, inc=1, device_id=device, device_id_type=MESH)
     pl.semaphore_wait(barrier, len(greet))
     gather_z("out0")
+    gather_z("up1")
     gather_z("dn1")
-    gather_z("up1")
     to_plane("x", tok, all_tok, True)
-    slice_1("w0", s_in.at[0], ws0)
-    gather_z("dn0")
-    gather_z("out1")
-    gather_z("q")
-    gather_z("up0")
     for i, (ref, _) in enumerate(raw):
         landed("raw" + str(i), ref)
         span = ref.shape[2]
         for m in range(2):
             for start in (0, 64):
                 meta[m, i : i + 1, start : start + span] = ref[m]
-    slice_1("w1", s_in.at[1, pl.ds(1, 2)], ws1)
+    gather_z("q")
+    slice_1("w0", s_in.at[0], ws0)
     gather_f("out0")
+    to_plane("meta", meta, in_meta)
+    gather_z("dn0")
+    to_plane("m", mem, all_mem, True)
     spread_1("x", all_tok, 0)
+    gather_z("up0")
+    gather_z("out1")
+    spread_1("x", all_tok, 1)
+    gather_f("q")
+    gather_1("out0")
+    landed("meta", in_meta)
     slice_2("w0", ws0)
-    gather_1("out0")
-    gather_f("q")
-    to_plane("meta", meta, in_meta)
-    spread_1("x", all_tok, 1)
+    lane = lax.broadcasted_iota(jnp.int32, (8, 128), 1)
+    all_meta[me_slot] = jnp.where(lane < 64, in_meta[0], in_meta[1])
+    gather_1("dn0")
+    for cc, yy, xx in plane_peers:
+        send("marks", all_meta.at[me_slot], all_meta.at[me_slot], (cc, at(z, yy, xx)))
+    spread_1("m", all_mem, 0)
     spread_2("x", all_tok, 0)
+    spread_2("x", all_tok, 1)
+    spread_1("m", all_mem, 1)
+    gather_1("out1")
     gather_f("up0")
     gather_2("out0")
+    spread_4("x", all_tok, 0)
+    spread_4("x", all_tok, 1)
     gather_1("q")
-    gather_1("out1")
+    slice_1("w1", s_in.at[1, pl.ds(1, 2)], ws1)
+    spread_2("m", all_mem, 0)
     slice_f("w0", ws0)
-    gather_1("up0")
-    to_plane("m", mem, all_mem, True)
+    sent_later("marks", all_meta.at[pl.ds(0, 7)])
     for i, (_, ref) in enumerate(given):
         landed("given" + str(i), ref)
-    spread_2("x", all_tok, 1)
-    landed("meta", in_meta)
-    lane = lax.broadcasted_iota(jnp.int32, (8, 128), 1)
-    gather_2("q")
-    slice_3("w0", ws0)
-    gather_1("dn0")
-    all_meta[me_slot] = jnp.where(lane < 64, in_meta[0], in_meta[1])
-    for cc, yy, xx in plane_peers:
-        send("marks", all_meta.at[me_slot], all_meta.at[me_slot], (cc, at(z, yy, xx)))
-    gather_3("out0")
-    gather_2("up0")
-    spread_4("x", all_tok, 0)
-    spread_4("x", all_tok, 1)
-    slice_2("w1", ws1)
-    slice_4("w0", ws0)
-    spread_3("x", all_tok)
-    gather_3("q")
-    spread_1("m", all_mem, 0)
-    gathered("out0")
-    spread_1("m", all_mem, 1)
-    gather_f("out1")
-    heads_weights(0, ws0)
-    sent_later("marks", all_meta.at[pl.ds(0, 7)])
-    gather_1("up1")
-    make_masks()
     for i, row in enumerate((0, 1, 4)):
         bias_cols[i] = jnp.transpose(jnp.broadcast_to(bias(row), (128, width)))
+    gather_1("up1")
+    gather_1("up0")
+    gather_2("q")
+    slice_2("w1", ws1)
+    slice_3("w0", ws0)
+    spread_2("m", all_mem, 1)
+    make_masks()
+    spread_3("x", all_tok)
+    gather_3("out0")
+    gather_f("dn0")
+    gather_2("up0")
+    slice_4("w0", ws0)
+    gather_1("dn1")
+    heads_weights(0, ws0)
     project_heads(all_tok, 0, qt0, k0, kt0, v0, vt0)
     attend(0, qt0, k0, vt0, pt0, l0, ot0, True, "x3", a3, b3)
-    gather_f("dn0")
+    gather_f("out1")
+    attend(1, qt0, k0, vt0, pt0, l0, ot0, True, "x3", a3, b3)
+    attend(2, qt0, k0, vt0, pt0, l0, ot0, True, "x3", a3, b3)
+    gather_2("dn0")
+    attend(3, qt0, k0, vt0, pt0, l0, ot0, True, "x3", a3, b3)
+    spread_4("m", all_mem, 0)
+    spread_4("m", all_mem, 1)
+    gathered("out0")
+    gather_3("up0")
+    gather_f("up1")
+    gather_3("q")
     gather_2("out1")
-    attend(1, qt0, k0, vt0, pt0, l0, ot0, True, "x3", a3, b3)
-    spread_2("m", all_mem, 0)
-    slice_f("w1", ws1)
-    spread_2("m", all_mem, 1)
-    attend(2, qt0, k0, vt0, pt0, l0, ot0, True, "x3", a3, b3)
-    gather_1("dn1")
-    attend(3, qt0, k0, vt0, pt0, l0, ot0, True, "x3", a3, b3)
-    slice_3("w1", ws1)
-    gather_3("up0")
-    gather_2("dn0")
-    gathered("q")
-    gather_f("up1")
+    gather_2("up1")
     landed("x3", b3)
     words_f = all_tok[me_slot].reshape(here, width).astype(F32)
+    gathered("q")
+    slice_f("w1", ws1)
     branch = tn(b3[...].reshape(width, here), matrix(w_out.at[0])) + bias(2)
+    spread_3("m", all_mem)
     h1, scale0 = norm(words_f * omega[0:1, :] + branch, 0, xh0)
     h1_f[...] = h1
-    gather_3("out1")
+    gather_f("dn1")
     h1_low = h1.astype(BF16)
-    slice_4("w1", ws1)
     by_head(a4, nn(h1_low, matrix(w_q.at[0])) + bias(3))
     to_heads("x4", a4, b4)
-    gather_2("up1")
-    gather_f("dn1")
-    spread_4("m", all_mem, 0)
-    spread_4("m", all_mem, 1)
+    to_plane("cot", cot, in_cot)
+    slice_3("w1", ws1)
+    gather_3("dn0")
+    gather_2("dn1")
+    slice_4("w1", ws1)
+    heads_weights(3, ws1)
+    project_heads(all_mem, 3, None, k1, kt1, v1, vt1)
+    gather_3("out1")
+    gathered("up0")
+    gather_3("up1")
     landed("x4", b4)
-    spread_3("m", all_mem)
-    gathered("out1")
-    heads_weights(3, ws1)
-    gather_2("dn1")
-    project_heads(all_mem, 3, None, k1, kt1, v1, vt1)
     for s in range(GROUP):
         qt1[:, s * here : (s + 1) * here] = (b4[s].astype(F32) * 0.125).astype(BF16)
-    gather_3("dn0")
-    gathered("up0")
-    gather_3("up1")
     attend(0, qt1, k1, vt1, pt1, l1, ot1, False, "x5", a5, b5)
     attend(1, qt1, k1, vt1, pt1, l1, ot1, False, "x5", a5, b5)
     attend(2, qt1, k1, vt1, pt1, l1, ot1, False, "x5", a5, b5)
     attend(3, qt1, k1, vt1, pt1, l1, ot1, False, "x5", a5, b5)
     gathered("dn0")
+    gathered("out1")
+    gathered("up1")
     gather_3("dn1")
-    to_plane("cot", cot, in_cot)
     gathered("dn1")
-    gathered("up1")
     landed("x5", b5)
     branch = tn(b5[...].reshape(width, here), matrix(w_out.at[1])) + bias(5)
     h2, scale1 = norm(h1_f[...] * omega[1:2, :] + branch, 1, xh1)
@@ -1491,138 +1491,138 @@
     dr, skip = norm_back(grad, 2, xh2, scale2, h2_f[...])
     gf = dr.astype(BF16)
     column(6, gf.astype(F32))
-    put(g_dn.at[0], tn(act[...], gf[:, 0:256]))
     back = feed_back(gf, skip)
-    scatter_0("dn0")
+    put(g_up.at[0], tn(h2_low, gul[:, 0:1024]))
+    scatter_0("up0")
     dr, skip = norm_back(back, 1, xh1, scale1, h1_f[...])
     gc = dr.astype(BF16)
     column(5, gc.astype(F32))
     by_head(a6, nt(gc, matrix(w_out.at[1])))
     to_heads("x6", a6, b6)
-    put(g_out.at[1], nn(b5[...].reshape(width, here), gc))
-    scatter_1("dn0")
+    put(g_dn.at[0], tn(act[...], gf[:, 0:256]))
+    from_plane("res", out_res, o_res)
+    scatter_1("up0")
     put(g_dn.at[1], tn(act[...], gf[:, 256:512]))
     scatter_0("dn1")
-    from_plane("res", out_res, o_res)
-    put(g_up.at[0], tn(h2_low, gul[:, 0:1024]))
+    put(g_out.at[1], nn(b5[...].reshape(width, here), gc))
+    scatter_0("out1")
     put(g_up.at[1], tn(h2_low, gul[:, 1024:2048]))
+    scatter_0("up1")
     back = skip
     landed("x6", b6)
     attend_start(b6, l1, ot1)
-    scatter_0("up0")
     scatter_1("dn1")
     attend_back(0, qt1, kt1, v1, pt1, False, "x7", a7, b7)
     attend_back(1, qt1, kt1, v1, pt1, False, "x7", a7, b7)
+    scatter_0("dn0")
     attend_back(2, qt1, kt1, v1, pt1, False, "x7", a7, b7)
-    scatter_2("dn0")
     attend_back(3, qt1, kt1, v1, pt1, False, "x7", a7, b7)
+    scatter_2("up0")
+    scatter_1("dn0")
     dt1[0:64, :] = acc_k[...].astype(BF16)
+    scatter_2("dn1")
     dt1[64:128, :] = acc_v[...].astype(BF16)
-    scatter_1("up0")
-    scatter_0("out1")
-    scatter_0("up1")
+    scatter_1("out1")
     rows_back(dt1, 3, dx1, 1 - c)
-    scatter_1("up1")
-    landed("x7", b7)
     merge_0("dm", dx1, dc1)
     rows_back(dt1, 3, dx1, c)
+    landed("x7", b7)
     dq = b7[...].reshape(width, here)
+    slices_back(dt1, all_mem, gs1)
+    unslice_0("u1", gs1, cs1)
     dq_row = flip(dq)
-    scatter_2("dn1")
     column(3, dq_row)
+    value_sums(dt1)
     back = back + nt(dq_row.astype(BF16), matrix(w_q.at[0]))
-    slices_back(dt1, all_mem, gs1)
     dr, skip = norm_back(back, 0, xh0, scale0, words_f)
     ga = dr.astype(BF16)
-    value_sums(dt1)
     column(2, ga.astype(F32))
-    small("s0", sg0, sr0, core_next)
+    scatter_3("up0")
     by_head(a8, nt(ga, matrix(w_out.at[0])))
     to_heads("x8", a8, b8)
     last = skip
-    scatter_f("dn0")
+    scatter_1("up1")
+    put(g_q.at[0], nt(flip(h1_low).astype(BF16), dq))
+    scatter_2("dn0")
     merge_1("dm", dx1, dc1, dp1)
-    unslice_0("u1", gs1, cs1)
+    scatter_2("out1")
+    small("s0", sg0, sr0, core_next)
+    scatter_f("up0")
     put(g_out.at[0], nn(b3[...].reshape(width, here), ga))
-    scatter_2("up1")
-    scatter_2("up0")
-    scatter_1("out1")
-    put(g_q.at[0], nt(flip(h1_low).astype(BF16), dq))
-    unslice_1("u1", gs1, cs1, zs1)
-    scatter_0("out0")
-    scatter_f("dn1")
     landed("x8", b8)
-    small_add("s0", sr0, sg0, sg1)
-    small("s1", sg1, sr1, y_next)
     attend_start(b8, l0, ot0)
     attend_back(0, qt0, kt0, v0, pt0, True, None, None, None)
+    scatter_f("dn1")
     attend_back(1, qt0, kt0, v0, pt0, True, None, None, None)
+    unslice_1("u1", gs1, cs1, zs1)
     attend_back(2, qt0, kt0, v0, pt0, True, None, None, None)
+    scatter_2("up1")
+    scatter_0("q")
+    small_add("s0", sr0, sg0, sg1)
+    scatter_0("out0")
+    scatter_f("dn0")
+    small("s1", sg1, sr1, y_next)
     merge_3("dm", dx1, dp1)
-    scatter_0("q")
-    scatter_3("up1")
     attend_back(3, qt0, kt0, v0, pt0, True, None, None, None)
     dt0[64:128, :] = acc_k[...].astype(BF16)
     dt0[128:192, :] = acc_v[...].astype(BF16)
-    rows_back(dt0, 0, dx0, 1 - c)
-    unslice_f("u1", gs1, zs1)
-    scatter_3("up0")
-    scatter_1("q")
+    scatter_3("out1")
     head_sums(dt0)
-    scatter_1("out0")
+    small("t0", tg0, tr0, core_next)
+    scatter_3("up1")
     slices_back(dt0, all_tok, gs0)
     unslice_0("u0", gs0, cs0)
+    scatter_1("q")
+    unslice_f("u1", gs1, zs1)
+    small_add("t0", tr0, tg0, tg1)
+    small_add("s1", sr1, sg1, sg2)
+    small("s2", sg2, sr2, x_next)
+    rows_back(dt0, 0, dx0, 1 - c)
+    unslice_1("u0", gs0, cs0, zs0)
+    merge_0("dx", dx0, dc0)
+    small("t1", tg1, tr1, y_next)
+    rows_back(dt0, 0, dx0, c)
+    scatter_1("out0")
+    out_mem[...] = merge_2("dm", dx1, dp1).astype(BF16).reshape(2, 64, width)
+    scatter_f("out1")
+    from_plane("gmem", out_mem, o_mem)
+    merge_1("dx", dx0, dc0, dp0)
+    scatter_2("q")
+    scattered("up0")
+    small_add("t1", tr1, tg1, tg2)
+    landed("res", o_res)
+    scatter_2("out0")
     scatter_f("up1")
-    scatter_2("out1")
-    small_add("s1", sr1, sg1, sg2)
-    merge_0("dx", dx0, dc0)
-    small("s2", sg2, sr2, x_next)
-    unslice_1("u0", gs0, cs0, zs0)
-    small("t0", tg0, tr0, core_next)
-    landed("res", o_res)
-    small_add("t0", tr0, tg0, tg1)
-    out_mem[...] = merge_2("dm", dx1, dp1).astype(BF16).reshape(2, 64, width)
-    from_plane("gmem", out_mem, o_mem)
-    rows_back(dt0, 0, dx0, c)
-    merge_1("dx", dx0, dc0, dp0)
-    scatter_2("out0")
     unslice_f("u0", gs0, zs0)
+    small("t2", tg2, tr2, x_next)
+    merge_3("dx", dx0, dp0)
+    scatter_3("q")
+    scatter_3("out0")
     small_add("s2", sr2, sg2, sg3)
-    scatter_f("up0")
-    scatter_2("q")
-    scatter_3("out1")
-    small("t1", tg1, tr1, y_next)
-    merge_3("dx", dx0, dp0)
-    scatter_3("out0")
-    scatter_3("q")
-    small_add("t1", tr1, tg1, tg2)
+    landed("gmem", o_mem)
     small_z("sa", sg3, slice(None), tile_own, sra)
-    small("t2", tg2, tr2, x_next)
+    small_z("sb", sg3, pl.ds(8, 8), tile_up, srb)
+    scatter_3("dn0")
+    scattered("out1")
     unslice_2("u1", gs1, zs1, fs1, o_in.at[1, pl.ds(1, 2)])
-    scatter_f("out0")
-    unslice_2("u0", gs0, zs0, fs0, o_in.at[0])
-    scattered("up0")
-    small_z("sb", sg3, pl.ds(8, 8), tile_up, srb)
-    scatter_f("out1")
     scatter_3("dn1")
-    scatter_f("q")
+    scattered("up1")
     small_add("t2", tr2, tg2, tg3)
     small_z("ta", tg3, slice(None), tile_own, tra)
+    scatter_f("q")
+    scatter_f("out0")
     out_tok[...] = (merge_2("dx", dx0, dp0) + last).astype(BF16).reshape(2, 64, width)
     from_plane("gtok", out_tok, o_tok)
-    unslice_3("u1", o_in.at[1, pl.ds(1, 2)])
-    scattered("up1")
-    scatter_3("dn0")
+    unslice_2("u0", gs0, zs0, fs0, o_in.at[0])
     scattered("q")
     scattered("out0")
-    landed("gmem", o_mem)
     scattered("dn1")
-    scattered("out1")
+    unslice_3("u1", o_in.at[1, pl.ds(1, 2)])
     scattered("dn0")
     keep("e3", o_dn, h_dn)
     small_out()
+    unslice_3("u0", o_in.at[0])
     keep("e2", o_up, h_up)
-    unslice_3("u0", o_in.at[0])
     keep("e1", o_out, h_out)
     keep("e0", o_in, h_in)
     landed("gtok", o_tok)

time: 99.7 us -> 98.9 us (level)
  no operation moved by 1% of the time
where the time goes in v9:
time: 98.9 us; the launch traced here: 98.7 us
  Pallas kernels  97.8 us (99%)
    pallas_call x1, Pallas kernels, fused_local(): pl.pallas_call(fused_kernel, name='layer', out_shape=(rows, rows, rows, *...  95.6 us
    pallas_call x1, Pallas kernels, fused_local(): pl.pallas_call(copy_kernel, name='hand_over', out_shape=tuple((jax.ShapeD...  2.23 us

profile of v9, /device:TPU:0, one launch (start us, length us, event | category | flops | bytes accessed | tf_op | source)
XLA Modules:
  0.0 98.7 jit_solution(2276690631272439508)
XLA Ops:
  0.7 95.6 %layer.1 = (bf16[2,64,512]{2,1,0:T(8,128)(2,1)}, bf16[2,64,512]{2,1,0:T(8,128)(2,1)}, bf16[2,64,512]{2,1,0:T(8,128)(2,1)}, f32[2,3,16,512]{3,2,1,0:T(8,128)}, f3...) custom-call(bf16[2,64,512]{2,1,0:T(8,128)(2,1)} %bitcast.24, ...), custom_call_target="tpu_custom_call" | custom-call | tf_op jit(solution)/shard_map/layer/pallas_call | solution.py:1716
  96.3 2.2 %hand_over.1 = (bf16[2,64,512]{2,1,0:T(8,128)(2,1)}, bf16[2,64,512]{2,1,0:T(8,128)(2,1)}, bf16[2,64,512]{2,1,0:T(8,128)(2,1)}, f32[2,3,16,512]{3,2,1,0:T(8,128)}...) custom-call(bf16[2,64,512]{2,1,0:T(8,128)(2,1)} %get-tuple-element.3, ...), custom_call_target="tpu_custom_call" | custom-call | tf_op jit(solution)/shard_map/hand_over/pallas_call | solution.py:1730

commit v10 on v9

--- a/solution.py
+++ b/solution.py
@@ -1655,9 +1655,16 @@
 
 
 def copy_kernel(*refs):
-    count = len(refs) // 2
+    count = len(refs) // 3
+    given, results, held = (refs[i * count : (i + 1) * count] for i in range(3))
+    arrived, left = refs[3 * count :]
     for i in range(count):
-        refs[count + i][...] = refs[i][...]
+        pltpu.make_async_copy(given[i], held[i], arrived.at[i]).start()
+    for i in range(count):
+        pltpu.make_async_copy(given[i], held[i], arrived.at[i]).wait()
+        pltpu.make_async_copy(held[i], results[i], left.at[i]).start()
+    for i in range(count):
+        pltpu.make_async_copy(held[i], results[i], left.at[i]).wait()
 
 
 def fused_local(
@@ -1731,8 +1738,9 @@
         copy_kernel,
         name="hand_over",
         out_shape=tuple(jax.ShapeDtypeStruct(out.shape, out.dtype) for out in outs),
-        in_specs=[vmem] * len(outs),
-        out_specs=(vmem,) * len(outs),
+        in_specs=[any_space] * len(outs),
+        out_specs=(any_space,) * len(outs),
+        scratch_shapes=[pltpu.VMEM(out.shape, out.dtype) for out in outs] + [pltpu.SemaphoreType.DMA((len(outs),))] * 2,
     )(*outs)
     shaped = [out.reshape(2, 64, 1, 512) for out in outs[:3]]
     return (

time: 98.9 us -> 98.8 us (level)
  no operation moved by 1% of the time
where the time goes in v10:
time: 98.8 us; the launch traced here: 98.6 us
  Pallas kernels  97.8 us (99%)
    pallas_call x1, Pallas kernels, fused_local(): pl.pallas_call(fused_kernel, name='layer', out_shape=(rows, rows, rows, *...  95.6 us
    pallas_call x1, Pallas kernels, fused_local(): pl.pallas_call(copy_kernel, name='hand_over', out_shape=tuple((jax.ShapeD...  2.14 us

profile of v10, /device:TPU:0, one launch (start us, length us, event | category | flops | bytes accessed | tf_op | source)
XLA Modules:
  0.0 98.6 jit_solution(2271434380731800258)
XLA Ops:
  0.7 95.6 %layer.1 = (bf16[2,64,512]{2,1,0:T(8,128)(2,1)}, bf16[2,64,512]{2,1,0:T(8,128)(2,1)}, bf16[2,64,512]{2,1,0:T(8,128)(2,1)}, f32[2,3,16,512]{3,2,1,0:T(8,128)}, f3...) custom-call(bf16[2,64,512]{2,1,0:T(8,128)(2,1)} %bitcast.24, ...), custom_call_target="tpu_custom_call" | custom-call | tf_op jit(solution)/shard_map/layer/pallas_call | solution.py:1723
  96.3 2.1 %hand_over.1 = (bf16[2,64,512]{2,1,0:T(8,128)(2,1)}, bf16[2,64,512]{2,1,0:T(8,128)(2,1)}, bf16[2,64,512]{2,1,0:T(8,128)(2,1)}, f32[2,3,16,512]{3,2,1,0:T(8,128)}...) custom-call(bf16[2,64,512]{2,1,0:T(8,128)(2,1)} %get-tuple-element.3, ...), custom_call_target="tpu_custom_call" | custom-call | tf_op jit(solution)/shard_map/hand_over/pallas_call | solution.py:1737
